TPU v7x, 32 devices: a whole 2x2x4 slice. The times are simulated.
32 devices in a mesh: batch: 2 (over x), head: 4 (over y, core), wide: 4 (over z).
Axes of the slice: x: 2, y: 2, z: 4, core: 2. Of those that a mesh axis runs over, the one named last changes fastest.
Arguments:
- tokens: bfloat16 [4, 1024, 768], P('batch', 'wide'), may hold values from -6 to 6
- patches: int32 [4, 4], P('batch'), may hold values from 0 to 1024, as said below
- w_qkv: bfloat16 [2, 3, 768, 768], P(None, None, 'head'), may hold values from -0.21875 to 0.21875
- w_att: bfloat16 [2, 768, 768], P(None, 'head'), may hold values from -0.875 to 0.875
- w_in: bfloat16 [2, 3072, 768], P(None, 'wide'), may hold values from -0.21875 to 0.21875
- w_mlp: bfloat16 [2, 3072, 768], P(None, 'wide'), may hold values from -0.21875 to 0.21875
- gains: float32 [2, 768], replicated, may hold values from 0.1 to 1.9
- cotangent: bfloat16 [4, 1024, 768], P('batch', 'wide'), may hold values from -6 to 6
Outputs:
- out: float32 [4, 1024, 768], P('batch', 'wide')
- d_tokens: float32 [4, 1024, 768], P('batch', 'wide')
- d_qkv: float32 [2, 3, 768, 768], P(None, None, 'head')
- d_att: float32 [2, 768, 768], P(None, 'head')
- d_in: float32 [2, 3072, 768], P(None, 'wide')
- d_mlp: float32 [2, 3072, 768], P(None, 'wide')
- d_gains: float32 [2, 768], replicated
Inputs may be any that keep to these rules, and one draw needn't show every extreme that they name: Each row packs images of 1024, 576 or 196 patches from its first slot on, entries of absent images are 0 and stand last, and the counts of a row sum to at most 1024; among the rows of each index of batch one holds a single image of 1024 patches.
All inputs are finite; a program needn't handle non-finite values.
Results may differ from a plain program's by a relative error of at most 0.023.
Values may be sent and summed in bfloat16 or wider, within the bound.
No kernel may reach another device: no remote copies, remote signals or barrier semaphores. Data moves between devices by JAX's collectives and lax.ppermute only.
A program may use at most 256 MiB of HBM per device.

v0:
```python
import functools

import jax
import jax.numpy as jnp
from jax import lax
from jax.experimental import pallas as pl
from jax.experimental.pallas import tpu as pltpu
from jax.sharding import PartitionSpec as P

HEAD_DIM = 64
EPS = 1e-06
NEGATIVE = -1e30
BF = jnp.bfloat16
F32 = jnp.float32
DIRECT = 8


def norm_parts(stream):
    centre = jnp.mean(stream, axis=-1, keepdims=True)
    centred = stream - centre
    spread = jnp.mean(centred * centred, axis=-1, keepdims=True)
    rstd = lax.rsqrt(spread + EPS)
    return centred * rstd, rstd


def norm_back(d_act, xhat, rstd, gain_row):
    dxh = d_act * gain_row
    m1 = jnp.mean(dxh, axis=-1, keepdims=True)
    m2 = jnp.mean(dxh * xhat, axis=-1, keepdims=True)
    return (dxh - m1 - xhat * m2) * rstd


def trans_dot(left, right):
    return lax.dot_general(left, right, (((0,), (0,)), ((), ())), preferred_element_type=F32)


def right_dot(left, right):
    return lax.dot_general(left, right, (((1,), (1,)), ((), ())), preferred_element_type=F32)


def plain_dot(left, right):
    return jnp.dot(left, right, preferred_element_type=F32)


def swap(x, bit):
    size = lax.axis_size("head")
    return lax.ppermute(x, "head", [(i, i ^ bit) for i in range(size)])


def shift(x, step):
    size = lax.axis_size("wide")
    return lax.ppermute(x, "wide", [(i, (i + step) % size) for i in range(size)])


def gather_wide(x):
    size = lax.axis_size("wide")
    if size <= DIRECT:
        return jnp.concatenate([x] + [shift(x, s) for s in range(1, size)], axis=0)
    whole = lax.all_gather(x, "wide", axis=0, tiled=False)
    order = (lax.axis_index("wide") - jnp.arange(size)) % size
    return whole[order].reshape(size * x.shape[0], *x.shape[1:])


def scatter_wide(parts):
    size = lax.axis_size("wide")
    rows = parts.shape[0] // size
    if size <= DIRECT:
        total = parts[:rows]
        low = [shift(parts[s * rows : (s + 1) * rows].astype(BF), -s) for s in range(1, size)]
        for piece in low:
            total = total + piece.astype(F32)
        return total
    order = (lax.axis_index("wide") - jnp.arange(size)) % size
    blocks = parts.astype(BF).reshape(size, rows, -1)[order]
    return lax.psum_scatter(blocks, "wide", scatter_dimension=0, tiled=False).astype(F32)


def gather_head(x):
    place = lax.axis_index("head")
    a = x
    b = swap(x, 2)
    c = swap(a, 1)
    d = swap(b, 1)
    low_bit = (place & 1) == 1
    high_bit = (place & 2) == 2
    a, c = jnp.where(low_bit, c, a), jnp.where(low_bit, a, c)
    b, d = jnp.where(low_bit, d, b), jnp.where(low_bit, b, d)
    a, b = jnp.where(high_bit, b, a), jnp.where(high_bit, a, b)
    c, d = jnp.where(high_bit, d, c), jnp.where(high_bit, c, d)
    return jnp.stack([a, c, b, d])


PAIR = 2 * HEAD_DIM
FLOOR = -1e29


def head_softmax(q, k, allowed):
    s = jnp.where(allowed, right_dot(q, k), NEGATIVE)
    top = jnp.maximum(jnp.max(s, axis=-1, keepdims=True), FLOOR)
    expo = jnp.exp(s - top)
    inverse = 1.0 / jnp.maximum(jnp.sum(expo, axis=-1, keepdims=True), 1.0)
    return expo * inverse, top, inverse


def attend_kernel(q_ref, k_ref, v_ref, qid_ref, kid_ref, o_ref, stat_ref):
    allowed = qid_ref[0] == kid_ref[0]
    q = q_ref[0] * jnp.asarray(HEAD_DIM ** (-0.5), BF)
    k, v = k_ref[0], v_ref[0]
    lane = lax.broadcasted_iota(jnp.int32, (q.shape[0], PAIR), 1)
    stats = jnp.zeros((q.shape[0], PAIR), F32)
    outs = []
    for j in range(2):
        cut = slice(j * HEAD_DIM, (j + 1) * HEAD_DIM)
        probs, top, inverse = head_softmax(q[:, cut], k[:, cut], allowed)
        outs.append(plain_dot(probs.astype(BF), v[:, cut]))
        stats = jnp.where(lane == 2 * j, top, jnp.where(lane == 2 * j + 1, inverse, stats))
    o_ref[0] = jnp.concatenate(outs, axis=1).astype(BF)
    stat_ref[0, 0] = stats


def attend_back_kernel(saved, q_ref, k_ref, v_ref, g_ref, qid_ref, kid_ref, *refs):
    if saved:
        stat_ref, dq_ref, dk_ref, dv_ref = refs
    else:
        o_ref, dq_ref, dk_ref, dv_ref = refs
    allowed = qid_ref[0] == kid_ref[0]
    scale = HEAD_DIM ** (-0.5)
    q = q_ref[0] * jnp.asarray(scale, BF)
    k, v, g = k_ref[0], v_ref[0], g_ref[0]
    outs, dqs, dks, dvs = [], [], [], []
    for j in range(2):
        cut = slice(j * HEAD_DIM, (j + 1) * HEAD_DIM)
        qj, kj, vj, gj = q[:, cut], k[:, cut], v[:, cut], g[:, cut]
        if saved:
            top = stat_ref[0, 0, :, 2 * j : 2 * j + 1]
            inverse = stat_ref[0, 0, :, 2 * j + 1 : 2 * j + 2]
            probs = jnp.exp(jnp.where(allowed, right_dot(qj, kj), NEGATIVE) - top) * inverse
        else:
            probs, top, inverse = head_softmax(qj, kj, allowed)
        low = probs.astype(BF)
        if not saved:
            outs.append(plain_dot(low, vj))
        dp = right_dot(gj, vj)
        ds = (probs * (dp - jnp.sum(probs * dp, axis=-1, keepdims=True))).astype(BF)
        dqs.append(plain_dot(ds, kj) * scale)
        dks.append(trans_dot(ds, qj))
        dvs.append(trans_dot(low, gj))
    if not saved:
        o_ref[0] = jnp.concatenate(outs, axis=1).astype(BF)
    dq_ref[0] = jnp.concatenate(dqs, axis=1).astype(BF)
    dk_ref[0] = jnp.concatenate(dks, axis=1).astype(BF)
    dv_ref[0] = jnp.concatenate(dvs, axis=1).astype(BF)


def attend_specs(q, k):
    rows, tq, width = q.shape
    tk = k.shape[1]
    q_spec = pl.BlockSpec((1, tq, PAIR), lambda r, j: (r, 0, j))
    k_spec = pl.BlockSpec((1, tk, PAIR), lambda r, j: (r, 0, j))
    qid_spec = pl.BlockSpec((1, tq, 1), lambda r, j: (r, 0, 0))
    kid_spec = pl.BlockSpec((1, 1, tk), lambda r, j: (r, 0, 0))
    stat_spec = pl.BlockSpec((1, 1, tq, PAIR), lambda r, j: (r, j, 0, 0))
    work = rows * tq * tk * width
    return (rows, width // PAIR), q_spec, k_spec, qid_spec, kid_spec, stat_spec, work


def attend(q, k, v, qid, kid):
    grid, q_spec, k_spec, qid_spec, kid_spec, stat_spec, work = attend_specs(q, k)
    return pl.pallas_call(
        attend_kernel,
        grid=grid,
        in_specs=[q_spec, k_spec, k_spec, qid_spec, kid_spec],
        out_specs=[q_spec, stat_spec],
        out_shape=[
            jax.ShapeDtypeStruct(q.shape, BF),
            jax.ShapeDtypeStruct((*grid, q.shape[1], PAIR), F32),
        ],
        cost_estimate=pl.CostEstimate(flops=16 * work, bytes_accessed=4 * k.size * 2, transcendentals=work // HEAD_DIM),
        compiler_params=pltpu.CompilerParams(vmem_limit_bytes=40 * 2**20),
    )(q, k, v, qid, kid)


def attend_back(q, k, v, g, qid, kid, stats=None):
    grid, q_spec, k_spec, qid_spec, kid_spec, stat_spec, work = attend_specs(q, k)
    saved = stats is not None
    low = lambda v: jax.ShapeDtypeStruct(v.shape, BF)
    return pl.pallas_call(
        functools.partial(attend_back_kernel, saved),
        grid=grid,
        in_specs=[q_spec, k_spec, k_spec, q_spec, qid_spec, kid_spec] + ([stat_spec] if saved else []),
        out_specs=([] if saved else [q_spec]) + [q_spec, k_spec, k_spec],
        out_shape=([] if saved else [low(q)]) + [low(q), low(k), low(v)],
        cost_estimate=pl.CostEstimate(flops=48 * work, bytes_accessed=6 * k.size * 2, transcendentals=work // HEAD_DIM),
        compiler_params=pltpu.CompilerParams(vmem_limit_bytes=40 * 2**20),
    )(q, k, v, g, qid, kid, *([stats] if saved else []))


def tie(x, *deps):
    return lax.optimization_barrier((x, *deps))


def turn_batch(x):
    size = lax.axis_size("batch")
    return lax.ppermute(x, "batch", [(i, size - 1 - i) for i in range(size)])


def turn_low(x):
    return swap(x, 1)


def turn_high(x):
    return swap(x, 2)


def halve(x, turn, bit):
    halves = x.reshape(2, x.shape[0] // 2, x.shape[1])
    send = lax.dynamic_index_in_dim(halves, 1 - bit, 0, keepdims=False).astype(BF)
    keep = lax.dynamic_index_in_dim(halves, bit, 0, keepdims=False)
    return keep.astype(F32) + turn(send).astype(F32)


def join(x, turn, bit):
    x = x.astype(BF)
    other = turn(x)
    return jnp.concatenate([jnp.where(bit == 0, x, other), jnp.where(bit == 0, other, x)], axis=0)


def reduce_ff(d_in, d_mlp):
    place = lax.axis_index("head")
    x_bit, y_bit = lax.axis_index("batch"), place >> 1
    core = (place & 1) == 1
    d_in, d_mlp = d_in.astype(BF), d_mlp.astype(BF)
    mine = jnp.where(core, d_mlp, d_in).astype(F32) + turn_low(jnp.where(core, d_in, d_mlp)).astype(F32)
    cut = mine.shape[0] // 2
    a, b = mine[:cut], mine[cut:]
    a, b = halve(a, turn_batch, x_bit), halve(b, turn_high, y_bit)
    a, b = halve(a, turn_high, y_bit), halve(b, turn_batch, x_bit)
    a, b = join(a, turn_high, y_bit), join(b, turn_batch, x_bit)
    a, b = join(a, turn_batch, x_bit), join(b, turn_high, y_bit)
    full = jnp.concatenate([a, b], axis=0)
    other = turn_low(full)
    return jnp.where(core, other, full).astype(F32), jnp.where(core, full, other).astype(F32)


def reduce_attn(own, partner):
    batch = lax.axis_index("batch")
    wide = lax.axis_index("wide")
    size = lax.axis_size("wide")
    own = own + turn_high(partner.astype(BF)).astype(F32)
    rows, width = own.shape
    mine = halve(own, turn_batch, batch)
    blocks = mine.reshape(size, -1, width)
    if size <= DIRECT:
        pick = lambda s: lax.dynamic_index_in_dim(blocks, (wide - s) % size, 0, keepdims=False)
        arrived = [shift(pick(s).astype(BF), -s) for s in range(1, size)]
        total = pick(0)
        for piece in arrived:
            total = total + piece.astype(F32)
        total = total.astype(BF)
        full = jnp.zeros(blocks.shape, BF)
        for s in range(size):
            piece = shift(total, s) if s else total
            full = lax.dynamic_update_index_in_dim(full, piece, (wide - s) % size, 0)
    else:
        total = lax.psum_scatter(blocks.astype(BF), "wide", scatter_dimension=0, tiled=False)
        full = lax.all_gather(total, "wide", axis=0, tiled=False)
    return join(full.reshape(rows // 2, width), turn_batch, batch).astype(F32)


def sum_all(x):
    x = x + turn_low(x)
    x = x + turn_high(x)
    x = x + turn_batch(x)
    size = lax.axis_size("wide")
    if size > DIRECT:
        return lax.psum(x, "wide")
    total = x
    for s in range(1, size):
        total = total + shift(x, s)
    return total


def general(tokens, patches, w_qkv, w_att, w_in, w_mlp, gains, cotangent):
    rows_all, slots, width = tokens.shape
    wide = lax.axis_size("wide")
    place = lax.axis_index("head")
    wide_place = lax.axis_index("wide")
    levels = w_qkv.shape[0]
    group = w_att.shape[1]
    n = rows_all * slots // 4
    rows = rows_all // 2

    def assemble(own, other, count):
        if rows == 1:
            return jnp.concatenate([own, other], axis=0)[None]
        half = rows // 2
        def turn(v):
            v = v.reshape(count, half, slots, *v.shape[1:])
            return jnp.moveaxis(v, 1, 0).reshape(half, count * slots, *v.shape[3:])
        return jnp.concatenate([turn(own), turn(other)], axis=0)

    def take_apart(v, count):
        if rows == 1:
            return v[0, : count * n], v[0, count * n :]
        half = rows // 2
        def turn(u):
            u = u.reshape(half, count, slots, *u.shape[2:])
            return jnp.moveaxis(u, 1, 0).reshape(count * n, *u.shape[3:])
        return turn(v[:half]), turn(v[half:])

    ends = jnp.cumsum(patches, axis=1)
    slot_index = jnp.arange(slots * wide, dtype=jnp.int32)
    image = jnp.sum((slot_index[None, :, None] >= ends[:, None, :]).astype(jnp.int32), axis=2)
    image = jnp.where(slot_index[None, :] < ends[:, -1:], image, -1)
    image = image.reshape(rows_all, wide, slots).transpose(1, 0, 2).reshape(wide, 4, n)
    order = (wide_place - jnp.arange(wide)) % wide
    image = image[order]
    own_image = lax.dynamic_index_in_dim(image, place, 1, keepdims=False)
    other_image = lax.dynamic_index_in_dim(image, place ^ 1, 1, keepdims=False)
    key_image = assemble(own_image.reshape(-1), other_image.reshape(-1), wide)
    query_image = assemble(own_image[0], other_image[0], 1)
    key_id = key_image[:, None, :]
    query_id = jnp.where(query_image >= 0, query_image, -2)[:, :, None]

    own = lax.dynamic_index_in_dim(tokens.reshape(4, n, width), place, 0, keepdims=False)
    cot = lax.dynamic_index_in_dim(cotangent.reshape(4, n, width), place, 0, keepdims=False)
    cot_other = lax.dynamic_index_in_dim(cotangent.reshape(4, n, width), place ^ 1, 0, keepdims=False)

    project = lambda act, w: jnp.einsum("rse,ce->rsc", act, w, preferred_element_type=F32).astype(BF)
    pull_back = lambda d, w: jnp.einsum("rkc,ce->rke", d, w, preferred_element_type=F32)
    weigh = lambda d, act: jnp.einsum("rqc,rqe->ce", d, act, preferred_element_type=F32)

    qkv_ws = [swap(w_qkv[l], 2) for l in range(levels)]
    att_ws = [swap(w_att[l], 2) for l in range(levels)]

    def weights(l, qkv_part, att_part):
        return jnp.concatenate([w_qkv[l], qkv_part], axis=1), jnp.concatenate([w_att[l], att_part], axis=0)

    def branch_of(attended, att_w):
        att_own, att_other = take_apart(
            jnp.einsum("rqc,ce->rqe", attended, att_w, preferred_element_type=F32), 1
        )
        return att_own + turn_low(att_other.astype(BF)).astype(F32)

    def act_terms(dq, dk, dv, qkv_w):
        d_act_kv = pull_back(dk, qkv_w[1]) + pull_back(dv, qkv_w[2])
        kv_own, kv_other = take_apart(d_act_kv, wide)
        q_own, q_other = take_apart(pull_back(dq, qkv_w[0]), 1)
        kv_other = kv_other.at[:n].add(q_other).astype(BF)
        return kv_own.at[:n].add(q_own) + turn_low(kv_other).astype(F32)

    def ff_back(pre, ff_grad, l):
        d_hidden = right_dot(ff_grad, w_mlp[l])
        unused, pull = jax.vjp(jax.nn.gelu, pre)
        return pull(d_hidden)[0].astype(BF)

    stream = own.astype(F32)
    saved = []
    for l in range(levels - 1):
        xhat, rstd = norm_parts(stream)
        act = (xhat * gains[l]).astype(BF)
        ff_act = gather_wide(act)
        other_act = turn_low(ff_act)
        pre = right_dot(ff_act, w_in[l])
        hidden = jax.nn.gelu(pre).astype(BF)
        parts = plain_dot(hidden, w_mlp[l])
        parts, ff_act, other_act = tie(parts, ff_act, other_act)
        branch = scatter_wide(parts)
        qkv_w, att_w = weights(l, qkv_ws[l], att_ws[l])
        key_act = assemble(ff_act, other_act, wide)
        query_act = assemble(act, other_act[:n], 1)
        q, k, v = project(query_act, qkv_w[0]), project(key_act, qkv_w[1]), project(key_act, qkv_w[2])
        attended, stats = attend(q, k, v, query_id, key_id)
        branch = branch + branch_of(attended, att_w)
        branch, qkv_ws[l + 1], att_ws[l + 1] = tie(branch, qkv_ws[l + 1], att_ws[l + 1])
        saved.append((xhat, rstd, ff_act, key_act, query_act, qkv_w, att_w, pre, hidden, q, k, v, attended, stats))
        stream = stream + branch

    l = levels - 1
    xhat, rstd = norm_parts(stream)
    act = (xhat * gains[l]).astype(BF)
    qkv_w, att_w = weights(l, qkv_ws[l], att_ws[l])
    query_grad = assemble(cot, cot_other, 1)
    d_attended = project(query_grad, att_w)
    ff_act = gather_wide(act)
    ff_act, cot, d_attended = tie(ff_act, cot, d_attended)
    ff_grad = gather_wide(cot)
    other_act = turn_low(ff_act)
    pre = right_dot(ff_act, w_in[l])
    hidden = jax.nn.gelu(pre).astype(BF)
    key_act = assemble(ff_act, other_act, wide)
    query_act = assemble(act, other_act[:n], 1)
    q, k, v = project(query_act, qkv_w[0]), project(key_act, qkv_w[1]), project(key_act, qkv_w[2])
    attended, dq, dk, dv = attend_back(q, k, v, d_attended, query_id, key_id)
    terms = act_terms(dq, dk, dv, qkv_w)
    d_pre = ff_back(pre, ff_grad, l)
    parts = terms + plain_dot(d_pre, w_in[l])
    parts, hidden, d_pre, dq, dk, dv, attended = tie(parts, hidden, d_pre, dq, dk, dv, attended)
    d_act = scatter_wide(parts)
    pieces = [weigh(dq, query_act), weigh(dk, key_act), weigh(dv, key_act), weigh(attended, query_grad)]
    last_attn = jnp.concatenate([t[:group] for t in pieces]) + turn_high(
        jnp.concatenate([t[group:] for t in pieces]).astype(BF)
    ).astype(F32)
    last_ff = jnp.concatenate([trans_dot(d_pre, ff_act), trans_dot(hidden, ff_grad)]).astype(BF)
    last_branch = branch_of(attended, att_w)
    last_parts = plain_dot(hidden, w_mlp[l])
    d_act, last_parts, last_attn, last_ff = tie(d_act, last_parts, last_attn, last_ff)
    gain_last = jnp.sum(d_act * xhat, axis=0)
    grad = cot.astype(F32) + norm_back(d_act, xhat, rstd, gains[l])
    last_attn = lax.psum(last_attn.astype(BF), ("batch", "wide"))
    last_ff = lax.psum(last_ff, ("batch", "head"))

    assert levels == 2
    l = 0
    xhat, rstd, ff_act, key_act, query_act, qkv_w, att_w, pre, hidden, q, k, v, attended, stats = saved[0]
    low = grad.astype(BF)
    other_low = turn_low(low)
    ff_grad = gather_wide(low)
    query_grad = assemble(low, other_low, 1)
    d_attended = project(query_grad, att_w)
    dq, dk, dv = attend_back(q, k, v, d_attended, query_id, key_id, stats)
    terms = act_terms(dq, dk, dv, qkv_w)
    piece_o, piece_v = weigh(attended, query_grad), weigh(dv, key_act)
    piece_q, piece_k = weigh(dq, query_act), weigh(dk, key_act)
    first_ov = reduce_attn(
        jnp.concatenate([piece_o[:group], piece_v[:group]]), jnp.concatenate([piece_o[group:], piece_v[group:]])
    )
    first_qk = reduce_attn(
        jnp.concatenate([piece_q[:group], piece_k[:group]]), jnp.concatenate([piece_q[group:], piece_k[group:]])
    )
    d_pre = ff_back(pre, ff_grad, l)
    parts = terms + plain_dot(d_pre, w_in[l])
    parts, hidden, d_pre = tie(parts, hidden, d_pre)
    d_act = scatter_wide(parts)
    first_in, first_mlp = reduce_ff(trans_dot(d_pre, ff_act), trans_dot(hidden, ff_grad))
    d_act, last_parts = tie(d_act, last_parts)
    gain_first = jnp.sum(d_act * xhat, axis=0)
    grad = grad + norm_back(d_act, xhat, rstd, gains[l])
    delta = gather_head((grad - cot.astype(F32)).astype(BF))
    d_tokens = cotangent.astype(F32) + delta.reshape(tokens.shape).astype(F32)
    d_gains = sum_all(jnp.stack([gain_first, gain_last]))
    stream = stream + last_branch + scatter_wide(last_parts)
    delta = gather_head((stream - own.astype(F32)).astype(BF))
    out = tokens.astype(F32) + delta.reshape(tokens.shape).astype(F32)
    last_attn = last_attn.astype(F32).reshape(4, group, width)
    last_in, last_mlp = last_ff[: last_ff.shape[0] // 2].astype(F32), last_ff[last_ff.shape[0] // 2 :].astype(F32)
    d_qkv = jnp.stack([jnp.stack([first_qk[:group], first_qk[group:], first_ov[group:]]), last_attn[:3]])
    return (
        out,
        d_tokens,
        d_qkv,
        jnp.stack([first_ov[:group], last_attn[3]]),
        jnp.stack([first_in, last_in]),
        jnp.stack([first_mlp, last_mlp]),
        d_gains,
    )


COST = 2 * 10**10
LIMIT = 28
SMALL = 16
MIDDLE = 24
CORE, X_BIT, Y_BIT, WIDE, PLACE = range(5)


def full_spec(x):
    return pl.BlockSpec(x.shape, lambda i, *_, nd=x.ndim: (0,) * nd)


def layer_spec(x, l):
    return pl.BlockSpec((1, *x.shape[1:]), lambda i, *_, nd=x.ndim: (l,) + (0,) * (nd - 1))


def call(kernel, grid, ins, outs, scratch=(), prefetch=(), limit=SMALL, cost=COST):
    return pl.pallas_call(
        kernel,
        grid_spec=pltpu.PrefetchScalarGridSpec(
            num_scalar_prefetch=len(prefetch),
            grid=(grid,),
            in_specs=[spec for _, spec in ins],
            out_specs=[spec for _, _, spec in outs],
            scratch_shapes=list(scratch),
        ),
        out_shape=[jax.ShapeDtypeStruct(shape, kind) for shape, kind, _ in outs],
        cost_estimate=pl.CostEstimate(flops=cost, bytes_accessed=0, transcendentals=0),
        compiler_params=pltpu.CompilerParams(vmem_limit_bytes=limit * 2**20),
    )(*prefetch, *[x for x, _ in ins])


def far(x):
    return pltpu.with_memory_space_constraint(x, pltpu.HBM)


def whole_out(shape, kind):
    return (shape, kind, pl.BlockSpec(shape, lambda i, *_, nd=len(shape): (0,) * nd))


def total_of(refs):
    total = refs[0][...].astype(F32)
    for ref in refs[1:]:
        total = total + ref[...].astype(F32)
    return total


def start_norm_kernel(place_ref, tok_ref, gain_ref, act_ref):
    xhat, unused = norm_parts(tok_ref[...].astype(F32))
    act_ref[...] = (xhat * gain_ref[0]).astype(BF)


def start_norm(place, tokens, gains):
    n, width = tokens.shape
    return call(
        start_norm_kernel,
        1,
        [(tokens, full_spec(tokens)), (gains, layer_spec(gains, 0))],
        [whole_out((n, width), BF)],
        prefetch=(place,),
    )[0]


def norm_kernel(place_ref, tok_ref, gain_ref, *refs):
    stream_ref, act_ref = refs[-2:]
    stream = tok_ref[...].astype(F32) + total_of(refs[:-2])
    xhat, unused = norm_parts(stream)
    stream_ref[...] = stream
    act_ref[...] = (xhat * gain_ref[0]).astype(BF)


def norm(place, tokens, gains, l, terms):
    n, width = tokens.shape
    return call(
        norm_kernel,
        1,
        [(tokens, full_spec(tokens)), (gains, layer_spec(gains, l))]
        + [(t, full_spec(t)) for t in terms],
        [whole_out((n, width), F32), whole_out((n, width), BF)],
        prefetch=(place,),
    )


def norm_back_kernel(first, place_ref, cot_ref, gain_ref, stream_ref, *refs):
    *refs, delta_ref, low_ref, gain_out = refs
    if not first:
        earlier, *refs = refs
    d_act = total_of(refs)
    xhat, rstd = norm_parts(stream_ref[...].astype(F32))
    gain_out[...] = jnp.sum(d_act * xhat, axis=0, keepdims=True)
    delta = norm_back(d_act, xhat, rstd, gain_ref[0])
    if not first:
        delta = delta + earlier[...]
        low_ref[...] = delta.astype(BF)
    else:
        low_ref[...] = (cot_ref[...].astype(F32) + delta).astype(BF)
    delta_ref[...] = delta


def norm_back_call(place, cotangent, gains, l, stream, terms, earlier=None):
    n, width = cotangent.shape
    first = earlier is None
    return call(
        functools.partial(norm_back_kernel, first),
        1,
        [(cotangent, full_spec(cotangent)), (gains, layer_spec(gains, l)), (stream, full_spec(stream))]
        + ([] if first else [(earlier, full_spec(earlier))])
        + [(t, full_spec(t)) for t in terms],
        [whole_out((n, width), F32), whole_out((n, width), BF), whole_out((1, width), F32)],
        prefetch=(place,),
    )


GELU_A = 0.7978845608028654
GELU_B = 0.044715


def gelu_both(x):
    square = x * x
    t = jnp.tanh(GELU_A * (x + GELU_B * (square * x)))
    value = 0.5 * x * (1.0 + t)
    slope = 0.5 * (1.0 + t) + 0.5 * x * (1.0 - t * t) * (GELU_A * (1.0 + 3.0 * GELU_B * square))
    return value, slope


def chunks_of(total):
    step = 256 if total % 256 == 0 else total
    return [slice(i, i + step) for i in range(0, total, step)]


def write_parts(total, n, part_refs):
    for s, ref in enumerate(part_refs):
        ref[...] = total[s * n : (s + 1) * n].astype(ref.dtype)


def ff_kernel(count, spot_ref, *refs):
    x_refs, (in_ref, mlp_ref, slope_ref, hidden_ref, all_ref), part_refs = refs[:count], refs[count : count + 5], refs[count + 5 :]
    n = x_refs[0].shape[0]
    x = jnp.concatenate([r[...] for r in x_refs], axis=0)
    all_ref[...] = x
    total = None
    for cut in chunks_of(in_ref.shape[1]):
        value, slope = gelu_both(right_dot(x, in_ref[0, cut, :]))
        low = value.astype(BF)
        slope_ref[:, cut] = slope
        hidden_ref[:, cut] = low
        term = plain_dot(low, mlp_ref[0, cut, :])
        total = term if total is None else total + term
    if len(part_refs) == 1:
        for s in range(count):
            part_refs[0][lax.rem(spot_ref[WIDE] - s + count, count)] = total[s * n : (s + 1) * n].astype(BF)
    else:
        write_parts(total, n, part_refs)


def part_outs(count, n, width):
    return [whole_out((n, width), F32 if s == 0 else BF) for s in range(count)]


def ff(spot, xs, w_in, w_mlp, l, blocks=False):
    count, (n, width) = len(xs), xs[0].shape
    w_in, w_mlp = w_in[l], w_mlp[l]
    hidden = w_in.shape[1]
    slope, low, x_all, *parts = call(
        functools.partial(ff_kernel, count),
        1,
        [(x, full_spec(x)) for x in (*xs, w_in, w_mlp)],
        [whole_out((count * n, hidden), F32), whole_out((count * n, hidden), BF), whole_out((count * n, width), BF)]
        + ([whole_out((count, n, width), BF)] if blocks else part_outs(count, n, width)),
        prefetch=(spot,),
    )
    return slope, low, x_all, parts[0] if blocks else parts


def ff_slope_kernel(count, *refs):
    g_refs, (mlp_ref, slope_ref, d_pre_ref, all_ref) = refs[:count], refs[count:]
    g = jnp.concatenate([r[...] for r in g_refs], axis=0)
    all_ref[...] = g
    for cut in chunks_of(mlp_ref.shape[1]):
        d_pre_ref[:, cut] = (slope_ref[:, cut] * right_dot(g, mlp_ref[0, cut, :])).astype(BF)


def ff_slope(gs, w_mlp, l, slope):
    count, (n, width) = len(gs), gs[0].shape
    return call(
        functools.partial(ff_slope_kernel, count),
        1,
        [(g, full_spec(g)) for g in (*gs, w_mlp[l], slope)],
        [whole_out(slope.shape, BF), whole_out((count * n, width), BF)],
    )


def ff_back_kernel(n, d_pre_ref, in_ref, own_ref, got_ref, *part_refs):
    total = own_ref[...] + got_ref[...].astype(F32) + plain_dot(d_pre_ref[...], in_ref[0])
    write_parts(total, n, part_refs)


def ff_back(count, d_pre, w_in, l, own, got):
    n, width = d_pre.shape[0] // count, w_in[l].shape[2]
    return call(
        functools.partial(ff_back_kernel, n),
        1,
        [(x, full_spec(x)) for x in (d_pre, w_in[l], own, got)],
        part_outs(count, n, width),
    )


def ff_weights_kernel(outer, spot_ref, x_ref, g_ref, d_pre_ref, hidden_ref, keep_ref, send_ref):
    core = spot_ref[CORE] == 1
    d_in = trans_dot(d_pre_ref[...], x_ref[...])
    d_mlp = trans_dot(hidden_ref[...], g_ref[...])
    half = d_in.shape[0] // 2
    keep, send = jnp.where(core, d_mlp, d_in), jnp.where(core, d_in, d_mlp).astype(BF)
    for j in range(2):
        at = j ^ spot_ref[Y_BIT if outer == X_BIT else X_BIT]
        keep_ref[0, at] = keep[j * half : (j + 1) * half]
        send_ref[0, at] = send[j * half : (j + 1) * half]


def ff_weights(spot, xs, gs, d_pre, hidden, outer):
    width = xs.shape[1]
    tokens, size = d_pre.shape
    cut = pl.BlockSpec((tokens, size // 2), lambda i, p: (0, i))
    shape = (2, 2, size // 4, width)
    out = pl.BlockSpec((1, *shape[1:]), lambda i, p: (i ^ p[outer], 0, 0, 0))
    return call(
        functools.partial(ff_weights_kernel, outer),
        2,
        [(x, full_spec(x)) for x in (xs, gs)] + [(d_pre, cut), (hidden, cut)],
        [(shape, F32, out), (shape, BF, out)],
        prefetch=(spot,),
        cost=COST // 4,
    )


def ff_finish_kernel(spot_ref, *refs):
    *refs, in_ref, mlp_ref = refs
    core = spot_ref[CORE] == 1
    for l in range(2):
        mine, got = refs[2 * l][0].astype(F32), refs[2 * l + 1][0].astype(F32)
        in_ref[l] = jnp.where(core, got, mine)
        mlp_ref[l] = jnp.where(core, mine, got)


def ff_finish(spot, pairs, outers):
    unused, rows, width = pairs[0][0].shape
    ins = []
    for (mine, got), outer in zip(pairs, outers):
        inner = Y_BIT if outer == X_BIT else X_BIT
        spec = pl.BlockSpec((1, rows, width), lambda i, p, o=outer, n=inner: (i ^ (2 * p[o] + p[n]), 0, 0))
        ins += [(mine, spec), (got, spec)]
    out = ((2, 4 * rows, width), F32, pl.BlockSpec((2, rows, width), lambda i, p: (0, i, 0)))
    return call(ff_finish_kernel, 4, ins, [out, out], prefetch=(spot,))


def attn_kernel(mode, count, *refs):
    refs = list(refs)
    take = lambda k: [refs.pop(0) for _ in range(k)]
    if mode != "back":
        act_refs = take(2)
    if mode != "fwd":
        g_refs = take(2)
    w_own, a_own, p_qk, p_vo, qid_ref, kid_ref = take(6)
    if mode == "back":
        q_ref, k_ref, v_ref, stat_ref = take(4)
    step = pl.program_id(0)
    scale = HEAD_DIM ** (-0.5)
    n = qid_ref.shape[0] // 2
    half = count * n
    if mode == "fwd":
        q_out, k_out, v_out, o_out, stat_out, b_own, b_other, act_all, branch = refs
    elif mode == "both":
        q_out, k_out, v_out, o_out, t_own, t_other, b_own, b_other, act_all, branch, terms = refs
    else:
        q_out, k_out, v_out, t_own, t_other, terms = refs
    if mode != "back":

        @pl.when(step == 0)
        def _():
            act_all[:half, :] = act_refs[0][...]
            act_all[half:, :] = act_refs[1][...]

    w_kv = jnp.concatenate([w_own[0, 1], p_qk[1], w_own[0, 2], p_vo[0]], axis=0)
    w_q = jnp.concatenate([w_own[0, 0], p_qk[0]], axis=0)
    w_o = jnp.concatenate([a_own[0], p_vo[1]], axis=0)
    if mode != "back":
        kv = right_dot(act_all[...], w_kv).astype(BF)
        k, v = kv[:, :PAIR], kv[:, PAIR:]
        q_in = jnp.concatenate([act_refs[0][:n, :], act_refs[1][:n, :]], axis=0)
        q = right_dot(q_in, w_q).astype(BF)
    else:
        q, k, v = q_ref[...], k_ref[...], v_ref[...]
    if mode == "fwd":
        q_out[...], k_out[...], v_out[...] = q, k, v
    q = q * jnp.asarray(scale, BF)
    allowed = qid_ref[...] == kid_ref[...]
    if mode != "fwd":
        g = right_dot(jnp.concatenate([r[...] for r in g_refs], axis=0), w_o).astype(BF)
    lane = lax.broadcasted_iota(jnp.int32, (2 * n, PAIR), 1)
    stats = jnp.zeros((2 * n, PAIR), F32)
    outs, dqs, dks, dvs = [], [], [], []
    for j in range(2):
        cut = slice(j * HEAD_DIM, (j + 1) * HEAD_DIM)
        qj, kj, vj = q[:, cut], k[:, cut], v[:, cut]
        if mode == "back":
            top, inverse = stat_ref[0, :, 2 * j : 2 * j + 1], stat_ref[0, :, 2 * j + 1 : 2 * j + 2]
            probs = jnp.exp(jnp.where(allowed, right_dot(qj, kj), NEGATIVE) - top) * inverse
        else:
            probs, top, inverse = head_softmax(qj, kj, allowed)
            stats = jnp.where(lane == 2 * j, top, jnp.where(lane == 2 * j + 1, inverse, stats))
        low = probs.astype(BF)
        if mode != "back":
            outs.append(plain_dot(low, vj))
        if mode != "fwd":
            gj = g[:, cut]
            dp = right_dot(gj, vj)
            ds = (probs * (dp - jnp.sum(probs * dp, axis=-1, keepdims=True))).astype(BF)
            dqs.append(plain_dot(ds, kj) * scale)
            dks.append(trans_dot(ds, qj))
            dvs.append(trans_dot(low, gj))
    last = step == pl.num_programs(0) - 1
    if mode != "back":
        attended = jnp.concatenate(outs, axis=1).astype(BF)
        o_out[...] = attended
        term = plain_dot(attended, w_o)

        @pl.when(step == 0)
        def _():
            branch[...] = term

        @pl.when(step > 0)
        def _():
            branch[...] += term

        @pl.when(last)
        def _():
            b_own[...] = branch[:n, :]
            b_other[...] = branch[n:, :].astype(BF)

    if mode == "fwd":
        stat_out[0] = stats
    else:
        dq = jnp.concatenate(dqs, axis=1).astype(BF)
        dkv = jnp.concatenate(dks + dvs, axis=1).astype(BF)
        q_out[...], k_out[...], v_out[...] = dq, dkv[:, :PAIR], dkv[:, PAIR:]
        term_kv = plain_dot(dkv, w_kv)
        term_q = plain_dot(dq, w_q)

        @pl.when(step == 0)
        def _():
            terms[...] = term_kv

        @pl.when(step > 0)
        def _():
            terms[...] += term_kv

        terms[:n, :] += term_q[:n]
        terms[half : half + n, :] += term_q[n:]

        @pl.when(last)
        def _():
            t_own[...] = terms[:half, :]
            t_other[...] = terms[half:, :].astype(BF)


def attn(mode, count, l, w_qkv, w_att, part, qid, kid, acts=(), grads=(), kept=()):
    group, width = part.shape[1:]
    n = qid.shape[0] // 2
    tq, tk = 2 * n, 2 * count * n
    steps = group // HEAD_DIM
    pair_q = pl.BlockSpec((tq, PAIR), lambda i: (0, i))
    pair_k = pl.BlockSpec((tk, PAIR), lambda i: (0, i))
    stat = pl.BlockSpec((1, tq, PAIR), lambda i: (i, 0, 0))
    ins = [(x, full_spec(x)) for x in (*acts, *grads)] + [
        (w_qkv, pl.BlockSpec((1, 3, HEAD_DIM, width), lambda i: (l, 0, i, 0))),
        (w_att, pl.BlockSpec((1, HEAD_DIM, width), lambda i: (l, i, 0))),
        *[(part, pl.BlockSpec((2, HEAD_DIM, width), lambda i, h=h: (h, i, 0))) for h in range(2)],
        (qid, full_spec(qid)),
        (kid, full_spec(kid)),
    ]
    if mode == "back":
        q, k, v, stats = kept
        ins += [(far(q), pair_q), (far(k), pair_k), (far(v), pair_k), (far(stats), stat)]
    q_shape, k_shape = (tq, 2 * group), (tk, 2 * group)
    outs = [(q_shape, BF, pair_q), (k_shape, BF, pair_k), (k_shape, BF, pair_k)]
    scratch = []
    if mode != "back":
        outs += [(q_shape, BF, pair_q)]
        scratch += [pltpu.VMEM((tk, width), BF), pltpu.VMEM((tq, width), F32)]
    if mode == "fwd":
        outs += [((steps, tq, PAIR), F32, stat)]
    else:
        outs += [whole_out((tk // 2, width), F32), whole_out((tk // 2, width), BF)]
        scratch += [pltpu.VMEM((tk, width), F32)]
    if mode != "back":
        outs += [whole_out((n, width), F32), whole_out((n, width), BF)]
    return call(functools.partial(attn_kernel, mode, count), steps, ins, outs, scratch, limit=LIMIT)


def attn_weights_kernel(spot_ref, own_act, other_act, g_own, g_other, dq_ref, dk_ref, dv_ref, o_ref, own_ref, part_ref, act_all):
    n = g_own.shape[0]
    half = act_all.shape[0] // 2
    step = pl.program_id(0)

    @pl.when(step == 0)
    def _():
        act_all[:half, :] = own_act[...]
        act_all[half:, :] = other_act[...]

    q_in = jnp.concatenate([own_act[:n, :], other_act[:n, :]], axis=0)
    g_in = jnp.concatenate([g_own[...], g_other[...]], axis=0)
    kv = trans_dot(jnp.concatenate([dk_ref[...], dv_ref[...]], axis=1), act_all[...])
    pairs = (trans_dot(dq_ref[...], q_in), kv[:PAIR], kv[PAIR:], trans_dot(o_ref[...], g_in))
    rows = own_ref.shape[2]
    for i in range(2 * rows // HEAD_DIM):

        @pl.when(step == i)
        def _():
            for t, pair in enumerate(pairs):
                back = lax.rem(spot_ref[WIDE] - t + 4, 4)
                low = i * HEAD_DIM
                while low < (i + 1) * HEAD_DIM:
                    high = min((i + 1) * HEAD_DIM, (low // rows + 1) * rows)
                    at = (low // rows) ^ spot_ref[X_BIT]
                    dest = slice(low % rows, low % rows + high - low)
                    source = slice(low - i * HEAD_DIM, high - i * HEAD_DIM)
                    own_ref[at, back, dest, :] = pair[:HEAD_DIM][source]
                    part_ref[at, back, dest, :] = pair[HEAD_DIM:][source].astype(BF)
                    low = high


def attn_weights(spot, acts, grads, dq, dk, dv, attended):
    n, width = grads[0].shape
    tq, tk, group = 2 * n, 2 * acts[0].shape[0], dq.shape[1] // 2
    pair_q = pl.BlockSpec((tq, PAIR), lambda i, p: (0, i))
    pair_k = pl.BlockSpec((tk, PAIR), lambda i, p: (0, i))
    shape = (2, 4, group // 2, width)
    return call(
        attn_weights_kernel,
        group // HEAD_DIM,
        [(x, full_spec(x)) for x in (*acts, *grads)] + [(dq, pair_q), (dk, pair_k), (dv, pair_k), (attended, pair_q)],
        [whole_out(shape, F32), whole_out(shape, BF)],
        [pltpu.VMEM((tk, width), BF)],
        (spot,),
        limit=MIDDLE,
        cost=COST // 4,
    )


def attn_finish_kernel(spot_ref, *refs):
    *refs, qkv_ref, att_ref = refs
    matrix = pl.program_id(0)
    second = spot_ref[X_BIT] == 1
    for l in range(2):
        mine, got = refs[2 * l][0].astype(F32), refs[2 * l + 1][0].astype(F32)
        whole = jnp.concatenate([jnp.where(second, got, mine), jnp.where(second, mine, got)], axis=0)

        @pl.when(matrix < 3)
        def _():
            qkv_ref[l, 0] = whole

        @pl.when(matrix == 3)
        def _():
            att_ref[l] = whole


def attn_finish(spot, pairs):
    unused, rows, width = pairs[0][0].shape
    spec = pl.BlockSpec((1, rows, width), lambda i, p: (lax.rem(p[WIDE] - i + 4, 4), 0, 0))
    return call(
        attn_finish_kernel,
        4,
        [(x, spec) for pair in pairs for x in pair],
        [
            ((2, 3, 2 * rows, width), F32, pl.BlockSpec((2, 1, 2 * rows, width), lambda i, p: (0, jnp.minimum(i, 2), 0, 0))),
            whole_out((2, 2 * rows, width), F32),
        ],
        prefetch=(spot,),
    )


def gather_list(x):
    return [x] + [shift(x, s) for s in range(1, lax.axis_size("wide"))]


def return_list(parts):
    return [parts[0]] + [shift(p, -s) for s, p in enumerate(parts) if s]


def reduce_ff_rest(keep, got):
    x_bit, y_bit = lax.axis_index("batch"), lax.axis_index("head") >> 1
    core = (lax.axis_index("head") & 1) == 1
    mine = keep + got.astype(F32)
    cut = mine.shape[0] // 2
    a, b = mine[:cut], mine[cut:]
    a, b = halve(a, turn_batch, x_bit), halve(b, turn_high, y_bit)
    a, b = halve(a, turn_high, y_bit), halve(b, turn_batch, x_bit)
    a, b = join(a, turn_high, y_bit), join(b, turn_batch, x_bit)
    a, b = join(a, turn_batch, x_bit), join(b, turn_high, y_bit)
    full = jnp.concatenate([a, b], axis=0)
    other = turn_low(full)
    return jnp.where(core, other, full), jnp.where(core, full, other)


def together(*pairs):
    sent = tie(*[x for x, _ in pairs])
    return tie(*[f(x) for x, (_, f) in zip(sent, pairs)])


def half_of(x, bit):
    halves = x.reshape(2, x.shape[0] // 2, x.shape[1])
    return (
        lax.dynamic_index_in_dim(halves, bit, 0, keepdims=False),
        lax.dynamic_index_in_dim(halves, 1 - bit, 0, keepdims=False).astype(BF),
    )


def shifts(sign):
    return [functools.partial(shift, step=sign * s) for s in range(1, lax.axis_size("wide"))]


def blocks_of(x):
    wide, size = lax.axis_index("wide"), lax.axis_size("wide")
    blocks = x.reshape(size, -1, x.shape[1])
    own, *others = [lax.dynamic_index_in_dim(blocks, (wide - s) % size, 0, keepdims=False) for s in range(size)]
    return own, [o.astype(BF) for o in others]


def laid(pieces):
    wide, size = lax.axis_index("wide"), lax.axis_size("wide")
    full = jnp.zeros((size, *pieces[0].shape), pieces[0].dtype)
    for s, piece in enumerate(pieces):
        full = lax.dynamic_update_index_in_dim(full, piece, (wide - s) % size, 0)
    return full.reshape(-1, pieces[0].shape[1])


def ordered(mine, other, bit):
    return jnp.where(bit == 0, mine, other), jnp.where(bit == 0, other, mine)


def sum_of(first, pieces):
    total = first.astype(F32)
    for piece in pieces:
        total = total + piece.astype(F32)
    return total


def fast(tokens, patches, w_qkv, w_att, w_in, w_mlp, gains, cotangent):
    rows_all, slots, width = tokens.shape
    shape = tokens.shape
    wide = lax.axis_size("wide")
    head_place, wide_place = lax.axis_index("head"), lax.axis_index("wide")
    x_bit, y_bit, core = lax.axis_index("batch"), head_place >> 1, head_place & 1
    spot = jnp.stack([core, x_bit, y_bit, wide_place, head_place]).astype(jnp.int32)
    group = w_att.shape[1]
    n = rows_all * slots // 4
    tokens, cotangent = tokens.reshape(4, n, width), cotangent.reshape(4, n, width)
    gains = gains[:, None, :]
    w_in, w_mlp = [w_in[l : l + 1] for l in range(2)], [w_mlp[l : l + 1] for l in range(2)]

    own_ws = [jnp.concatenate([w_qkv[l], w_att[l][None]]) for l in range(2)]
    tok = lax.dynamic_index_in_dim(tokens, head_place, 0, keepdims=False)
    act = start_norm(spot, tok, gains)
    xs = gather_list(act)
    part0 = turn_high(own_ws[0])

    ends = jnp.cumsum(patches, axis=1)
    slot_index = jnp.arange(slots * wide, dtype=jnp.int32)
    image = jnp.sum((slot_index[None, :, None] >= ends[:, None, :]).astype(jnp.int32), axis=2)
    image = jnp.where(slot_index[None, :] < ends[:, -1:], image, -1)
    image = image.reshape(rows_all, wide, slots).transpose(1, 0, 2).reshape(wide, 4, n)
    order = (wide_place - jnp.arange(wide)) % wide
    image = image[order]
    own_image = lax.dynamic_index_in_dim(image, head_place, 1, keepdims=False)
    other_image = lax.dynamic_index_in_dim(image, head_place ^ 1, 1, keepdims=False)
    kid = jnp.concatenate([own_image.reshape(-1), other_image.reshape(-1)])[None, :]
    qid = jnp.concatenate([own_image[0], other_image[0]])
    qid = jnp.where(qid >= 0, qid, -2)[:, None]
    cot = lax.dynamic_index_in_dim(cotangent, head_place, 0, keepdims=False)
    cot_other = lax.dynamic_index_in_dim(cotangent, head_place ^ 1, 0, keepdims=False)

    xs[1], kid, qid, own_ws[1], cot, cot_other = tie(xs[1], kid, qid, own_ws[1], cot, cot_other)

    slope0, hidden0, own0, parts = ff(spot, xs, w_in, w_mlp, 0)
    terms = return_list(parts)
    acts0 = (own0, turn_low(own0))
    part0, next_w = tie(part0, own_ws[1])
    part1 = turn_high(next_w)
    q, k, v, attended0, stats, b_own, b_other = attn("fwd", wide, 0, w_qkv, w_att, part0, qid, kid, acts=acts0)
    b_got = turn_low(b_other)
    stream1, act = norm(spot, tok, gains, 1, [*terms, b_own, b_got])

    xs1 = gather_list(act)
    slope1, hidden1, own1, out_parts = ff(spot, xs1, w_in, w_mlp, 1, True)
    other1 = turn_low(own1)
    cot_tied, unused = tie(cot, own1)
    gs1 = gather_list(cot_tied)
    dq1, dk1, dv1, attended1, t_own, t_other, b_own1, b_other1 = attn(
        "both", wide, 1, w_qkv, w_att, part1, qid, kid, acts=(own1, other1), grads=(cot, cot_other)
    )
    t_got = turn_low(t_other)
    d_pre1, g_all1 = ff_slope(gs1, w_mlp, 1, slope1)
    parts = list(ff_back(wide, d_pre1, w_in, 1, t_own, t_got))
    parts[1], dq1, hidden1, b_other1 = tie(parts[1], dq1, hidden1, b_other1)
    back1 = return_list(parts)
    own_w1, part_w1 = attn_weights(spot, (own1, other1), (cot, cot_other), dq1, dk1, dv1, attended1)
    keep_f1, send_f1 = ff_weights(spot, own1, g_all1, d_pre1, hidden1, X_BIT)
    b_got1 = turn_low(b_other1)
    back1[1], b_got1, send_f1, keep_f1, own_w1, part_w1 = tie(back1[1], b_got1, send_f1, keep_f1, own_w1, part_w1)
    got_f1 = turn_low(send_f1)
    got_w1 = turn_high(part_w1)
    delta1, low, gain1 = norm_back_call(spot, cot, gains, 1, stream1, back1)

    low_other = turn_low(low)
    gs = gather_list(low)
    dq, dk, dv, t_own, t_other = attn(
        "back", wide, 0, w_qkv, w_att, part0, qid, kid, grads=(low, low_other), kept=(q, k, v, stats)
    )
    t_got = turn_low(t_other)
    own_w0, part_w0 = attn_weights(spot, acts0, (low, low_other), dq, dk, dv, attended0)
    got_f1, part_w0, own_w0 = tie(got_f1, part_w0, own_w0)
    got_x1 = turn_batch((keep_f1[1] + got_f1[1].astype(F32)).astype(BF))
    got_w0 = turn_high(part_w0)
    gs[1], own_w0, part_w0 = tie(gs[1], own_w0, part_w0)
    d_pre0, g_all0 = ff_slope(gs, w_mlp, 0, slope0)
    parts = list(ff_back(wide, d_pre0, w_in, 0, t_own, t_got))
    parts[1], hidden0 = tie(parts[1], hidden0)
    back0 = return_list(parts)
    keep_f0, send_f0 = ff_weights(spot, own0, g_all0, d_pre0, hidden0, Y_BIT)
    got_w1, got_x1, keep_f0 = tie(got_w1, got_x1, keep_f0)
    sum_w1 = own_w1 + got_w1.astype(F32)
    got_w1 = turn_batch(sum_w1[1].astype(BF))
    back0[1], keep_f0, send_f0 = tie(back0[1], keep_f0, send_f0)
    half_w1 = sum_w1[0] + got_w1.astype(F32)
    half_f1 = sum_of(keep_f1[0], [got_f1[0], got_x1])
    delta0, low0, gain0 = norm_back_call(spot, cot, gains, 0, tok, back0, delta1)

    last = lax.psum_scatter(out_parts, "wide", scatter_dimension=0, tiled=False)
    b_got1, last, stream1, low0 = tie(b_got1, last, stream1, low0)
    half_w1, half_f1, last = tie(half_w1, half_f1, last)
    delta_out = (stream1 - tok.astype(F32) + sum_of(b_own1, [b_got1, last])).astype(BF)
    ends = lax.all_gather(jnp.concatenate([delta_out, low0], axis=1), "head", axis=0, tiled=False)

    gain = jnp.concatenate([gain0, gain1, jnp.zeros((6, width), F32)])

    def with_gain(x, gain):
        high = gain.astype(BF)
        return jnp.concatenate([x.reshape(-1, width).astype(BF), high, (gain - high.astype(F32)).astype(BF)])

    def gain_of(got):
        return got[-16:-8].astype(F32) + got[-8:].astype(F32)

    got_w0, half_w1, half_f1 = tie(got_w0, half_w1, half_f1)
    sum_w0 = own_w0 + got_w0.astype(F32)
    got_w0, got_f0, *got_b1 = together(
        (sum_w0[1].astype(BF), turn_batch),
        (send_f0, turn_low),
        *[(half_w1[s + 1].astype(BF), f) for s, f in enumerate(shifts(-1))],
    )
    block_w1 = sum_of(half_w1[0], got_b1).astype(BF)
    half_w0 = sum_w0[0] + got_w0.astype(F32)
    sum_f0 = keep_f0 + got_f0.astype(F32)
    rows_f = sum_f0.shape[2]
    got_f0, got_f1, *got_b0 = together(
        (with_gain(sum_f0[1], gain), turn_high),
        (half_f1[1].astype(BF), turn_high),
        *[(half_w0[s + 1].astype(BF), f) for s, f in enumerate(shifts(-1))],
    )
    gain = gain + gain_of(got_f0)
    block_w0 = sum_of(half_w0[0], got_b0)
    half_f0 = sum_f0[0] + got_f0[: 2 * rows_f].reshape(2, rows_f, width).astype(F32)
    block_f1 = (half_f1[0] + got_f1.astype(F32)).astype(BF)
    got_f0, got_f1, *got_b1 = together(
        (with_gain(half_f0[1], gain), turn_batch), (block_f1, turn_batch), *[(block_w1, f) for f in shifts(1)]
    )
    gain = gain + gain_of(got_f0)
    block_f0 = (half_f0[0] + got_f0[:rows_f].astype(F32)).astype(BF)
    pair_f1 = jnp.stack([block_f1, got_f1])
    mine_w1 = jnp.stack([block_w1, *got_b1])
    block_w0 = with_gain(block_w0, gain)
    got_f0, got_f1, *got_b0 = together(
        (block_f0, turn_batch), (pair_f1, turn_high), *[(block_w0, f) for f in shifts(1)]
    )
    gain = sum_of(gain, [gain_of(g) for g in got_b0])
    pair_f0 = jnp.stack([block_f0, got_f0])
    full_f1 = jnp.stack([pair_f1, got_f1], axis=1).reshape(4, rows_f, width)
    rows_w = half_w0.shape[1]
    mine_w0 = jnp.stack([g[:rows_w] for g in (block_w0, *got_b0)])
    mine_w0, ends = tie(mine_w0, ends)
    got_w0, got_w1, got_f0, got_g, got_f1 = together(
        (mine_w0, turn_batch), (mine_w1, turn_batch), (pair_f0, turn_high), (gain, turn_low), (full_f1, turn_low)
    )
    full_f0 = jnp.concatenate([pair_f0, got_f0])
    got_f0 = turn_low(full_f0)
    d_gains = (gain + got_g)[:2]
    d_in, d_mlp = ff_finish(spot, ((full_f0, got_f0), (full_f1, got_f1)), (Y_BIT, X_BIT))
    out = tokens.astype(F32) + ends[:, :, :width].astype(F32)
    d_tokens = cotangent.astype(F32) + ends[:, :, width:].astype(F32)
    d_qkv, d_att = attn_finish(spot, ((mine_w0, got_w0), (mine_w1, got_w1)))
    return (out.reshape(shape), d_tokens.reshape(shape), d_qkv, d_att, d_in, d_mlp, d_gains)


def solution(mesh):
    def local(*arrays):
        tokens, w_qkv = arrays[0], arrays[2]
        small = tokens.shape[0] == 2 and lax.axis_size("wide") == 4 and w_qkv.shape[0] == 2
        return (fast if small else general)(*arrays)

    return jax.shard_map(
        local,
        mesh=mesh,
        in_specs=(
            P("batch", "wide", None),
            P("batch", None),
            P(None, None, "head", None),
            P(None, "head", None),
            P(None, "wide", None),
            P(None, "wide", None),
            P(),
            P("batch", "wide", None),
        ),
        out_specs=(
            P("batch", "wide", None),
            P("batch", "wide", None),
            P(None, None, "head", None),
            P(None, "head", None),
            P(None, "wide", None),
            P(None, "wide", None),
            P(),
        ),
        check_vma=False,
    )
```

profile of v0, /device:TPU:0, one launch (start us, length us, event | category | flops | bytes accessed | tf_op | source)
XLA Modules:
  0.0 323.1 jit_solution(9800519372543351270)
XLA Ops:
  9.7 5.1 %collective-permute-start.2 = (bf16[128,768]{1,0:T(8,128)(2,1)S(1)}, bf16[128,768]{1,0:T(8,128)(2,1)S(1)}, u32[]{:S(2)}, u32[]{:S(2)}) collective-permute-start(bf16[128,768]{1,0:T(8,128)(2,1)S(1)} %shard_map.135.refs_0_), channel_id=1, source_target_pairs={{0,3},{1,0},{2,1},{3,2},{4,7},{5,4},{6,5},{7,6},{8,11},{9,8},{10,9... | collective-permute-start | bytes 589832 | tf_op jit(solution)/shard_map/ppermute | solution.py:52
  18.8 1.5 collective-permute-start.7
  24.7 1.9 fusion.35
  31.5 2.7 shard_map.136
  36.3 1.4 collective-permute-start.3
  37.8 1.4 collective-permute-start.4
  39.2 2.0 collective-permute-start.5
  41.2 4.7 %collective-permute-done.7.refs_4_.refs_5_ = bf16[4,192,768]{2,1,0:T(8,128)(2,1)} collective-permute-done((bf16[4,192,768]{2,1,0:T(8,128)(2,1)}, bf16[4,192,768]{2,1,0:T(8,128)(2,1)}, u32[]{:S(2)}, u32[]{:S(2)}) %collective-permute-start.7) | collective-permute-done | bytes 1179680 | tf_op jit(solution)/shard_map/ppermute | solution.py:47
  45.9 10.5 %shard_map.137 = (bf16[256,384]{1,0:T(8,128)(2,1)S(1)}, bf16[1024,384]{1,0:T(8,128)(2,1)S(1)}, bf16[1024,384]{1,0:T(8,128)(2,1)S(1)}, bf16[256,384]{1,0:T(8,128)...) custom-call(bf16[512,768]{1,0:T(8,128)(2,1)S(1)} %get-tuple-element.169.refs_0_.own_act., ...), custom_call_target="tpu_custom_call" | custom-call | flops 20000000000 | tf_op jit(solution)/shard_map/pallas_call | solution.py:475
  59.0 3.1 collective-permute-start.11
  63.2 1.5 collective-permute-start.16
  64.7 2.7 collective-permute-done.11.refs_3_
  67.4 13.1 %collective-permute-done.10.refs_2_ = bf16[128,768]{1,0:T(8,128)(2,1)S(1)} collective-permute-done((bf16[128,768]{1,0:T(8,128)(2,1)S(1)}, bf16[128,768]{1,0:T(8,128)(2,1)S(1)}, u32[]{:S(2)}, u32[]{:S(2)}) %collective-permute-start.10) | collective-permute-done | bytes 196640 | tf_op jit(solution)/shard_map/ppermute | solution.py:52
  80.5 3.6 %shard_map.139 = (f32[512,768]{1,0:T(8,128)S(1)}, bf16[512,768]{1,0:T(8,128)(2,1)S(1)}, bf16[512,768]{1,0:T(8,128)(2,1)S(1)}, bf16[4,128,768]{2,1,0:T(8,128)(2,1)}) custom-call(s32[5]{0:T(128)S(1)} %stack.80.place_ref.spot_ref, bf16[128,768]{1,0:T(8,128)(2,1)S(1)} %get-tuple-element.177.refs_0_, bf16[128,768]{1,0:T(8,128)(2,1)S(1)} %collective-permute-done.9.refs_1_, ...), custom_call_target="tpu_custom_call" | custom-call | flops 20000000000 | tf_op jit(solution)/shard_map/pallas_call | solution.py:475
  84.1 1.5 collective-permute-start.13
  85.6 2.0 collective-permute-start.12
  87.6 2.8 collective-permute-done.16.refs_6_.refs_7_
  90.4 16.3 %shard_map.141 = (bf16[256,384]{1,0:T(8,128)(2,1)S(1)}, bf16[1024,384]{1,0:T(8,128)(2,1)S(1)}, bf16[1024,384]{1,0:T(8,128)(2,1)S(1)}, bf16[256,384]{1,0:T(8,128)...) custom-call(bf16[512,768]{1,0:T(8,128)(2,1)S(1)} %get-tuple-element., ...), custom_call_target="tpu_custom_call" | custom-call | flops 20000000000 | tf_op jit(solution)/shard_map/pallas_call | solution.py:475
  109.9 3.6 %collective-permute-start.18 = (bf16[128,768]{1,0:T(8,128)(2,1)S(1)}, bf16[128,768]{1,0:T(8,128)(2,1)S(1)}, u32[]{:S(2)}, u32[]{:S(2)}) collective-permute-start(bf16[128,768]{1,0:T(8,128)(2,1)S(1)} %get-tuple-element.191), channel_id=1, source_target_pairs={{0,3},{1,0},{2,1},{3,2},{4,7},{5,4},{6,5},{7,6},{8,11},{9,8},{10,9... | collective-permute-start | bytes 589832 | tf_op jit(solution)/shard_map/ppermute | solution.py:52
  114.3 2.4 shard_map.143
  117.7 3.5 %shard_map.144 = (f32[2,4,96,768]{3,2,1,0:T(8,128)S(1)}, bf16[2,4,96,768]{3,2,1,0:T(8,128)(2,1)S(1)}) custom-call(s32[5]{0:T(128)S(1)} %stack.80.place_ref.spot_ref, bf16[512,768]{1,0:T(8,128)(2,1)S(1)} %get-tuple-element.178.refs_0_.x_ref.own_act, bf16[512,768]{1,0:T(8,128)(2,1)S(1)} %collective-permute-done.15.refs_1_.other_act, ...), custom_call_target="tpu_custom_call" | custom-call | flops 5000000000 | tf_op jit(solution)/shard_map/pallas_call | solution.py:475
  121.3 10.0 %collective-permute-done.20.refs_2_ = bf16[128,768]{1,0:T(8,128)(2,1)S(1)} collective-permute-done((bf16[128,768]{1,0:T(8,128)(2,1)S(1)}, bf16[128,768]{1,0:T(8,128)(2,1)S(1)}, u32[]{:S(2)}, u32[]{:S(2)}) %collective-permute-start.20) | collective-permute-done | bytes 196640 | tf_op jit(solution)/shard_map/ppermute | solution.py:52
  132.0 1.6 shard_map.145
  134.5 2.3 collective-permute-start.28
  136.9 1.9 collective-permute-start.22
  138.8 1.5 collective-permute-start.26
  140.3 1.5 copy-done.7
  142.7 11.5 %shard_map.146 = (bf16[256,384]{1,0:T(8,128)(2,1)S(1)}, bf16[1024,384]{1,0:T(8,128)(2,1)S(1)}, bf16[1024,384]{1,0:T(8,128)(2,1)S(1)}, f32[512,768]{1,0:T(8,128)S(1)}, bf16[512,768]{1,0:T(8,128)(2,1)S(1)}) custom-call(bf16[128,768]{1,0:T(8,128)(2,1)} %get-tuple-element.206.refs_0_.g_own, bf16[128,768]{1,0:T(8,128)(2,1)} %collective-permute-done.24.refs_1_.g_other, ...), custom_call_target="tpu_custom_call" | custom-call | flops 20000000000 | tf_op jit(solution)/shard_map/pallas_call | solution.py:475
  154.3 5.4 %shard_map.147 = (f32[2,4,96,768]{3,2,1,0:T(8,128)S(1)}, bf16[2,4,96,768]{3,2,1,0:T(8,128)(2,1)}) custom-call(s32[5]{0:T(128)S(1)} %copy-done.21, bf16[512,768]{1,0:T(8,128)(2,1)S(1)} %copy-done.28, bf16[512,768]{1,0:T(8,128)(2,1)S(1)} %copy-done.30, bf16[128,768]{1,0:T(8,128)(2,1)} %get-tuple-element.206.refs_0_.g_own, ...), custom_call_target="tpu_custom_call" | custom-call | flops 5000000000 | tf_op jit(solution)/shard_map/pallas_call | solution.py:475
  160.2 1.5 collective-permute-start.25
  161.9 1.6 collective-permute-start.27
  163.5 1.5 collective-permute-done.28.refs_2_
  164.9 1.9 shard_map.148
  167.7 4.1 %collective-permute-start.33 = (bf16[128,768]{1,0:T(8,128)(2,1)S(1)}, bf16[128,768]{1,0:T(8,128)(2,1)S(1)}, u32[]{:S(2)}, u32[]{:S(2)}) collective-permute-start(bf16[128,768]{1,0:T(8,128)(2,1)S(1)} %get-tuple-element.245), channel_id=1, source_target_pairs={{0,2},{1,3},{2,0},{3,1},{4,6},{5,7},{6,4},{7,5},{8,10},{9,11},{10,... | collective-permute-start | bytes 589832 | tf_op jit(solution)/shard_map/ppermute | solution.py:52
  171.8 2.4 shard_map.150
  175.6 1.9 collective-permute-start.34
  179.8 9.1 %collective-permute-done.33.refs_3_ = bf16[128,768]{1,0:T(8,128)(2,1)S(1)} collective-permute-done((bf16[128,768]{1,0:T(8,128)(2,1)S(1)}, bf16[128,768]{1,0:T(8,128)(2,1)S(1)}, u32[]{:S(2)}, u32[]{:S(2)}) %collective-permute-start.33) | collective-permute-done | bytes 196640 | tf_op jit(solution)/shard_map/ppermute | solution.py:52
  188.9 1.7 shard_map.151
  190.6 1.5 bitcast_add_fusion
  194.7 1.6 convert_add_fusion.1
  198.3 2.7 collective-permute-start.37
  201.0 3.5 %collective-permute-start.38 = (bf16[96,768]{1,0:T(8,128)(2,1)S(1)}, bf16[96,768]{1,0:T(8,128)(2,1)S(1)}, u32[]{:S(2)}, u32[]{:S(2)}) collective-permute-start(bf16[96,768]{1,0:T(8,128)(2,1)S(1)} %get-tuple-element.257), channel_id=1, source_target_pairs={{0,2},{1,3},{2,0},{3,1},{4,6},{5,7},{6,4},{7,5},{8,10},{9,11},{10,... | collective-permute-start | bytes 442376 | tf_op jit(solution)/shard_map/ppermute | solution.py:52
  204.5 2.0 collective-permute-start.39
  206.6 11.6 %collective-permute-done.38 = bf16[96,768]{1,0:T(8,128)(2,1)S(1)} collective-permute-done((bf16[96,768]{1,0:T(8,128)(2,1)S(1)}, bf16[96,768]{1,0:T(8,128)(2,1)S(1)}, u32[]{:S(2)}, u32[]{:S(2)}) %collective-permute-start.38) | collective-permute-done | bytes 147488 | tf_op jit(solution)/shard_map/ppermute | solution.py:52
  218.4 1.5 copy-done.3
  220.8 1.5 collective-permute-start.41
  223.9 1.9 collective-permute-start.44
  225.9 3.9 %collective-permute-done.42 = bf16[96,768]{1,0:T(8,128)(2,1)S(1)} collective-permute-done((bf16[96,768]{1,0:T(8,128)(2,1)S(1)}, bf16[96,768]{1,0:T(8,128)(2,1)S(1)}, u32[]{:S(2)}, u32[]{:S(2)}) %collective-permute-start.42) | collective-permute-done | bytes 147488 | tf_op jit(solution)/shard_map/ppermute | solution.py:52
  229.8 6.7 %collective-permute-done.43 = bf16[96,768]{1,0:T(8,128)(2,1)S(1)} collective-permute-done((bf16[96,768]{1,0:T(8,128)(2,1)S(1)}, bf16[96,768]{1,0:T(8,128)(2,1)S(1)}, u32[]{:S(2)}, u32[]{:S(2)}) %collective-permute-start.43) | collective-permute-done | bytes 147488 | tf_op jit(solution)/shard_map/ppermute | solution.py:52
  236.5 5.6 %collective-permute-done.41 = bf16[192,768]{1,0:T(8,128)(2,1)S(1)} collective-permute-done((bf16[192,768]{1,0:T(8,128)(2,1)S(1)}, bf16[192,768]{1,0:T(8,128)(2,1)S(1)}, u32[]{:S(2)}, u32[]{:S(2)}) %collective-permute-start.41) | collective-permute-done | bytes 294944 | tf_op jit(solution)/shard_map/ppermute | solution.py:47
  244.4 1.5 collective-permute-start.45
  247.2 3.4 %collective-permute-start.49 = (bf16[96,768]{1,0:T(8,128)(2,1)S(1)}, bf16[96,768]{1,0:T(8,128)(2,1)S(1)}, u32[]{:S(2)}, u32[]{:S(2)}) collective-permute-start(bf16[96,768]{1,0:T(8,128)(2,1)S(1)} %fusion.17), channel_id=1, source_target_pairs={{0,3},{1,0},{2,1},{3,2},{4,7},{5,4},{6,5},{7,6},{8,11},{9,8},{10,9... | collective-permute-start | bytes 442376 | tf_op jit(solution)/shard_map/ppermute | solution.py:52
  251.6 3.8 %collective-permute-done.47 = bf16[96,768]{1,0:T(8,128)(2,1)S(1)} collective-permute-done((bf16[96,768]{1,0:T(8,128)(2,1)S(1)}, bf16[96,768]{1,0:T(8,128)(2,1)S(1)}, u32[]{:S(2)}, u32[]{:S(2)}) %collective-permute-start.47) | collective-permute-done | bytes 147488 | tf_op jit(solution)/shard_map/ppermute | solution.py:52
  255.4 3.7 %collective-permute-done.48 = bf16[96,768]{1,0:T(8,128)(2,1)S(1)} collective-permute-done((bf16[96,768]{1,0:T(8,128)(2,1)S(1)}, bf16[96,768]{1,0:T(8,128)(2,1)S(1)}, u32[]{:S(2)}, u32[]{:S(2)}) %collective-permute-start.48) | collective-permute-done | bytes 147488 | tf_op jit(solution)/shard_map/ppermute | solution.py:52
  263.1 2.7 collective-permute-start.52
  268.3 4.0 %collective-permute-done.52 = bf16[112,768]{1,0:T(8,128)(2,1)S(1)} collective-permute-done((bf16[112,768]{1,0:T(8,128)(2,1)S(1)}, bf16[112,768]{1,0:T(8,128)(2,1)S(1)}, u32[]{:S(2)}, u32[]{:S(2)}) %collective-permute-start.52) | collective-permute-done | bytes 172064 | tf_op jit(solution)/shard_map/ppermute | solution.py:52
  272.2 4.5 %collective-permute-done.53 = bf16[112,768]{1,0:T(8,128)(2,1)S(1)} collective-permute-done((bf16[112,768]{1,0:T(8,128)(2,1)S(1)}, bf16[112,768]{1,0:T(8,128)(2,1)S(1)}, u32[]{:S(2)}, u32[]{:S(2)}) %collective-permute-start.53) | collective-permute-done | bytes 172064 | tf_op jit(solution)/shard_map/ppermute | solution.py:52
  278.1 1.6 collective-permute-start.55
  280.2 1.5 collective-permute-start.57
  281.7 3.9 %convert_add_fusion.3 = (f32[4,128,768]{2,1,0:T(8,128)}, f32[4,128,768]{2,1,0:T(8,128)}) fusion(bf16[4,128,768]{2,1,0:T(8,128)(2,1)} %bitcast.132, bf16[4,128,1536]{2,1,0:T(8,128)(2,1)} %bitcast.136, bf16[4,128,768]{2,1,0:T(8,128)(2,1)} %bitcast.135), kind=kLoop, calls=%fused_computation.4 | loop fusion | flops 2359296 | bytes 6291456 | tf_op jit(solution)/shard_map/add | solution.py:1155
  285.6 8.7 %collective-permute-done.55.refs_1_ = bf16[4,96,768]{2,1,0:T(8,128)(2,1)S(1)} collective-permute-done((bf16[4,96,768]{2,1,0:T(8,128)(2,1)S(1)}, bf16[4,96,768]{2,1,0:T(8,128)(2,1)S(1)}, u32[]{:S(2)}, u32[]{:S(2)}) %collective-permute-start.55) | collective-permute-done | bytes 589856 | tf_op jit(solution)/shard_map/ppermute | solution.py:204
  294.3 12.2 %collective-permute-done.56.refs_3_ = bf16[4,96,768]{2,1,0:T(8,128)(2,1)S(1)} collective-permute-done((bf16[4,96,768]{2,1,0:T(8,128)(2,1)S(1)}, bf16[4,96,768]{2,1,0:T(8,128)(2,1)S(1)}, u32[]{:S(2)}, u32[]{:S(2)}) %collective-permute-start.56) | collective-permute-done | bytes 589856 | tf_op jit(solution)/shard_map/ppermute | solution.py:204
  307.7 3.8 %shard_map.152 = (f32[2,3,192,768]{3,2,1,0:T(8,128)}, f32[2,192,768]{2,1,0:T(8,128)}) custom-call(s32[5]{0:T(128)S(1)} %copy-done.22, bf16[4,96,768]{2,1,0:T(8,128)(2,1)S(1)} %pad_maximum_fusion.6.refs_0_, bf16[4,96,768]{2,1,0:T(8,128)(2,1)S(1)} %collective-permute-done.55.refs_1_, bf16[4,96,768]{2,1,0:T(8,128)(2,1)S(1)} %pad_maximum_fusion.7.refs_2_, ...), custom_call_target="tpu_custom_call" | custom-call | flops 20000000000 | tf_op jit(solution)/shard_map/pallas_call | solution.py:475
  311.6 4.7 %shard_map.153 = (f32[2,768,768]{2,1,0:T(8,128)}, f32[2,768,768]{2,1,0:T(8,128)}) custom-call(s32[5]{0:T(128)S(1)} %copy-done.22, bf16[4,192,768]{2,1,0:T(8,128)(2,1)S(1)} %pad_maximum_fusion.3.refs_0_, bf16[4,192,768]{2,1,0:T(8,128)(2,1)S(1)} %collective-permute-done.60.refs_1_, bf16[4,192,768]{2,1,0:T(8,128)(2,1)S(1)} %bitcast.123, ...), custom_call_target="tpu_custom_call" | custom-call | flops 20000000000 | tf_op jit(solution)/shard_map/pallas_call | solution.py:475
  (275 shorter events, 55.1 us)
Async XLA Ops:
  7.2 183.4 %reduce-scatter.2.cloned.1.call-start = ((), (), s32[]{:S(2)}) async-start(), calls=%async_computation.1 | async-start | bytes 983040 | tf_op jit(solution)/shard_map/reduce_scatter | solution.py:1095
  9.0 108.8 %copy-start.19 = (s32[5]{0:T(128)}, s32[5]{0:T(128)S(1)}, u32[]{:S(2)}) copy-start(s32[5]{0:T(128)S(1)} %stack.80.place_ref.spot_ref) | copy-start | bytes 64
  9.7 20.4 %collective-permute-start.2 = (bf16[128,768]{1,0:T(8,128)(2,1)S(1)}, bf16[128,768]{1,0:T(8,128)(2,1)S(1)}, u32[]{:S(2)}, u32[]{:S(2)}) collective-permute-start(bf16[128,768]{1,0:T(8,128)(2,1)S(1)} %shard_map.135.refs_0_), channel_id=1, source_target_pairs={{0,3},{1,0},{2,1},{3,2},{4,7},{5,4},{6,5},{7,6},{8,11},{9,8},{10,9... | collective-permute-start | bytes 589832 | tf_op jit(solution)/shard_map/ppermute | solution.py:52
  14.8 16.7 %collective-permute-start.1 = (bf16[128,768]{1,0:T(8,128)(2,1)S(1)}, bf16[128,768]{1,0:T(8,128)(2,1)S(1)}, u32[]{:S(2)}, u32[]{:S(2)}) collective-permute-start(bf16[128,768]{1,0:T(8,128)(2,1)S(1)} %shard_map.135.refs_0_), channel_id=1, source_target_pairs={{0,2},{1,3},{2,0},{3,1},{4,6},{5,7},{6,4},{7,5},{8,10},{9,11},{10,... | collective-permute-start | bytes 589832 | tf_op jit(solution)/shard_map/ppermute | solution.py:52
  14.8 15.3 %collective-permute-start = (bf16[128,768]{1,0:T(8,128)(2,1)S(1)}, bf16[128,768]{1,0:T(8,128)(2,1)S(1)}, u32[]{:S(2)}, u32[]{:S(2)}) collective-permute-start(bf16[128,768]{1,0:T(8,128)(2,1)S(1)} %shard_map.135.refs_0_), channel_id=1, source_target_pairs={{0,1},{1,2},{2,3},{3,0},{4,5},{5,6},{6,7},{7,4},{8,9},{9,10},{10,1... | collective-permute-start | bytes 589832 | tf_op jit(solution)/shard_map/ppermute | solution.py:52
  18.8 27.2 %collective-permute-start.7 = (bf16[4,192,768]{2,1,0:T(8,128)(2,1)}, bf16[4,192,768]{2,1,0:T(8,128)(2,1)}, u32[]{:S(2)}, u32[]{:S(2)}) collective-permute-start(bf16[4,192,768]{2,1,0:T(8,128)(2,1)} %pad_maximum_fusion.1), channel_id=1, source_target_pairs={{0,8},{4,12},{8,0},{12,4},{1,9},{5,13},{9,1},{13,5},{2,10},{6,14},... | collective-permute-start | bytes 3538952 | tf_op jit(solution)/shard_map/ppermute | solution.py:47
  36.3 9.6 %collective-permute-start.6 = (bf16[512,768]{1,0:T(8,128)(2,1)S(1)}, bf16[512,768]{1,0:T(8,128)(2,1)S(1)}, u32[]{:S(2)}, u32[]{:S(2)}) collective-permute-start(bf16[512,768]{1,0:T(8,128)(2,1)S(1)} %get-tuple-element.169.refs_0_.own_act.x_ref), channel_id=1, source_target_pairs={{0,4},{4,0},{8,12},{12,8},{1,5},{5,1},{9,13},{13,9},{2,6},{6,2},{1... | collective-permute-start | bytes 2359304 | tf_op jit(solution)/shard_map/ppermute | solution.py:47
  36.3 20.3 %collective-permute-start.3 = (bf16[128,768]{1,0:T(8,128)(2,1)S(1)}, bf16[128,768]{1,0:T(8,128)(2,1)S(1)}, u32[]{:S(2)}, u32[]{:S(2)}) collective-permute-start(bf16[128,768]{1,0:T(8,128)(2,1)S(1)} %get-tuple-element.166), channel_id=1, source_target_pairs={{0,3},{1,0},{2,1},{3,2},{4,7},{5,4},{6,5},{7,6},{8,11},{9,8},{10,9... | collective-permute-start | bytes 589832 | tf_op jit(solution)/shard_map/ppermute | solution.py:52
  37.8 19.6 %collective-permute-start.4 = (bf16[128,768]{1,0:T(8,128)(2,1)S(1)}, bf16[128,768]{1,0:T(8,128)(2,1)S(1)}, u32[]{:S(2)}, u32[]{:S(2)}) collective-permute-start(bf16[128,768]{1,0:T(8,128)(2,1)S(1)} %get-tuple-element.167), channel_id=1, source_target_pairs={{0,2},{1,3},{2,0},{3,1},{4,6},{5,7},{6,4},{7,5},{8,10},{9,11},{10,... | collective-permute-start | bytes 589832 | tf_op jit(solution)/shard_map/ppermute | solution.py:52
  39.2 18.1 %collective-permute-start.5 = (bf16[128,768]{1,0:T(8,128)(2,1)S(1)}, bf16[128,768]{1,0:T(8,128)(2,1)S(1)}, u32[]{:S(2)}, u32[]{:S(2)}) collective-permute-start(bf16[128,768]{1,0:T(8,128)(2,1)S(1)} %get-tuple-element.168), channel_id=1, source_target_pairs={{0,1},{1,2},{2,3},{3,0},{4,5},{5,6},{6,7},{7,4},{8,9},{9,10},{10,1... | collective-permute-start | bytes 589832 | tf_op jit(solution)/shard_map/ppermute | solution.py:52
  56.5 1.5 collective-permute-start.8
  59.0 8.5 %collective-permute-start.11 = (bf16[128,768]{1,0:T(8,128)(2,1)S(1)}, bf16[128,768]{1,0:T(8,128)(2,1)S(1)}, u32[]{:S(2)}, u32[]{:S(2)}) collective-permute-start(bf16[128,768]{1,0:T(8,128)(2,1)S(1)} %get-tuple-element.177.refs_0_), channel_id=1, source_target_pairs={{0,3},{1,0},{2,1},{3,2},{4,7},{5,4},{6,5},{7,6},{8,11},{9,8},{10,9... | collective-permute-start | bytes 589832 | tf_op jit(solution)/shard_map/ppermute | solution.py:52
  62.1 18.4 %collective-permute-start.10 = (bf16[128,768]{1,0:T(8,128)(2,1)S(1)}, bf16[128,768]{1,0:T(8,128)(2,1)S(1)}, u32[]{:S(2)}, u32[]{:S(2)}) collective-permute-start(bf16[128,768]{1,0:T(8,128)(2,1)S(1)} %get-tuple-element.177.refs_0_), channel_id=1, source_target_pairs={{0,2},{1,3},{2,0},{3,1},{4,6},{5,7},{6,4},{7,5},{8,10},{9,11},{10,... | collective-permute-start | bytes 589832 | tf_op jit(solution)/shard_map/ppermute | solution.py:52
  62.9 17.6 %collective-permute-start.9 = (bf16[128,768]{1,0:T(8,128)(2,1)S(1)}, bf16[128,768]{1,0:T(8,128)(2,1)S(1)}, u32[]{:S(2)}, u32[]{:S(2)}) collective-permute-start(bf16[128,768]{1,0:T(8,128)(2,1)S(1)} %get-tuple-element.177.refs_0_), channel_id=1, source_target_pairs={{0,1},{1,2},{2,3},{3,0},{4,5},{5,6},{6,7},{7,4},{8,9},{9,10},{10,1... | collective-permute-start | bytes 589832 | tf_op jit(solution)/shard_map/ppermute | solution.py:52
  63.2 27.2 %collective-permute-start.16 = (bf16[4,192,768]{2,1,0:T(8,128)(2,1)S(1)}, bf16[4,192,768]{2,1,0:T(8,128)(2,1)S(1)}, u32[]{:S(2)}, u32[]{:S(2)}) collective-permute-start(bf16[4,192,768]{2,1,0:T(8,128)(2,1)S(1)} %pad_maximum_fusion), channel_id=1, source_target_pairs={{0,8},{4,12},{8,0},{12,4},{1,9},{5,13},{9,1},{13,5},{2,10},{6,14},... | collective-permute-start | bytes 3538952 | tf_op jit(solution)/shard_map/ppermute | solution.py:47
  84.1 6.3 %collective-permute-start.15 = (bf16[512,768]{1,0:T(8,128)(2,1)S(1)}, bf16[512,768]{1,0:T(8,128)(2,1)S(1)}, u32[]{:S(2)}, u32[]{:S(2)}) collective-permute-start(bf16[512,768]{1,0:T(8,128)(2,1)S(1)} %get-tuple-element.178.refs_0_.x_ref.own_act), channel_id=1, source_target_pairs={{0,4},{4,0},{8,12},{12,8},{1,5},{5,1},{9,13},{13,9},{2,6},{6,2},{1... | collective-permute-start | bytes 2359304 | tf_op jit(solution)/shard_map/ppermute | solution.py:47
  84.1 22.8 %collective-permute-start.14 = (bf16[128,768]{1,0:T(8,128)(2,1)S(1)}, bf16[128,768]{1,0:T(8,128)(2,1)S(1)}, u32[]{:S(2)}, u32[]{:S(2)}) collective-permute-start(bf16[128,768]{1,0:T(8,128)(2,1)S(1)} %get-tuple-element.179.refs_0_.refs_2_.g_own.cot_ref), channel_id=1, source_target_pairs={{0,3},{1,0},{2,1},{3,2},{4,7},{5,4},{6,5},{7,6},{8,11},{9,8},{10,9... | collective-permute-start | bytes 589832 | tf_op jit(solution)/shard_map/ppermute | solution.py:52
  84.1 22.8 %collective-permute-start.13 = (bf16[128,768]{1,0:T(8,128)(2,1)S(1)}, bf16[128,768]{1,0:T(8,128)(2,1)S(1)}, u32[]{:S(2)}, u32[]{:S(2)}) collective-permute-start(bf16[128,768]{1,0:T(8,128)(2,1)S(1)} %get-tuple-element.179.refs_0_.refs_2_.g_own.cot_ref), channel_id=1, source_target_pairs={{0,2},{1,3},{2,0},{3,1},{4,6},{5,7},{6,4},{7,5},{8,10},{9,11},{10,... | collective-permute-start | bytes 589832 | tf_op jit(solution)/shard_map/ppermute | solution.py:52
  85.6 21.3 %collective-permute-start.12 = (bf16[128,768]{1,0:T(8,128)(2,1)S(1)}, bf16[128,768]{1,0:T(8,128)(2,1)S(1)}, u32[]{:S(2)}, u32[]{:S(2)}) collective-permute-start(bf16[128,768]{1,0:T(8,128)(2,1)S(1)} %get-tuple-element.179.refs_0_.refs_2_.g_own.cot_ref), channel_id=1, source_target_pairs={{0,1},{1,2},{2,3},{3,0},{4,5},{5,6},{6,7},{7,4},{8,9},{9,10},{10,1... | collective-permute-start | bytes 589832 | tf_op jit(solution)/shard_map/ppermute | solution.py:52
  106.8 2.4 collective-permute-start.17
  109.9 11.4 %collective-permute-start.18 = (bf16[128,768]{1,0:T(8,128)(2,1)S(1)}, bf16[128,768]{1,0:T(8,128)(2,1)S(1)}, u32[]{:S(2)}, u32[]{:S(2)}) collective-permute-start(bf16[128,768]{1,0:T(8,128)(2,1)S(1)} %get-tuple-element.191), channel_id=1, source_target_pairs={{0,3},{1,0},{2,1},{3,2},{4,7},{5,4},{6,5},{7,6},{8,11},{9,8},{10,9... | collective-permute-start | bytes 589832 | tf_op jit(solution)/shard_map/ppermute | solution.py:52
  113.5 7.8 %collective-permute-start.19 = (bf16[128,768]{1,0:T(8,128)(2,1)S(1)}, bf16[128,768]{1,0:T(8,128)(2,1)S(1)}, u32[]{:S(2)}, u32[]{:S(2)}) collective-permute-start(bf16[128,768]{1,0:T(8,128)(2,1)S(1)} %get-tuple-element.192), channel_id=1, source_target_pairs={{0,4},{4,0},{8,12},{12,8},{1,5},{5,1},{9,13},{13,9},{2,6},{6,2},{1... | collective-permute-start | bytes 589832 | tf_op jit(solution)/shard_map/ppermute | solution.py:47
  113.5 17.8 %collective-permute-start.20 = (bf16[128,768]{1,0:T(8,128)(2,1)S(1)}, bf16[128,768]{1,0:T(8,128)(2,1)S(1)}, u32[]{:S(2)}, u32[]{:S(2)}) collective-permute-start(bf16[128,768]{1,0:T(8,128)(2,1)S(1)} %get-tuple-element.204), channel_id=1, source_target_pairs={{0,2},{1,3},{2,0},{3,1},{4,6},{5,7},{6,4},{7,5},{8,10},{9,11},{10,... | collective-permute-start | bytes 589832 | tf_op jit(solution)/shard_map/ppermute | solution.py:52
  113.8 17.6 %collective-permute-start.21 = (bf16[128,768]{1,0:T(8,128)(2,1)S(1)}, bf16[128,768]{1,0:T(8,128)(2,1)S(1)}, u32[]{:S(2)}, u32[]{:S(2)}) collective-permute-start(bf16[128,768]{1,0:T(8,128)(2,1)S(1)} %get-tuple-element.205), channel_id=1, source_target_pairs={{0,1},{1,2},{2,3},{3,0},{4,5},{5,6},{6,7},{7,4},{8,9},{9,10},{10,1... | collective-permute-start | bytes 589832 | tf_op jit(solution)/shard_map/ppermute | solution.py:52
  134.4 4.4 %collective-permute-start.24 = (bf16[128,768]{1,0:T(8,128)(2,1)}, bf16[128,768]{1,0:T(8,128)(2,1)}, u32[]{:S(2)}, u32[]{:S(2)}) collective-permute-start(bf16[128,768]{1,0:T(8,128)(2,1)} %get-tuple-element.206.refs_0_.g_own), channel_id=1, source_target_pairs={{0,4},{4,0},{8,12},{12,8},{1,5},{5,1},{9,13},{13,9},{2,6},{6,2},{1... | collective-permute-start | bytes 589832 | tf_op jit(solution)/shard_map/ppermute | solution.py:47
  134.4 143.5 %all-gather.3.cloned.1.call-start = ((), (), s32[]{:S(2)}) async-start(), calls=%async_computation.2 | async-start | bytes 1966080 | tf_op jit(solution)/shard_map/all_gather | solution.py:1099
  134.5 27.4 %collective-permute-start.29 = (bf16[128,768]{1,0:T(8,128)(2,1)}, bf16[128,768]{1,0:T(8,128)(2,1)S(1)}, u32[]{:S(2)}, u32[]{:S(2)}) collective-permute-start(bf16[128,768]{1,0:T(8,128)(2,1)} %get-tuple-element.206.refs_0_.g_own), channel_id=1, source_target_pairs={{0,3},{1,0},{2,1},{3,2},{4,7},{5,4},{6,5},{7,6},{8,11},{9,8},{10,9... | collective-permute-start | bytes 589832 | tf_op jit(solution)/shard_map/ppermute | solution.py:52
  134.5 30.4 %collective-permute-start.28 = (bf16[128,768]{1,0:T(8,128)(2,1)}, bf16[128,768]{1,0:T(8,128)(2,1)S(1)}, u32[]{:S(2)}, u32[]{:S(2)}) collective-permute-start(bf16[128,768]{1,0:T(8,128)(2,1)} %get-tuple-element.206.refs_0_.g_own), channel_id=1, source_target_pairs={{0,2},{1,3},{2,0},{3,1},{4,6},{5,7},{6,4},{7,5},{8,10},{9,11},{10,... | collective-permute-start | bytes 589832 | tf_op jit(solution)/shard_map/ppermute | solution.py:52
  136.9 23.4 %collective-permute-start.22 = (bf16[128,768]{1,0:T(8,128)(2,1)}, bf16[128,768]{1,0:T(8,128)(2,1)S(1)}, u32[]{:S(2)}, u32[]{:S(2)}) collective-permute-start(bf16[128,768]{1,0:T(8,128)(2,1)} %get-tuple-element.206.refs_0_.g_own), channel_id=1, source_target_pairs={{0,1},{1,2},{2,3},{3,0},{4,5},{5,6},{6,7},{7,4},{8,9},{9,10},{10,1... | collective-permute-start | bytes 589832 | tf_op jit(solution)/shard_map/ppermute | solution.py:52
  138.8 20.9 %collective-permute-start.23 = (bf16[2,2,192,768]{3,2,1,0:T(8,128)(2,1)}, bf16[2,2,192,768]{3,2,1,0:T(8,128)(2,1)S(1)}, u32[]{:S(2)}, u32[]{:S(2)}) collective-permute-start(bf16[2,2,192,768]{3,2,1,0:T(8,128)(2,1)} %copy-done.26), channel_id=1, source_target_pairs={{0,4},{4,0},{8,12},{12,8},{1,5},{5,1},{9,13},{13,9},{2,6},{6,2},{1... | collective-permute-start | bytes 3538952 | tf_op jit(solution)/shard_map/ppermute | solution.py:47
  138.8 36.8 %collective-permute-start.26 = (bf16[2,4,96,768]{3,2,1,0:T(8,128)(2,1)}, bf16[2,4,96,768]{3,2,1,0:T(8,128)(2,1)S(1)}, u32[]{:S(2)}, u32[]{:S(2)}) collective-permute-start(bf16[2,4,96,768]{3,2,1,0:T(8,128)(2,1)} %copy-done.23), channel_id=1, source_target_pairs={{0,8},{4,12},{8,0},{12,4},{1,9},{5,13},{9,1},{13,5},{2,10},{6,14},... | collective-permute-start | bytes 3538952 | tf_op jit(solution)/shard_map/ppermute | solution.py:47
  159.7 7.1 %collective-permute-start.30 = (bf16[512,768]{1,0:T(8,128)(2,1)S(1)}, bf16[512,768]{1,0:T(8,128)(2,1)S(1)}, u32[]{:S(2)}, u32[]{:S(2)}) collective-permute-start(bf16[512,768]{1,0:T(8,128)(2,1)S(1)} %get-tuple-element.230), channel_id=1, source_target_pairs={{0,4},{4,0},{8,12},{12,8},{1,5},{5,1},{9,13},{13,9},{2,6},{6,2},{1... | collective-permute-start | bytes 2359304 | tf_op jit(solution)/shard_map/ppermute | solution.py:47
  160.2 34.5 %collective-permute-start.25 = (bf16[2,4,96,768]{3,2,1,0:T(8,128)(2,1)}, bf16[2,4,96,768]{3,2,1,0:T(8,128)(2,1)}, u32[]{:S(2)}, u32[]{:S(2)}) collective-permute-start(bf16[2,4,96,768]{3,2,1,0:T(8,128)(2,1)} %get-tuple-element.219), channel_id=1, source_target_pairs={{0,8},{4,12},{8,0},{12,4},{1,9},{5,13},{9,1},{13,5},{2,10},{6,14},... | collective-permute-start | bytes 3538952 | tf_op jit(solution)/shard_map/ppermute | solution.py:47
  161.9 15.7 %collective-permute-start.27 = (bf16[2,192,768]{2,1,0:T(8,128)(2,1)S(1)}, bf16[2,192,768]{2,1,0:T(8,128)(2,1)S(1)}, u32[]{:S(2)}, u32[]{:S(2)}) collective-permute-start(bf16[2,192,768]{2,1,0:T(8,128)(2,1)S(1)} %fusion.3), channel_id=1, source_target_pairs={{0,16},{16,0},{1,17},{17,1},{2,18},{18,2},{3,19},{19,3},{4,20},{20... | collective-permute-start | bytes 1769480 | tf_op jit(solution)/shard_map/ppermute | solution.py:204
  167.6 9.9 %collective-permute-start.32 = (bf16[128,768]{1,0:T(8,128)(2,1)S(1)}, bf16[128,768]{1,0:T(8,128)(2,1)S(1)}, u32[]{:S(2)}, u32[]{:S(2)}) collective-permute-start(bf16[128,768]{1,0:T(8,128)(2,1)S(1)} %get-tuple-element.241), channel_id=1, source_target_pairs={{0,3},{1,0},{2,1},{3,2},{4,7},{5,4},{6,5},{7,6},{8,11},{9,8},{10,9... | collective-permute-start | bytes 589832 | tf_op jit(solution)/shard_map/ppermute | solution.py:52
  167.7 21.2 %collective-permute-start.33 = (bf16[128,768]{1,0:T(8,128)(2,1)S(1)}, bf16[128,768]{1,0:T(8,128)(2,1)S(1)}, u32[]{:S(2)}, u32[]{:S(2)}) collective-permute-start(bf16[128,768]{1,0:T(8,128)(2,1)S(1)} %get-tuple-element.245), channel_id=1, source_target_pairs={{0,2},{1,3},{2,0},{3,1},{4,6},{5,7},{6,4},{7,5},{8,10},{9,11},{10,... | collective-permute-start | bytes 589832 | tf_op jit(solution)/shard_map/ppermute | solution.py:52
  175.6 13.3 %collective-permute-start.34 = (bf16[128,768]{1,0:T(8,128)(2,1)S(1)}, bf16[128,768]{1,0:T(8,128)(2,1)S(1)}, u32[]{:S(2)}, u32[]{:S(2)}) collective-permute-start(bf16[128,768]{1,0:T(8,128)(2,1)S(1)} %get-tuple-element.246), channel_id=1, source_target_pairs={{0,1},{1,2},{2,3},{3,0},{4,5},{5,6},{6,7},{7,4},{8,9},{9,10},{10,1... | collective-permute-start | bytes 589832 | tf_op jit(solution)/shard_map/ppermute | solution.py:52
  179.3 14.2 %collective-permute-start.31 = (bf16[4,96,768]{2,1,0:T(8,128)(2,1)}, bf16[4,96,768]{2,1,0:T(8,128)(2,1)}, u32[]{:S(2)}, u32[]{:S(2)}) collective-permute-start(bf16[4,96,768]{2,1,0:T(8,128)(2,1)} %fusion.4), channel_id=1, source_target_pairs={{0,16},{16,0},{1,17},{17,1},{2,18},{18,2},{3,19},{19,3},{4,20},{20... | collective-permute-start | bytes 1769480 | tf_op jit(solution)/shard_map/ppermute | solution.py:204
  197.6 20.6 %collective-permute-start.36 = (bf16[2,2,192,768]{3,2,1,0:T(8,128)(2,1)S(1)}, bf16[2,2,192,768]{3,2,1,0:T(8,128)(2,1)S(1)}, u32[]{:S(2)}, u32[]{:S(2)}) collective-permute-start(bf16[2,2,192,768]{3,2,1,0:T(8,128)(2,1)S(1)} %copy-done.25), channel_id=1, source_target_pairs={{0,4},{4,0},{8,12},{12,8},{1,5},{5,1},{9,13},{13,9},{2,6},{6,2},{1... | collective-permute-start | bytes 3538952 | tf_op jit(solution)/shard_map/ppermute | solution.py:47
  197.7 20.5 %collective-permute-start.35 = (bf16[4,96,768]{2,1,0:T(8,128)(2,1)S(1)}, bf16[4,96,768]{2,1,0:T(8,128)(2,1)S(1)}, u32[]{:S(2)}, u32[]{:S(2)}) collective-permute-start(bf16[4,96,768]{2,1,0:T(8,128)(2,1)S(1)} %fusion.5), channel_id=1, source_target_pairs={{0,16},{16,0},{1,17},{17,1},{2,18},{18,2},{3,19},{19,3},{4,20},{20... | collective-permute-start | bytes 1769480 | tf_op jit(solution)/shard_map/ppermute | solution.py:204
  198.3 8.2 %collective-permute-start.37 = (bf16[96,768]{1,0:T(8,128)(2,1)S(1)}, bf16[96,768]{1,0:T(8,128)(2,1)S(1)}, u32[]{:S(2)}, u32[]{:S(2)}) collective-permute-start(bf16[96,768]{1,0:T(8,128)(2,1)S(1)} %get-tuple-element.256), channel_id=1, source_target_pairs={{0,3},{1,0},{2,1},{3,2},{4,7},{5,4},{6,5},{7,6},{8,11},{9,8},{10,9... | collective-permute-start | bytes 442376 | tf_op jit(solution)/shard_map/ppermute | solution.py:52
  201.0 17.1 %collective-permute-start.38 = (bf16[96,768]{1,0:T(8,128)(2,1)S(1)}, bf16[96,768]{1,0:T(8,128)(2,1)S(1)}, u32[]{:S(2)}, u32[]{:S(2)}) collective-permute-start(bf16[96,768]{1,0:T(8,128)(2,1)S(1)} %get-tuple-element.257), channel_id=1, source_target_pairs={{0,2},{1,3},{2,0},{3,1},{4,6},{5,7},{6,4},{7,5},{8,10},{9,11},{10,... | collective-permute-start | bytes 442376 | tf_op jit(solution)/shard_map/ppermute | solution.py:52
  204.5 13.6 %collective-permute-start.39 = (bf16[96,768]{1,0:T(8,128)(2,1)S(1)}, bf16[96,768]{1,0:T(8,128)(2,1)S(1)}, u32[]{:S(2)}, u32[]{:S(2)}) collective-permute-start(bf16[96,768]{1,0:T(8,128)(2,1)S(1)} %get-tuple-element.258), channel_id=1, source_target_pairs={{0,1},{1,2},{2,3},{3,0},{4,5},{5,6},{6,7},{7,4},{8,9},{9,10},{10,1... | collective-permute-start | bytes 442376 | tf_op jit(solution)/shard_map/ppermute | solution.py:52
  220.3 21.9 %collective-permute-start.40 = (bf16[400,768]{1,0:T(8,128)(2,1)S(1)}, bf16[400,768]{1,0:T(8,128)(2,1)S(1)}, u32[]{:S(2)}, u32[]{:S(2)}) collective-permute-start(bf16[400,768]{1,0:T(8,128)(2,1)S(1)} %pad_maximum_fusion.4), channel_id=1, source_target_pairs={{0,8},{4,12},{8,0},{12,4},{1,9},{5,13},{9,1},{13,5},{2,10},{6,14},... | collective-permute-start | bytes 1843208 | tf_op jit(solution)/shard_map/ppermute | solution.py:47
  220.8 21.3 %collective-permute-start.41 = (bf16[192,768]{1,0:T(8,128)(2,1)S(1)}, bf16[192,768]{1,0:T(8,128)(2,1)S(1)}, u32[]{:S(2)}, u32[]{:S(2)}) collective-permute-start(bf16[192,768]{1,0:T(8,128)(2,1)S(1)} %fusion.9), channel_id=1, source_target_pairs={{0,8},{4,12},{8,0},{12,4},{1,9},{5,13},{9,1},{13,5},{2,10},{6,14},... | collective-permute-start | bytes 884744 | tf_op jit(solution)/shard_map/ppermute | solution.py:47
  223.4 6.4 %collective-permute-start.42 = (bf16[96,768]{1,0:T(8,128)(2,1)S(1)}, bf16[96,768]{1,0:T(8,128)(2,1)S(1)}, u32[]{:S(2)}, u32[]{:S(2)}) collective-permute-start(bf16[96,768]{1,0:T(8,128)(2,1)S(1)} %get-tuple-element.267), channel_id=1, source_target_pairs={{0,3},{1,0},{2,1},{3,2},{4,7},{5,4},{6,5},{7,6},{8,11},{9,8},{10,9... | collective-permute-start | bytes 442376 | tf_op jit(solution)/shard_map/ppermute | solution.py:52
  223.5 13.0 %collective-permute-start.43 = (bf16[96,768]{1,0:T(8,128)(2,1)S(1)}, bf16[96,768]{1,0:T(8,128)(2,1)S(1)}, u32[]{:S(2)}, u32[]{:S(2)}) collective-permute-start(bf16[96,768]{1,0:T(8,128)(2,1)S(1)} %get-tuple-element.268), channel_id=1, source_target_pairs={{0,2},{1,3},{2,0},{3,1},{4,6},{5,7},{6,4},{7,5},{8,10},{9,11},{10,... | collective-permute-start | bytes 442376 | tf_op jit(solution)/shard_map/ppermute | solution.py:52
  223.9 12.6 %collective-permute-start.44 = (bf16[96,768]{1,0:T(8,128)(2,1)S(1)}, bf16[96,768]{1,0:T(8,128)(2,1)S(1)}, u32[]{:S(2)}, u32[]{:S(2)}) collective-permute-start(bf16[96,768]{1,0:T(8,128)(2,1)S(1)} %get-tuple-element.269), channel_id=1, source_target_pairs={{0,1},{1,2},{2,3},{3,0},{4,5},{5,6},{6,7},{7,4},{8,9},{9,10},{10,1... | collective-permute-start | bytes 442376 | tf_op jit(solution)/shard_map/ppermute | solution.py:52
  243.8 15.2 %collective-permute-start.46 = (bf16[192,768]{1,0:T(8,128)(2,1)S(1)}, bf16[192,768]{1,0:T(8,128)(2,1)}, u32[]{:S(2)}, u32[]{:S(2)}) collective-permute-start(bf16[192,768]{1,0:T(8,128)(2,1)S(1)} %fusion.8), channel_id=1, source_target_pairs={{0,16},{16,0},{1,17},{17,1},{2,18},{18,2},{3,19},{19,3},{4,20},{20... | collective-permute-start | bytes 884744 | tf_op jit(solution)/shard_map/ppermute | solution.py:204
  244.4 14.7 %collective-permute-start.45 = (bf16[208,768]{1,0:T(8,128)(2,1)}, bf16[208,768]{1,0:T(8,128)(2,1)}, u32[]{:S(2)}, u32[]{:S(2)}) collective-permute-start(bf16[208,768]{1,0:T(8,128)(2,1)} %pad_maximum_fusion.10), channel_id=1, source_target_pairs={{0,16},{16,0},{1,17},{17,1},{2,18},{18,2},{3,19},{19,3},{4,20},{20... | collective-permute-start | bytes 958472 | tf_op jit(solution)/shard_map/ppermute | solution.py:204
  246.7 8.7 %collective-permute-start.47 = (bf16[96,768]{1,0:T(8,128)(2,1)S(1)}, bf16[96,768]{1,0:T(8,128)(2,1)S(1)}, u32[]{:S(2)}, u32[]{:S(2)}) collective-permute-start(bf16[96,768]{1,0:T(8,128)(2,1)S(1)} %fusion.17), channel_id=1, source_target_pairs={{0,1},{1,2},{2,3},{3,0},{4,5},{5,6},{6,7},{7,4},{8,9},{9,10},{10,1... | collective-permute-start | bytes 442376 | tf_op jit(solution)/shard_map/ppermute | solution.py:52
  246.7 12.3 %collective-permute-start.48 = (bf16[96,768]{1,0:T(8,128)(2,1)S(1)}, bf16[96,768]{1,0:T(8,128)(2,1)S(1)}, u32[]{:S(2)}, u32[]{:S(2)}) collective-permute-start(bf16[96,768]{1,0:T(8,128)(2,1)S(1)} %fusion.17), channel_id=1, source_target_pairs={{0,2},{1,3},{2,0},{3,1},{4,6},{5,7},{6,4},{7,5},{8,10},{9,11},{10,... | collective-permute-start | bytes 442376 | tf_op jit(solution)/shard_map/ppermute | solution.py:52
  247.2 11.9 %collective-permute-start.49 = (bf16[96,768]{1,0:T(8,128)(2,1)S(1)}, bf16[96,768]{1,0:T(8,128)(2,1)S(1)}, u32[]{:S(2)}, u32[]{:S(2)}) collective-permute-start(bf16[96,768]{1,0:T(8,128)(2,1)S(1)} %fusion.17), channel_id=1, source_target_pairs={{0,3},{1,0},{2,1},{3,2},{4,7},{5,4},{6,5},{7,6},{8,11},{9,8},{10,9... | collective-permute-start | bytes 442376 | tf_op jit(solution)/shard_map/ppermute | solution.py:52
  262.0 14.8 %collective-permute-start.51 = (bf16[2,192,768]{2,1,0:T(8,128)(2,1)S(1)}, bf16[2,192,768]{2,1,0:T(8,128)(2,1)S(1)}, u32[]{:S(2)}, u32[]{:S(2)}) collective-permute-start(bf16[2,192,768]{2,1,0:T(8,128)(2,1)S(1)} %get-tuple-element.286), channel_id=1, source_target_pairs={{0,8},{4,12},{8,0},{12,4},{1,9},{5,13},{9,1},{13,5},{2,10},{6,14},... | collective-permute-start | bytes 1769480 | tf_op jit(solution)/shard_map/ppermute | solution.py:47
  262.6 14.2 %collective-permute-start.50 = (bf16[192,768]{1,0:T(8,128)(2,1)S(1)}, bf16[192,768]{1,0:T(8,128)(2,1)S(1)}, u32[]{:S(2)}, u32[]{:S(2)}) collective-permute-start(bf16[192,768]{1,0:T(8,128)(2,1)S(1)} %fusion.7), channel_id=1, source_target_pairs={{0,16},{16,0},{1,17},{17,1},{2,18},{18,2},{3,19},{19,3},{4,20},{20... | collective-permute-start | bytes 884744 | tf_op jit(solution)/shard_map/ppermute | solution.py:204
  263.1 9.1 %collective-permute-start.52 = (bf16[112,768]{1,0:T(8,128)(2,1)S(1)}, bf16[112,768]{1,0:T(8,128)(2,1)S(1)}, u32[]{:S(2)}, u32[]{:S(2)}) collective-permute-start(bf16[112,768]{1,0:T(8,128)(2,1)S(1)} %pad_maximum_fusion.11), channel_id=1, source_target_pairs={{0,1},{1,2},{2,3},{3,0},{4,5},{5,6},{6,7},{7,4},{8,9},{9,10},{10,1... | collective-permute-start | bytes 516104 | tf_op jit(solution)/shard_map/ppermute | solution.py:52
  265.8 10.9 %collective-permute-start.53 = (bf16[112,768]{1,0:T(8,128)(2,1)S(1)}, bf16[112,768]{1,0:T(8,128)(2,1)S(1)}, u32[]{:S(2)}, u32[]{:S(2)}) collective-permute-start(bf16[112,768]{1,0:T(8,128)(2,1)S(1)} %pad_maximum_fusion.11), channel_id=1, source_target_pairs={{0,2},{1,3},{2,0},{3,1},{4,6},{5,7},{6,4},{7,5},{8,10},{9,11},{10,... | collective-permute-start | bytes 516104 | tf_op jit(solution)/shard_map/ppermute | solution.py:52
  267.0 9.7 %collective-permute-start.54 = (bf16[112,768]{1,0:T(8,128)(2,1)S(1)}, bf16[112,768]{1,0:T(8,128)(2,1)S(1)}, u32[]{:S(2)}, u32[]{:S(2)}) collective-permute-start(bf16[112,768]{1,0:T(8,128)(2,1)S(1)} %pad_maximum_fusion.11), channel_id=1, source_target_pairs={{0,3},{1,0},{2,1},{3,2},{4,7},{5,4},{6,5},{7,6},{8,11},{9,8},{10,9... | collective-permute-start | bytes 516104 | tf_op jit(solution)/shard_map/ppermute | solution.py:52
  278.0 28.5 %collective-permute-start.59 = (bf16[4,192,768]{2,1,0:T(8,128)(2,1)S(1)}, bf16[4,192,768]{2,1,0:T(8,128)(2,1)S(1)}, u32[]{:S(2)}, u32[]{:S(2)}) collective-permute-start(bf16[4,192,768]{2,1,0:T(8,128)(2,1)S(1)} %bitcast.122), channel_id=1, source_target_pairs={{0,4},{4,0},{8,12},{12,8},{1,5},{5,1},{9,13},{13,9},{2,6},{6,2},{1... | collective-permute-start | bytes 3538952 | tf_op jit(solution)/shard_map/ppermute | solution.py:47
  278.1 16.2 %collective-permute-start.55 = (bf16[4,96,768]{2,1,0:T(8,128)(2,1)S(1)}, bf16[4,96,768]{2,1,0:T(8,128)(2,1)S(1)}, u32[]{:S(2)}, u32[]{:S(2)}) collective-permute-start(bf16[4,96,768]{2,1,0:T(8,128)(2,1)S(1)} %pad_maximum_fusion.6.refs_0_), channel_id=1, source_target_pairs={{0,16},{16,0},{1,17},{17,1},{2,18},{18,2},{3,19},{19,3},{4,20},{20... | collective-permute-start | bytes 1769480 | tf_op jit(solution)/shard_map/ppermute | solution.py:204
  279.7 26.8 %collective-permute-start.56 = (bf16[4,96,768]{2,1,0:T(8,128)(2,1)S(1)}, bf16[4,96,768]{2,1,0:T(8,128)(2,1)S(1)}, u32[]{:S(2)}, u32[]{:S(2)}) collective-permute-start(bf16[4,96,768]{2,1,0:T(8,128)(2,1)S(1)} %pad_maximum_fusion.7.refs_2_), channel_id=1, source_target_pairs={{0,16},{16,0},{1,17},{17,1},{2,18},{18,2},{3,19},{19,3},{4,20},{20... | collective-permute-start | bytes 1769480 | tf_op jit(solution)/shard_map/ppermute | solution.py:204
  280.2 26.3 %collective-permute-start.57 = (bf16[2,192,768]{2,1,0:T(8,128)(2,1)S(1)}, bf16[2,192,768]{2,1,0:T(8,128)(2,1)S(1)}, u32[]{:S(2)}, u32[]{:S(2)}) collective-permute-start(bf16[2,192,768]{2,1,0:T(8,128)(2,1)S(1)} %pad_maximum_fusion.8), channel_id=1, source_target_pairs={{0,8},{4,12},{8,0},{12,4},{1,9},{5,13},{9,1},{13,5},{2,10},{6,14},... | collective-permute-start | bytes 1769480 | tf_op jit(solution)/shard_map/ppermute | solution.py:47
  281.7 3.9 %collective-permute-start.58 = (f32[8,768]{1,0:T(8,128)S(1)}, f32[8,768]{1,0:T(8,128)S(1)}, u32[]{:S(2)}, u32[]{:S(2)}) collective-permute-start(f32[8,768]{1,0:T(8,128)S(1)} %add_add_fusion), channel_id=1, source_target_pairs={{0,4},{4,0},{8,12},{12,8},{1,5},{5,1},{9,13},{13,9},{2,6},{6,2},{1... | collective-permute-start | bytes 73736 | tf_op jit(solution)/shard_map/ppermute | solution.py:47
  307.2 4.4 %collective-permute-start.60 = (bf16[4,192,768]{2,1,0:T(8,128)(2,1)S(1)}, bf16[4,192,768]{2,1,0:T(8,128)(2,1)S(1)}, u32[]{:S(2)}, u32[]{:S(2)}) collective-permute-start(bf16[4,192,768]{2,1,0:T(8,128)(2,1)S(1)} %pad_maximum_fusion.3.refs_0_), channel_id=1, source_target_pairs={{0,4},{4,0},{8,12},{12,8},{1,5},{5,1},{9,13},{13,9},{2,6},{6,2},{1... | collective-permute-start | bytes 3538952 | tf_op jit(solution)/shard_map/ppermute | solution.py:47
  (60 other events, 377.9 us)
Sparse Core Ops, SparseCore 0:
  134.5 34.5 reduce-scatter.1
  246.8 16.7 all-gather.2
where the time goes:
time: 325 us; the launch traced here: 323 us
  waiting for transfers between devices  114 us (35%)
  Pallas kernels  76.1 us (23%)
  starting transfers between devices  71.3 us (22%)
  local copies, waits for them, and re-layouts  26.7 us (8%)
  other arithmetic  19.5 us (6%)
  between operations  15 us (5%)
    ppermute x33, waiting for transfers between devices, shift(): lax.ppermute(x, 'wide', [(i, (i + step) % size) for i in range(size)])  76.9 us
    pallas_call x19, Pallas kernels, call(): pl.pallas_call(kernel, grid_spec=pltpu.PrefetchScalarGridSpec(num_scalar_...  76.1 us
    ppermute x33, starting transfers between devices, shift(): lax.ppermute(x, 'wide', [(i, (i + step) % size) for i in range(size)])  53.1 us
    ppermute x8, waiting for transfers between devices, turn_batch(): return lax.ppermute(x, 'batch', [(i, size - 1 - i) for i in range(size)])  22.2 us
    unnamed x122, local copies, waits for them, and re-layouts  15.8 us
    ppermute x20, waiting for transfers between devices, swap(): return lax.ppermute(x, 'head', [(i, i ^ bit) for i in range(size)])  15.2 us
    ppermute x20, starting transfers between devices, swap(): return lax.ppermute(x, 'head', [(i, i ^ bit) for i in range(size)])  10.9 us
    ppermute x8, starting transfers between devices, turn_batch(): return lax.ppermute(x, 'batch', [(i, size - 1 - i) for i in range(size)])  7.22 us
  transfers between devices with their start and end apart: 63, of which 23 were waited for; matrix products, arithmetic and copies ran while one was open for 8% of the time, Pallas kernels for 21%

commit v1 on v0

--- a/solution.py
+++ b/solution.py
@@ -457,6 +457,9 @@
 
 
 COST = 2 * 10**10
+BACK_COST = COST
+FF_COST = 10**8
+NORM_COST = COST
 LIMIT = 28
 SMALL = 16
 MIDDLE = 24
@@ -471,7 +474,9 @@
     return pl.BlockSpec((1, *x.shape[1:]), lambda i, *_, nd=x.ndim: (l,) + (0,) * (nd - 1))
 
 
-def call(kernel, grid, ins, outs, scratch=(), prefetch=(), limit=SMALL, cost=COST):
+def call(kernel, grid, ins, outs, scratch=(), prefetch=(), limit=SMALL, cost=COST, earlier=()):
+    first = len(prefetch) + len(ins)
+    ins = [*ins, *[(x, pl.BlockSpec(memory_space=pl.ANY)) for x in earlier]]
     return pl.pallas_call(
         kernel,
         grid_spec=pltpu.PrefetchScalarGridSpec(
@@ -482,6 +487,7 @@
             scratch_shapes=list(scratch),
         ),
         out_shape=[jax.ShapeDtypeStruct(shape, kind) for shape, kind, _ in outs],
+        input_output_aliases={first + i: i for i in range(len(earlier))},
         cost_estimate=pl.CostEstimate(flops=cost, bytes_accessed=0, transcendentals=0),
         compiler_params=pltpu.CompilerParams(vmem_limit_bytes=limit * 2**20),
     )(*prefetch, *[x for x, _ in ins])
@@ -535,6 +541,7 @@
         + [(t, full_spec(t)) for t in terms],
         [whole_out((n, width), F32), whole_out((n, width), BF)],
         prefetch=(place,),
+        cost=FF_COST,
     )
 
 
@@ -565,6 +572,7 @@
         + [(t, full_spec(t)) for t in terms],
         [whole_out((n, width), F32), whole_out((n, width), BF), whole_out((1, width), F32)],
         prefetch=(place,),
+        cost=NORM_COST,
     )
 
 
@@ -625,6 +633,7 @@
         [whole_out((count * n, hidden), F32), whole_out((count * n, hidden), BF), whole_out((count * n, width), BF)]
         + ([whole_out((count, n, width), BF)] if blocks else part_outs(count, n, width)),
         prefetch=(spot,),
+        cost=FF_COST,
     )
     return slope, low, x_all, parts[0] if blocks else parts
 
@@ -683,31 +692,27 @@
     return call(
         functools.partial(ff_weights_kernel, outer),
         2,
-        [(x, full_spec(x)) for x in (xs, gs)] + [(d_pre, cut), (hidden, cut)],
+        [(far(x), full_spec(x)) for x in (xs, gs)] + [(far(d_pre), cut), (far(hidden), cut)],
         [(shape, F32, out), (shape, BF, out)],
         prefetch=(spot,),
         cost=COST // 4,
     )
 
 
-def ff_finish_kernel(spot_ref, *refs):
-    *refs, in_ref, mlp_ref = refs
+def ff_finish_kernel(spot_ref, mine_ref, got_ref, *refs):
+    in_ref, mlp_ref = refs[-2:]
     core = spot_ref[CORE] == 1
-    for l in range(2):
-        mine, got = refs[2 * l][0].astype(F32), refs[2 * l + 1][0].astype(F32)
-        in_ref[l] = jnp.where(core, got, mine)
-        mlp_ref[l] = jnp.where(core, mine, got)
-
-
-def ff_finish(spot, pairs, outers):
-    unused, rows, width = pairs[0][0].shape
-    ins = []
-    for (mine, got), outer in zip(pairs, outers):
-        inner = Y_BIT if outer == X_BIT else X_BIT
-        spec = pl.BlockSpec((1, rows, width), lambda i, p, o=outer, n=inner: (i ^ (2 * p[o] + p[n]), 0, 0))
-        ins += [(mine, spec), (got, spec)]
-    out = ((2, 4 * rows, width), F32, pl.BlockSpec((2, rows, width), lambda i, p: (0, i, 0)))
-    return call(ff_finish_kernel, 4, ins, [out, out], prefetch=(spot,))
+    mine, got = mine_ref[0].astype(F32), got_ref[0].astype(F32)
+    in_ref[0] = jnp.where(core, got, mine)
+    mlp_ref[0] = jnp.where(core, mine, got)
+
+
+def ff_finish(spot, l, mine, got, outer, earlier=()):
+    unused, rows, width = mine.shape
+    inner = Y_BIT if outer == X_BIT else X_BIT
+    spec = pl.BlockSpec((1, rows, width), lambda i, p: (i ^ (2 * p[outer] + p[inner]), 0, 0))
+    out = ((2, 4 * rows, width), F32, pl.BlockSpec((1, rows, width), lambda i, p: (l, i, 0)))
+    return call(ff_finish_kernel, 4, [(mine, spec), (got, spec)], [out, out], prefetch=(spot,), earlier=earlier)
 
 
 def attn_kernel(mode, count, *refs):
@@ -829,9 +834,9 @@
     pair_k = pl.BlockSpec((tk, PAIR), lambda i: (0, i))
     stat = pl.BlockSpec((1, tq, PAIR), lambda i: (i, 0, 0))
     ins = [(x, full_spec(x)) for x in (*acts, *grads)] + [
-        (w_qkv, pl.BlockSpec((1, 3, HEAD_DIM, width), lambda i: (l, 0, i, 0))),
-        (w_att, pl.BlockSpec((1, HEAD_DIM, width), lambda i: (l, i, 0))),
-        *[(part, pl.BlockSpec((2, HEAD_DIM, width), lambda i, h=h: (h, i, 0))) for h in range(2)],
+        (far(w_qkv), pl.BlockSpec((1, 3, HEAD_DIM, width), lambda i: (l, 0, i, 0))),
+        (far(w_att), pl.BlockSpec((1, HEAD_DIM, width), lambda i: (l, i, 0))),
+        *[(far(part), pl.BlockSpec((2, HEAD_DIM, width), lambda i, h=h: (h, i, 0))) for h in range(2)],
         (qid, full_spec(qid)),
         (kid, full_spec(kid)),
     ]
@@ -851,7 +856,8 @@
         scratch += [pltpu.VMEM((tk, width), F32)]
     if mode != "back":
         outs += [whole_out((n, width), F32), whole_out((n, width), BF)]
-    return call(functools.partial(attn_kernel, mode, count), steps, ins, outs, scratch, limit=LIMIT)
+    cost = BACK_COST if mode == "back" else COST
+    return call(functools.partial(attn_kernel, mode, count), steps, ins, outs, scratch, limit=LIMIT, cost=cost)
 
 
 def attn_weights_kernel(spot_ref, own_act, other_act, g_own, g_other, dq_ref, dk_ref, dv_ref, o_ref, own_ref, part_ref, act_all):
@@ -904,35 +910,35 @@
     )
 
 
-def attn_finish_kernel(spot_ref, *refs):
-    *refs, qkv_ref, att_ref = refs
+def attn_finish_kernel(spot_ref, mine_ref, got_ref, *refs):
+    qkv_ref, att_ref = refs[-2:]
     matrix = pl.program_id(0)
     second = spot_ref[X_BIT] == 1
-    for l in range(2):
-        mine, got = refs[2 * l][0].astype(F32), refs[2 * l + 1][0].astype(F32)
-        whole = jnp.concatenate([jnp.where(second, got, mine), jnp.where(second, mine, got)], axis=0)
-
-        @pl.when(matrix < 3)
-        def _():
-            qkv_ref[l, 0] = whole
-
-        @pl.when(matrix == 3)
-        def _():
-            att_ref[l] = whole
-
-
-def attn_finish(spot, pairs):
-    unused, rows, width = pairs[0][0].shape
+    mine, got = mine_ref[0].astype(F32), got_ref[0].astype(F32)
+    whole = jnp.concatenate([jnp.where(second, got, mine), jnp.where(second, mine, got)], axis=0)
+
+    @pl.when(matrix < 3)
+    def _():
+        qkv_ref[0, 0] = whole
+
+    @pl.when(matrix == 3)
+    def _():
+        att_ref[0] = whole
+
+
+def attn_finish(spot, l, mine, got, earlier=()):
+    unused, rows, width = mine.shape
     spec = pl.BlockSpec((1, rows, width), lambda i, p: (lax.rem(p[WIDE] - i + 4, 4), 0, 0))
     return call(
         attn_finish_kernel,
         4,
-        [(x, spec) for pair in pairs for x in pair],
+        [(mine, spec), (got, spec)],
         [
-            ((2, 3, 2 * rows, width), F32, pl.BlockSpec((2, 1, 2 * rows, width), lambda i, p: (0, jnp.minimum(i, 2), 0, 0))),
-            whole_out((2, 2 * rows, width), F32),
+            ((2, 3, 2 * rows, width), F32, pl.BlockSpec((1, 1, 2 * rows, width), lambda i, p: (l, jnp.minimum(i, 2), 0, 0))),
+            ((2, 2 * rows, width), F32, pl.BlockSpec((1, 2 * rows, width), lambda i, p: (l, 0, 0))),
         ],
         prefetch=(spot,),
+        earlier=earlier,
     )
 
 
@@ -1107,53 +1113,55 @@
     def gain_of(got):
         return got[-16:-8].astype(F32) + got[-8:].astype(F32)
 
-    got_w0, half_w1, half_f1 = tie(got_w0, half_w1, half_f1)
+    got_f0 = turn_low(send_f0)
+    got_w0, half_w1, half_f1, got_f0 = tie(got_w0, half_w1, half_f1, got_f0)
     sum_w0 = own_w0 + got_w0.astype(F32)
-    got_w0, got_f0, *got_b1 = together(
+    got_w0, got_f1, *got_b1 = together(
         (sum_w0[1].astype(BF), turn_batch),
-        (send_f0, turn_low),
+        (half_f1[1].astype(BF), turn_high),
         *[(half_w1[s + 1].astype(BF), f) for s, f in enumerate(shifts(-1))],
     )
     block_w1 = sum_of(half_w1[0], got_b1).astype(BF)
     half_w0 = sum_w0[0] + got_w0.astype(F32)
+    block_f1 = (half_f1[0] + got_f1.astype(F32)).astype(BF)
     sum_f0 = keep_f0 + got_f0.astype(F32)
     rows_f = sum_f0.shape[2]
     got_f0, got_f1, *got_b0 = together(
         (with_gain(sum_f0[1], gain), turn_high),
-        (half_f1[1].astype(BF), turn_high),
+        (block_f1, turn_batch),
         *[(half_w0[s + 1].astype(BF), f) for s, f in enumerate(shifts(-1))],
     )
     gain = gain + gain_of(got_f0)
     block_w0 = sum_of(half_w0[0], got_b0)
     half_f0 = sum_f0[0] + got_f0[: 2 * rows_f].reshape(2, rows_f, width).astype(F32)
-    block_f1 = (half_f1[0] + got_f1.astype(F32)).astype(BF)
+    pair_f1 = jnp.stack([block_f1, got_f1])
     got_f0, got_f1, *got_b1 = together(
-        (with_gain(half_f0[1], gain), turn_batch), (block_f1, turn_batch), *[(block_w1, f) for f in shifts(1)]
+        (with_gain(half_f0[1], gain), turn_batch), (pair_f1, turn_high), *[(block_w1, f) for f in shifts(1)]
     )
     gain = gain + gain_of(got_f0)
     block_f0 = (half_f0[0] + got_f0[:rows_f].astype(F32)).astype(BF)
-    pair_f1 = jnp.stack([block_f1, got_f1])
+    full_f1 = jnp.stack([pair_f1, got_f1], axis=1).reshape(4, rows_f, width)
     mine_w1 = jnp.stack([block_w1, *got_b1])
     block_w0 = with_gain(block_w0, gain)
-    got_f0, got_f1, *got_b0 = together(
-        (block_f0, turn_batch), (pair_f1, turn_high), *[(block_w0, f) for f in shifts(1)]
+    got_f0, got_w1, *got_b0 = together(
+        (block_f0, turn_batch), (mine_w1, turn_batch), *[(block_w0, f) for f in shifts(1)]
     )
     gain = sum_of(gain, [gain_of(g) for g in got_b0])
     pair_f0 = jnp.stack([block_f0, got_f0])
-    full_f1 = jnp.stack([pair_f1, got_f1], axis=1).reshape(4, rows_f, width)
     rows_w = half_w0.shape[1]
     mine_w0 = jnp.stack([g[:rows_w] for g in (block_w0, *got_b0)])
     mine_w0, ends = tie(mine_w0, ends)
-    got_w0, got_w1, got_f0, got_g, got_f1 = together(
-        (mine_w0, turn_batch), (mine_w1, turn_batch), (pair_f0, turn_high), (gain, turn_low), (full_f1, turn_low)
+    got_w0, got_f0, got_g, got_f1 = together(
+        (mine_w0, turn_batch), (pair_f0, turn_high), (gain, turn_low), (full_f1, turn_low)
     )
     full_f0 = jnp.concatenate([pair_f0, got_f0])
     got_f0 = turn_low(full_f0)
     d_gains = (gain + got_g)[:2]
-    d_in, d_mlp = ff_finish(spot, ((full_f0, got_f0), (full_f1, got_f1)), (Y_BIT, X_BIT))
+    late = ff_finish(spot, 1, full_f1, got_f1, X_BIT)
+    d_in, d_mlp = ff_finish(spot, 0, full_f0, got_f0, Y_BIT, late)
     out = tokens.astype(F32) + ends[:, :, :width].astype(F32)
     d_tokens = cotangent.astype(F32) + ends[:, :, width:].astype(F32)
-    d_qkv, d_att = attn_finish(spot, ((mine_w0, got_w0), (mine_w1, got_w1)))
+    d_qkv, d_att = attn_finish(spot, 0, mine_w0, got_w0, attn_finish(spot, 1, mine_w1, got_w1))
     return (out.reshape(shape), d_tokens.reshape(shape), d_qkv, d_att, d_in, d_mlp, d_gains)
 
 

time: 325 us -> 310 us (0.954)
  waiting for transfers between devices: 114 us -> 77.5 us
  Pallas kernels: 76.1 us -> 86.4 us
  other arithmetic: 19.5 us -> 25.1 us
    ppermute x33, waiting for transfers between devices: 76.9 us -> 57 us  [shift(): lax.ppermute(x, 'wide', [(i, (i + step) % size) for i in range(size)])]
    pallas_call x19 -> x21, Pallas kernels: 76.1 us -> 86.4 us  [call(): pl.pallas_call(kernel, grid_spec=pltpu.PrefetchScalarGridSpec(num_scalar_...]
    ppermute x8, waiting for transfers between devices: 22.2 us -> 13.1 us  [turn_batch(): return lax.ppermute(x, 'batch', [(i, size - 1 - i) for i in range(size)])]
    ppermute x20, waiting for transfers between devices: 15.2 us -> 7.44 us  [swap(): return lax.ppermute(x, 'head', [(i, i ^ bit) for i in range(size)])]
    ppermute x33, starting transfers between devices: 53.1 us -> 56.7 us  [shift(): lax.ppermute(x, 'wide', [(i, (i + step) % size) for i in range(size)])]
    unnamed x122 -> x156, local copies, waits for them, and re-layouts: 15.8 us -> 14.9 us
  transfers between devices with their start and end apart: 63 -> 63, of which waited for: 23 -> 16; matrix products, arithmetic and copies ran while one was open for 8% -> 10% of each run, Pallas kernels for 21% -> 25%
where the time goes in v1:
time: 310 us; the launch traced here: 306 us
  Pallas kernels  86.4 us (28%)
  waiting for transfers between devices  77.5 us (25%)
  starting transfers between devices  74.2 us (24%)
  local copies, waits for them, and re-layouts  27.4 us (9%)
  other arithmetic  25.1 us (8%)
  between operations  15.1 us (5%)
    pallas_call x21, Pallas kernels, call(): pl.pallas_call(kernel, grid_spec=pltpu.PrefetchScalarGridSpec(num_scalar_...  86.4 us
    ppermute x33, waiting for transfers between devices, shift(): lax.ppermute(x, 'wide', [(i, (i + step) % size) for i in range(size)])  57 us
    ppermute x33, starting transfers between devices, shift(): lax.ppermute(x, 'wide', [(i, (i + step) % size) for i in range(size)])  56.7 us
    unnamed x156, local copies, waits for them, and re-layouts  14.9 us
    ppermute x8, waiting for transfers between devices, turn_batch(): return lax.ppermute(x, 'batch', [(i, size - 1 - i) for i in range(size)])  13.1 us
    ppermute x20, starting transfers between devices, swap(): return lax.ppermute(x, 'head', [(i, i ^ bit) for i in range(size)])  9.86 us
    ppermute x8, starting transfers between devices, turn_batch(): return lax.ppermute(x, 'batch', [(i, size - 1 - i) for i in range(size)])  7.53 us
    ppermute x20, waiting for transfers between devices, swap(): return lax.ppermute(x, 'head', [(i, i ^ bit) for i in range(size)])  7.44 us
  transfers between devices with their start and end apart: 63, of which 16 were waited for; matrix products, arithmetic and copies ran while one was open for 10% of the time, Pallas kernels for 25%

profile of v1, /device:TPU:0, one launch (start us, length us, event | category | flops | bytes accessed | tf_op | source)
XLA Modules:
  0.0 305.7 jit_solution(8816413739668178758)
XLA Ops:
  9.0 1.4 shard_map.135.refs_0_
  10.4 3.0 collective-permute-start
  13.4 2.6 collective-permute-start.1
  16.0 1.3 collective-permute-start.2
  20.3 1.5 collective-permute-start.7
  23.9 2.9 fusion.34
  27.6 1.5 copy.36
  29.0 1.4 copy.35
  30.5 1.4 pad_maximum_fusion
  31.9 3.9 %shard_map.136 = (f32[512,768]{1,0:T(8,128)S(1)}, bf16[512,768]{1,0:T(8,128)(2,1)S(1)}, bf16[512,768]{1,0:T(8,128)(2,1)S(1)}, f32[128,768]{1,0:T(8,128)S(1)}, bf...) custom-call(s32[5]{0:T(128)S(1)} %stack.80.place_ref.spot_ref, ...), custom_call_target="tpu_custom_call" | custom-call | flops 100000000 | tf_op jit(solution)/shard_map/pallas_call | solution.py:480
  37.9 3.0 collective-permute-start.3
  41.5 6.0 %collective-permute-done.7.refs_4_.refs_5_ = bf16[4,192,768]{2,1,0:T(8,128)(2,1)} collective-permute-done((bf16[4,192,768]{2,1,0:T(8,128)(2,1)}, bf16[4,192,768]{2,1,0:T(8,128)(2,1)}, u32[]{:S(2)}, u32[]{:S(2)}) %collective-permute-start.7) | collective-permute-done | bytes 1179680 | tf_op jit(solution)/shard_map/ppermute | solution.py:47
  47.5 10.6 %shard_map.137 = (bf16[256,384]{1,0:T(8,128)(2,1)S(1)}, bf16[1024,384]{1,0:T(8,128)(2,1)S(1)}, bf16[1024,384]{1,0:T(8,128)(2,1)S(1)}, bf16[256,384]{1,0:T(8,128)...) custom-call(bf16[512,768]{1,0:T(8,128)(2,1)S(1)} %get-tuple-element.172.refs_0_.own_act., ...), custom_call_target="tpu_custom_call" | custom-call | flops 20000000000 | tf_op jit(solution)/shard_map/pallas_call | solution.py:480
  59.1 1.6 collective-permute-start.16
  62.1 2.6 collective-permute-start.11
  64.7 10.0 %collective-permute-done.10.refs_2_ = bf16[128,768]{1,0:T(8,128)(2,1)S(1)} collective-permute-done((bf16[128,768]{1,0:T(8,128)(2,1)S(1)}, bf16[128,768]{1,0:T(8,128)(2,1)S(1)}, u32[]{:S(2)}, u32[]{:S(2)}) %collective-permute-start.10) | collective-permute-done | bytes 196640 | tf_op jit(solution)/shard_map/ppermute | solution.py:52
  74.7 3.5 %collective-permute-done.9.refs_1_ = bf16[128,768]{1,0:T(8,128)(2,1)S(1)} collective-permute-done((bf16[128,768]{1,0:T(8,128)(2,1)S(1)}, bf16[128,768]{1,0:T(8,128)(2,1)S(1)}, u32[]{:S(2)}, u32[]{:S(2)}) %collective-permute-start.9) | collective-permute-done | bytes 196640 | tf_op jit(solution)/shard_map/ppermute | solution.py:52
  78.2 3.7 %shard_map.139 = (f32[512,768]{1,0:T(8,128)S(1)}, bf16[512,768]{1,0:T(8,128)(2,1)S(1)}, bf16[512,768]{1,0:T(8,128)(2,1)S(1)}, bf16[4,128,768]{2,1,0:T(8,128)(2,1)}) custom-call(s32[5]{0:T(128)S(1)} %stack.80.place_ref.spot_ref, bf16[128,768]{1,0:T(8,128)(2,1)S(1)} %get-tuple-element.180.refs_0_, bf16[128,768]{1,0:T(8,128)(2,1)S(1)} %collective-permute-done.9.refs_1_, ...), custom_call_target="tpu_custom_call" | custom-call | flops 100000000 | tf_op jit(solution)/shard_map/pallas_call | solution.py:480
  82.8 4.6 %collective-permute-start.12 = (bf16[128,768]{1,0:T(8,128)(2,1)S(1)}, bf16[128,768]{1,0:T(8,128)(2,1)S(1)}, u32[]{:S(2)}, u32[]{:S(2)}) collective-permute-start(bf16[128,768]{1,0:T(8,128)(2,1)S(1)} %copy-done.17), channel_id=1, source_target_pairs={{0,1},{1,2},{2,3},{3,0},{4,5},{5,6},{6,7},{7,4},{8,9},{9,10},{10,1... | collective-permute-start | bytes 589832 | tf_op jit(solution)/shard_map/ppermute | solution.py:52
  87.4 2.5 collective-permute-start.14
  90.9 17.3 %shard_map.141 = (bf16[256,384]{1,0:T(8,128)(2,1)S(1)}, bf16[1024,384]{1,0:T(8,128)(2,1)S(1)}, bf16[1024,384]{1,0:T(8,128)(2,1)S(1)}, bf16[256,384]{1,0:T(8,128)...) custom-call(bf16[512,768]{1,0:T(8,128)(2,1)S(1)} %get-tuple-element., ...), custom_call_target="tpu_custom_call" | custom-call | flops 20000000000 | tf_op jit(solution)/shard_map/pallas_call | solution.py:480
  109.2 1.4 collective-permute-done.17.got_ref
  111.4 2.0 collective-permute-start.18
  114.2 3.8 %shard_map.143 = (f32[2,2,192,768]{3,2,1,0:T(8,128)S(1)}, bf16[2,2,192,768]{3,2,1,0:T(8,128)(2,1)S(1)}) custom-call(s32[5]{0:T(128)S(1)} %stack.80.place_ref.spot_ref, bf16[512,768]{1,0:T(8,128)(2,1)} %copy-done.31, bf16[512,768]{1,0:T(8,128)(2,1)} %copy-done.40, bf16[512,768]{1,0:T(8,128)(2,1)} %copy-done.39, bf16[512,768]{1,0:T(8,128)(2,1)} %copy-done.33), custom_call_target="tpu_custom_call" | custom-call | flops 5000000000 | tf_op jit(solution)/shard_map/pallas_call | solution.py:480
  118.0 1.4 copy-done.1
  120.5 3.5 %shard_map.144 = (f32[2,4,96,768]{3,2,1,0:T(8,128)S(1)}, bf16[2,4,96,768]{3,2,1,0:T(8,128)(2,1)S(1)}) custom-call(s32[5]{0:T(128)S(1)} %stack.80.place_ref.spot_ref, bf16[512,768]{1,0:T(8,128)(2,1)S(1)} %copy-done.32, bf16[512,768]{1,0:T(8,128)(2,1)S(1)} %collective-permute-done.15.refs_1_.other_act, bf16[128,768]{1,0:T(8,128)(2,1)S(1)} %copy-done.17, ...), custom_call_target="tpu_custom_call" | custom-call | flops 5000000000 | tf_op jit(solution)/shard_map/pallas_call | solution.py:480
  124.1 6.2 %collective-permute-done.20.refs_2_ = bf16[128,768]{1,0:T(8,128)(2,1)S(1)} collective-permute-done((bf16[128,768]{1,0:T(8,128)(2,1)S(1)}, bf16[128,768]{1,0:T(8,128)(2,1)S(1)}, u32[]{:S(2)}, u32[]{:S(2)}) %collective-permute-start.20) | collective-permute-done | bytes 196640 | tf_op jit(solution)/shard_map/ppermute | solution.py:52
  130.3 1.6 shard_map.145
  132.8 1.3 collective-permute-start.22
  134.2 2.0 collective-permute-start.28
  136.2 2.8 collective-permute-start.29
  142.0 11.5 %shard_map.146 = (bf16[256,384]{1,0:T(8,128)(2,1)S(1)}, bf16[1024,384]{1,0:T(8,128)(2,1)S(1)}, bf16[1024,384]{1,0:T(8,128)(2,1)S(1)}, f32[512,768]{1,0:T(8,128)S(1)}, bf16[512,768]{1,0:T(8,128)(2,1)S(1)}) custom-call(bf16[128,768]{1,0:T(8,128)(2,1)} %get-tuple-element.209.refs_0_.g_own, bf16[128,768]{1,0:T(8,128)(2,1)S(1)} %copy-done.37, ...), custom_call_target="tpu_custom_call" | custom-call | flops 20000000000 | tf_op jit(solution)/shard_map/pallas_call | solution.py:480
  153.5 5.4 %shard_map.147 = (f32[2,4,96,768]{3,2,1,0:T(8,128)S(1)}, bf16[2,4,96,768]{3,2,1,0:T(8,128)(2,1)}) custom-call(s32[5]{0:T(128)S(1)} %stack.80.place_ref.spot_ref, bf16[512,768]{1,0:T(8,128)(2,1)S(1)} %copy-done.28, bf16[512,768]{1,0:T(8,128)(2,1)S(1)} %copy-done.30, bf16[128,768]{1,0:T(8,128)(2,1)} %get-tuple-element.209.refs_0_.g_own, ...), custom_call_target="tpu_custom_call" | custom-call | flops 5000000000 | tf_op jit(solution)/shard_map/pallas_call | solution.py:480
  160.3 1.5 collective-permute-start.27
  161.8 1.8 shard_map.148
  165.4 8.5 %collective-permute-start.32 = (bf16[128,768]{1,0:T(8,128)(2,1)S(1)}, bf16[128,768]{1,0:T(8,128)(2,1)S(1)}, u32[]{:S(2)}, u32[]{:S(2)}) collective-permute-start(bf16[128,768]{1,0:T(8,128)(2,1)S(1)} %get-tuple-element.244), channel_id=1, source_target_pairs={{0,3},{1,0},{2,1},{3,2},{4,7},{5,4},{6,5},{7,6},{8,11},{9,8},{10,9... | collective-permute-start | bytes 589832 | tf_op jit(solution)/shard_map/ppermute | solution.py:52
  173.9 4.8 %shard_map.150 = (f32[2,2,192,768]{3,2,1,0:T(8,128)S(1)}, bf16[2,2,192,768]{3,2,1,0:T(8,128)(2,1)}) custom-call(s32[5]{0:T(128)S(1)} %stack.80.place_ref.spot_ref, bf16[512,768]{1,0:T(8,128)(2,1)} %copy-done.27, bf16[512,768]{1,0:T(8,128)(2,1)} %copy-done.42, bf16[512,768]{1,0:T(8,128)(2,1)} %copy-done.41, bf16[512,768]{1,0:T(8,128)(2,1)} %copy-done.26), custom_call_target="tpu_custom_call" | custom-call | flops 5000000000 | tf_op jit(solution)/shard_map/pallas_call | solution.py:480
  178.7 1.4 copy-done.8
  183.3 6.4 %collective-permute-done.33.refs_3_ = bf16[128,768]{1,0:T(8,128)(2,1)S(1)} collective-permute-done((bf16[128,768]{1,0:T(8,128)(2,1)S(1)}, bf16[128,768]{1,0:T(8,128)(2,1)S(1)}, u32[]{:S(2)}, u32[]{:S(2)}) %collective-permute-start.33) | collective-permute-done | bytes 196640 | tf_op jit(solution)/shard_map/ppermute | solution.py:52
  189.7 1.7 shard_map.151
  191.5 1.5 bitcast_add_fusion
  193.1 3.3 %collective-permute-done.31 = bf16[4,96,768]{2,1,0:T(8,128)(2,1)} collective-permute-done((bf16[4,96,768]{2,1,0:T(8,128)(2,1)}, bf16[4,96,768]{2,1,0:T(8,128)(2,1)}, u32[]{:S(2)}, u32[]{:S(2)}) %collective-permute-start.31) | collective-permute-done | bytes 589856 | tf_op jit(solution)/shard_map/ppermute | solution.py:204
  197.6 1.6 convert_add_fusion.1
  201.5 3.5 %collective-permute-start.38 = (bf16[96,768]{1,0:T(8,128)(2,1)S(1)}, bf16[96,768]{1,0:T(8,128)(2,1)S(1)}, u32[]{:S(2)}, u32[]{:S(2)}) collective-permute-start(bf16[96,768]{1,0:T(8,128)(2,1)S(1)} %get-tuple-element.260), channel_id=1, source_target_pairs={{0,3},{1,0},{2,1},{3,2},{4,7},{5,4},{6,5},{7,6},{8,11},{9,8},{10,9... | collective-permute-start | bytes 442376 | tf_op jit(solution)/shard_map/ppermute | solution.py:52
  205.8 1.6 convert_add_fusion
  207.5 2.2 collective-permute-done.38
  209.7 5.8 %collective-permute-done.39 = bf16[96,768]{1,0:T(8,128)(2,1)S(1)} collective-permute-done((bf16[96,768]{1,0:T(8,128)(2,1)S(1)}, bf16[96,768]{1,0:T(8,128)(2,1)S(1)}, u32[]{:S(2)}, u32[]{:S(2)}) %collective-permute-start.39) | collective-permute-done | bytes 147488 | tf_op jit(solution)/shard_map/ppermute | solution.py:52
  219.3 2.0 collective-permute-start.45
  222.8 8.0 %collective-permute-done.44 = bf16[96,768]{1,0:T(8,128)(2,1)S(1)} collective-permute-done((bf16[96,768]{1,0:T(8,128)(2,1)S(1)}, bf16[96,768]{1,0:T(8,128)(2,1)S(1)}, u32[]{:S(2)}, u32[]{:S(2)}) %collective-permute-start.44) | collective-permute-done | bytes 147488 | tf_op jit(solution)/shard_map/ppermute | solution.py:52
  239.1 2.8 collective-permute-start.50
  243.1 3.0 collective-permute-done.48
  246.1 2.6 collective-permute-done.49
  252.0 1.7 collective-permute-start.51
  253.7 2.6 collective-permute-start.53
  256.3 3.3 %collective-permute-start.54 = (bf16[112,768]{1,0:T(8,128)(2,1)S(1)}, bf16[112,768]{1,0:T(8,128)(2,1)S(1)}, u32[]{:S(2)}, u32[]{:S(2)}) collective-permute-start(bf16[112,768]{1,0:T(8,128)(2,1)S(1)} %pad_maximum_fusion.11), channel_id=1, source_target_pairs={{0,2},{1,3},{2,0},{3,1},{4,6},{5,7},{6,4},{7,5},{8,10},{9,11},{10,... | collective-permute-start | bytes 516104 | tf_op jit(solution)/shard_map/ppermute | solution.py:52
  260.9 3.5 %collective-permute-done.53 = bf16[112,768]{1,0:T(8,128)(2,1)S(1)} collective-permute-done((bf16[112,768]{1,0:T(8,128)(2,1)S(1)}, bf16[112,768]{1,0:T(8,128)(2,1)S(1)}, u32[]{:S(2)}, u32[]{:S(2)}) %collective-permute-start.53) | collective-permute-done | bytes 172064 | tf_op jit(solution)/shard_map/ppermute | solution.py:52
  264.4 5.1 %collective-permute-done.54 = bf16[112,768]{1,0:T(8,128)(2,1)S(1)} collective-permute-done((bf16[112,768]{1,0:T(8,128)(2,1)S(1)}, bf16[112,768]{1,0:T(8,128)(2,1)S(1)}, u32[]{:S(2)}, u32[]{:S(2)}) %collective-permute-start.54) | collective-permute-done | bytes 172064 | tf_op jit(solution)/shard_map/ppermute | solution.py:52
  270.5 1.4 add_add_fusion
  274.3 2.8 shard_map.152
  277.1 2.0 convert_add_fusion.3
  279.1 9.8 %collective-permute-done.56.got_ref = bf16[4,96,768]{2,1,0:T(8,128)(2,1)S(1)} collective-permute-done((bf16[4,96,768]{2,1,0:T(8,128)(2,1)S(1)}, bf16[4,96,768]{2,1,0:T(8,128)(2,1)S(1)}, u32[]{:S(2)}, u32[]{:S(2)}) %collective-permute-start.56) | collective-permute-done | bytes 589856 | tf_op jit(solution)/shard_map/ppermute | solution.py:204
  289.5 3.2 %shard_map.154 = (f32[2,768,768]{2,1,0:T(8,128)}, f32[2,768,768]{2,1,0:T(8,128)}) custom-call(s32[5]{0:T(128)S(1)} %stack.80.place_ref.spot_ref, bf16[4,192,768]{2,1,0:T(8,128)(2,1)S(1)} %bitcast.123, bf16[4,192,768]{2,1,0:T(8,128)(2,1)S(1)} %collective-permute-done.59.got_ref), custom_call_target="tpu_custom_call" | custom-call | flops 20000000000 | tf_op jit(solution)/shard_map/pallas_call | solution.py:480
  292.9 2.8 shard_map.153
  295.7 3.2 %shard_map.155 = (f32[2,768,768]{2,1,0:T(8,128)}, f32[2,768,768]{2,1,0:T(8,128)}) custom-call(s32[5]{0:T(128)S(1)} %stack.80.place_ref.spot_ref, bf16[4,192,768]{2,1,0:T(8,128)(2,1)S(1)} %pad_maximum_fusion.3.mine_ref, bf16[4,192,768]{2,1,0:T(8,128)(2,1)S(1)} %collective-permute-done.60.got_ref, ...), custom_call_target="tpu_custom_call", output_to_operand_aliasing={{0}: (3, {}), {1}: (4, {})} | custom-call | flops 20000000000 | tf_op jit(solution)/shard_map/pallas_call | solution.py:480
  (311 shorter events, 55.8 us)
Async XLA Ops:
  7.2 184.3 %reduce-scatter.2.cloned.1.call-start = ((), (), s32[]{:S(2)}) async-start(), calls=%async_computation.1 | async-start | bytes 983040 | tf_op jit(solution)/shard_map/reduce_scatter | solution.py:1101
  10.4 21.5 %collective-permute-start = (bf16[128,768]{1,0:T(8,128)(2,1)}, bf16[128,768]{1,0:T(8,128)(2,1)}, u32[]{:S(2)}, u32[]{:S(2)}) collective-permute-start(bf16[128,768]{1,0:T(8,128)(2,1)} %shard_map.135.refs_0_), channel_id=1, source_target_pairs={{0,1},{1,2},{2,3},{3,0},{4,5},{5,6},{6,7},{7,4},{8,9},{9,10},{10,1... | collective-permute-start | bytes 589832 | tf_op jit(solution)/shard_map/ppermute | solution.py:52
  13.4 18.5 %collective-permute-start.1 = (bf16[128,768]{1,0:T(8,128)(2,1)}, bf16[128,768]{1,0:T(8,128)(2,1)}, u32[]{:S(2)}, u32[]{:S(2)}) collective-permute-start(bf16[128,768]{1,0:T(8,128)(2,1)} %shard_map.135.refs_0_), channel_id=1, source_target_pairs={{0,2},{1,3},{2,0},{3,1},{4,6},{5,7},{6,4},{7,5},{8,10},{9,11},{10,... | collective-permute-start | bytes 589832 | tf_op jit(solution)/shard_map/ppermute | solution.py:52
  16.0 15.9 %collective-permute-start.2 = (bf16[128,768]{1,0:T(8,128)(2,1)}, bf16[128,768]{1,0:T(8,128)(2,1)}, u32[]{:S(2)}, u32[]{:S(2)}) collective-permute-start(bf16[128,768]{1,0:T(8,128)(2,1)} %shard_map.135.refs_0_), channel_id=1, source_target_pairs={{0,3},{1,0},{2,1},{3,2},{4,7},{5,4},{6,5},{7,6},{8,11},{9,8},{10,9... | collective-permute-start | bytes 589832 | tf_op jit(solution)/shard_map/ppermute | solution.py:52
  20.3 27.2 %collective-permute-start.7 = (bf16[4,192,768]{2,1,0:T(8,128)(2,1)}, bf16[4,192,768]{2,1,0:T(8,128)(2,1)}, u32[]{:S(2)}, u32[]{:S(2)}) collective-permute-start(bf16[4,192,768]{2,1,0:T(8,128)(2,1)} %pad_maximum_fusion.1), channel_id=1, source_target_pairs={{0,8},{4,12},{8,0},{12,4},{1,9},{5,13},{9,1},{13,5},{2,10},{6,14},... | collective-permute-start | bytes 3538952 | tf_op jit(solution)/shard_map/ppermute | solution.py:47
  37.9 9.5 %collective-permute-start.6 = (bf16[512,768]{1,0:T(8,128)(2,1)S(1)}, bf16[512,768]{1,0:T(8,128)(2,1)S(1)}, u32[]{:S(2)}, u32[]{:S(2)}) collective-permute-start(bf16[512,768]{1,0:T(8,128)(2,1)S(1)} %get-tuple-element.172.refs_0_.own_act.x_ref), channel_id=1, source_target_pairs={{0,4},{4,0},{8,12},{12,8},{1,5},{5,1},{9,13},{13,9},{2,6},{6,2},{1... | collective-permute-start | bytes 2359304 | tf_op jit(solution)/shard_map/ppermute | solution.py:47
  37.9 22.8 %collective-permute-start.3 = (bf16[128,768]{1,0:T(8,128)(2,1)S(1)}, bf16[128,768]{1,0:T(8,128)(2,1)S(1)}, u32[]{:S(2)}, u32[]{:S(2)}) collective-permute-start(bf16[128,768]{1,0:T(8,128)(2,1)S(1)} %get-tuple-element.169), channel_id=1, source_target_pairs={{0,3},{1,0},{2,1},{3,2},{4,7},{5,4},{6,5},{7,6},{8,11},{9,8},{10,9... | collective-permute-start | bytes 589832 | tf_op jit(solution)/shard_map/ppermute | solution.py:52
  40.9 19.8 %collective-permute-start.4 = (bf16[128,768]{1,0:T(8,128)(2,1)S(1)}, bf16[128,768]{1,0:T(8,128)(2,1)S(1)}, u32[]{:S(2)}, u32[]{:S(2)}) collective-permute-start(bf16[128,768]{1,0:T(8,128)(2,1)S(1)} %get-tuple-element.170), channel_id=1, source_target_pairs={{0,2},{1,3},{2,0},{3,1},{4,6},{5,7},{6,4},{7,5},{8,10},{9,11},{10,... | collective-permute-start | bytes 589832 | tf_op jit(solution)/shard_map/ppermute | solution.py:52
  41.4 19.3 %collective-permute-start.5 = (bf16[128,768]{1,0:T(8,128)(2,1)S(1)}, bf16[128,768]{1,0:T(8,128)(2,1)S(1)}, u32[]{:S(2)}, u32[]{:S(2)}) collective-permute-start(bf16[128,768]{1,0:T(8,128)(2,1)S(1)} %get-tuple-element.171), channel_id=1, source_target_pairs={{0,1},{1,2},{2,3},{3,0},{4,5},{5,6},{6,7},{7,4},{8,9},{9,10},{10,1... | collective-permute-start | bytes 589832 | tf_op jit(solution)/shard_map/ppermute | solution.py:52
  59.0 1.7 collective-permute-start.8
  59.1 30.8 %collective-permute-start.16 = (bf16[4,192,768]{2,1,0:T(8,128)(2,1)S(1)}, bf16[4,192,768]{2,1,0:T(8,128)(2,1)S(1)}, u32[]{:S(2)}, u32[]{:S(2)}) collective-permute-start(bf16[4,192,768]{2,1,0:T(8,128)(2,1)S(1)} %pad_maximum_fusion), channel_id=1, source_target_pairs={{0,8},{4,12},{8,0},{12,4},{1,9},{5,13},{9,1},{13,5},{2,10},{6,14},... | collective-permute-start | bytes 3538952 | tf_op jit(solution)/shard_map/ppermute | solution.py:47
  61.6 68.7 %copy-start.13 = (f32[128,768]{1,0:T(8,128)}, f32[128,768]{1,0:T(8,128)S(1)}, u32[]{:S(2)}) copy-start(f32[128,768]{1,0:T(8,128)S(1)} %get-tuple-element.299.stream_ref) | copy-start | bytes 1179652
  61.6 13.1 %collective-permute-start.10 = (bf16[128,768]{1,0:T(8,128)(2,1)S(1)}, bf16[128,768]{1,0:T(8,128)(2,1)S(1)}, u32[]{:S(2)}, u32[]{:S(2)}) collective-permute-start(bf16[128,768]{1,0:T(8,128)(2,1)S(1)} %get-tuple-element.180.refs_0_), channel_id=1, source_target_pairs={{0,2},{1,3},{2,0},{3,1},{4,6},{5,7},{6,4},{7,5},{8,10},{9,11},{10,... | collective-permute-start | bytes 589832 | tf_op jit(solution)/shard_map/ppermute | solution.py:52
  62.1 12.6 %collective-permute-start.11 = (bf16[128,768]{1,0:T(8,128)(2,1)S(1)}, bf16[128,768]{1,0:T(8,128)(2,1)S(1)}, u32[]{:S(2)}, u32[]{:S(2)}) collective-permute-start(bf16[128,768]{1,0:T(8,128)(2,1)S(1)} %get-tuple-element.180.refs_0_), channel_id=1, source_target_pairs={{0,3},{1,0},{2,1},{3,2},{4,7},{5,4},{6,5},{7,6},{8,11},{9,8},{10,9... | collective-permute-start | bytes 589832 | tf_op jit(solution)/shard_map/ppermute | solution.py:52
  64.7 13.5 %collective-permute-start.9 = (bf16[128,768]{1,0:T(8,128)(2,1)S(1)}, bf16[128,768]{1,0:T(8,128)(2,1)S(1)}, u32[]{:S(2)}, u32[]{:S(2)}) collective-permute-start(bf16[128,768]{1,0:T(8,128)(2,1)S(1)} %get-tuple-element.180.refs_0_), channel_id=1, source_target_pairs={{0,1},{1,2},{2,3},{3,0},{4,5},{5,6},{6,7},{7,4},{8,9},{9,10},{10,1... | collective-permute-start | bytes 589832 | tf_op jit(solution)/shard_map/ppermute | solution.py:52
  82.8 7.1 %collective-permute-start.15 = (bf16[512,768]{1,0:T(8,128)(2,1)S(1)}, bf16[512,768]{1,0:T(8,128)(2,1)S(1)}, u32[]{:S(2)}, u32[]{:S(2)}) collective-permute-start(bf16[512,768]{1,0:T(8,128)(2,1)S(1)} %get-tuple-element.181.refs_0_.x_ref.own_act), channel_id=1, source_target_pairs={{0,4},{4,0},{8,12},{12,8},{1,5},{5,1},{9,13},{13,9},{2,6},{6,2},{1... | collective-permute-start | bytes 2359304 | tf_op jit(solution)/shard_map/ppermute | solution.py:47
  82.8 25.5 %collective-permute-start.12 = (bf16[128,768]{1,0:T(8,128)(2,1)S(1)}, bf16[128,768]{1,0:T(8,128)(2,1)S(1)}, u32[]{:S(2)}, u32[]{:S(2)}) collective-permute-start(bf16[128,768]{1,0:T(8,128)(2,1)S(1)} %copy-done.17), channel_id=1, source_target_pairs={{0,1},{1,2},{2,3},{3,0},{4,5},{5,6},{6,7},{7,4},{8,9},{9,10},{10,1... | collective-permute-start | bytes 589832 | tf_op jit(solution)/shard_map/ppermute | solution.py:52
  87.4 20.9 %collective-permute-start.13 = (bf16[128,768]{1,0:T(8,128)(2,1)S(1)}, bf16[128,768]{1,0:T(8,128)(2,1)S(1)}, u32[]{:S(2)}, u32[]{:S(2)}) collective-permute-start(bf16[128,768]{1,0:T(8,128)(2,1)S(1)} %copy-done.17), channel_id=1, source_target_pairs={{0,2},{1,3},{2,0},{3,1},{4,6},{5,7},{6,4},{7,5},{8,10},{9,11},{10,... | collective-permute-start | bytes 589832 | tf_op jit(solution)/shard_map/ppermute | solution.py:52
  87.4 20.9 %collective-permute-start.14 = (bf16[128,768]{1,0:T(8,128)(2,1)S(1)}, bf16[128,768]{1,0:T(8,128)(2,1)S(1)}, u32[]{:S(2)}, u32[]{:S(2)}) collective-permute-start(bf16[128,768]{1,0:T(8,128)(2,1)S(1)} %copy-done.17), channel_id=1, source_target_pairs={{0,3},{1,0},{2,1},{3,2},{4,7},{5,4},{6,5},{7,6},{8,11},{9,8},{10,9... | collective-permute-start | bytes 589832 | tf_op jit(solution)/shard_map/ppermute | solution.py:52
  108.2 2.4 collective-permute-start.17
  111.4 12.7 %collective-permute-start.18 = (bf16[128,768]{1,0:T(8,128)(2,1)S(1)}, bf16[128,768]{1,0:T(8,128)(2,1)S(1)}, u32[]{:S(2)}, u32[]{:S(2)}) collective-permute-start(bf16[128,768]{1,0:T(8,128)(2,1)S(1)} %get-tuple-element.194), channel_id=1, source_target_pairs={{0,3},{1,0},{2,1},{3,2},{4,7},{5,4},{6,5},{7,6},{8,11},{9,8},{10,9... | collective-permute-start | bytes 589832 | tf_op jit(solution)/shard_map/ppermute | solution.py:52
  113.4 10.7 %collective-permute-start.19 = (bf16[128,768]{1,0:T(8,128)(2,1)S(1)}, bf16[128,768]{1,0:T(8,128)(2,1)S(1)}, u32[]{:S(2)}, u32[]{:S(2)}) collective-permute-start(bf16[128,768]{1,0:T(8,128)(2,1)S(1)} %get-tuple-element.195), channel_id=1, source_target_pairs={{0,4},{4,0},{8,12},{12,8},{1,5},{5,1},{9,13},{13,9},{2,6},{6,2},{1... | collective-permute-start | bytes 589832 | tf_op jit(solution)/shard_map/ppermute | solution.py:47
  113.4 16.9 %collective-permute-start.20 = (bf16[128,768]{1,0:T(8,128)(2,1)S(1)}, bf16[128,768]{1,0:T(8,128)(2,1)S(1)}, u32[]{:S(2)}, u32[]{:S(2)}) collective-permute-start(bf16[128,768]{1,0:T(8,128)(2,1)S(1)} %get-tuple-element.207), channel_id=1, source_target_pairs={{0,2},{1,3},{2,0},{3,1},{4,6},{5,7},{6,4},{7,5},{8,10},{9,11},{10,... | collective-permute-start | bytes 589832 | tf_op jit(solution)/shard_map/ppermute | solution.py:52
  113.4 16.9 %collective-permute-start.21 = (bf16[128,768]{1,0:T(8,128)(2,1)S(1)}, bf16[128,768]{1,0:T(8,128)(2,1)S(1)}, u32[]{:S(2)}, u32[]{:S(2)}) collective-permute-start(bf16[128,768]{1,0:T(8,128)(2,1)S(1)} %get-tuple-element.208), channel_id=1, source_target_pairs={{0,1},{1,2},{2,3},{3,0},{4,5},{5,6},{6,7},{7,4},{8,9},{9,10},{10,1... | collective-permute-start | bytes 589832 | tf_op jit(solution)/shard_map/ppermute | solution.py:52
  132.7 6.3 %collective-permute-start.24 = (bf16[128,768]{1,0:T(8,128)(2,1)}, bf16[128,768]{1,0:T(8,128)(2,1)S(1)}, u32[]{:S(2)}, u32[]{:S(2)}) collective-permute-start(bf16[128,768]{1,0:T(8,128)(2,1)} %get-tuple-element.209.refs_0_.g_own), channel_id=1, source_target_pairs={{0,4},{4,0},{8,12},{12,8},{1,5},{5,1},{9,13},{13,9},{2,6},{6,2},{1... | collective-permute-start | bytes 589832 | tf_op jit(solution)/shard_map/ppermute | solution.py:47
  132.8 139.1 %all-gather.3.cloned.1.call-start = ((), (), s32[]{:S(2)}) async-start(), calls=%async_computation.2 | async-start | bytes 1966080 | tf_op jit(solution)/shard_map/all_gather | solution.py:1105
  132.8 26.4 %collective-permute-start.22 = (bf16[128,768]{1,0:T(8,128)(2,1)}, bf16[128,768]{1,0:T(8,128)(2,1)S(1)}, u32[]{:S(2)}, u32[]{:S(2)}) collective-permute-start(bf16[128,768]{1,0:T(8,128)(2,1)} %get-tuple-element.209.refs_0_.g_own), channel_id=1, source_target_pairs={{0,1},{1,2},{2,3},{3,0},{4,5},{5,6},{6,7},{7,4},{8,9},{9,10},{10,1... | collective-permute-start | bytes 589832 | tf_op jit(solution)/shard_map/ppermute | solution.py:52
  134.2 26.2 %collective-permute-start.28 = (bf16[128,768]{1,0:T(8,128)(2,1)}, bf16[128,768]{1,0:T(8,128)(2,1)S(1)}, u32[]{:S(2)}, u32[]{:S(2)}) collective-permute-start(bf16[128,768]{1,0:T(8,128)(2,1)} %get-tuple-element.209.refs_0_.g_own), channel_id=1, source_target_pairs={{0,2},{1,3},{2,0},{3,1},{4,6},{5,7},{6,4},{7,5},{8,10},{9,11},{10,... | collective-permute-start | bytes 589832 | tf_op jit(solution)/shard_map/ppermute | solution.py:52
  136.2 25.7 %collective-permute-start.29 = (bf16[128,768]{1,0:T(8,128)(2,1)}, bf16[128,768]{1,0:T(8,128)(2,1)S(1)}, u32[]{:S(2)}, u32[]{:S(2)}) collective-permute-start(bf16[128,768]{1,0:T(8,128)(2,1)} %get-tuple-element.209.refs_0_.g_own), channel_id=1, source_target_pairs={{0,3},{1,0},{2,1},{3,2},{4,7},{5,4},{6,5},{7,6},{8,11},{9,8},{10,9... | collective-permute-start | bytes 589832 | tf_op jit(solution)/shard_map/ppermute | solution.py:52
  139.0 19.9 %collective-permute-start.23 = (bf16[2,2,192,768]{3,2,1,0:T(8,128)(2,1)}, bf16[2,2,192,768]{3,2,1,0:T(8,128)(2,1)S(1)}, u32[]{:S(2)}, u32[]{:S(2)}) collective-permute-start(bf16[2,2,192,768]{3,2,1,0:T(8,128)(2,1)} %copy-done.25), channel_id=1, source_target_pairs={{0,4},{4,0},{8,12},{12,8},{1,5},{5,1},{9,13},{13,9},{2,6},{6,2},{1... | collective-permute-start | bytes 3538952 | tf_op jit(solution)/shard_map/ppermute | solution.py:47
  139.7 40.3 %collective-permute-start.26 = (bf16[2,4,96,768]{3,2,1,0:T(8,128)(2,1)}, bf16[2,4,96,768]{3,2,1,0:T(8,128)(2,1)S(1)}, u32[]{:S(2)}, u32[]{:S(2)}) collective-permute-start(bf16[2,4,96,768]{3,2,1,0:T(8,128)(2,1)} %copy-done.24), channel_id=1, source_target_pairs={{0,8},{4,12},{8,0},{12,4},{1,9},{5,13},{9,1},{13,5},{2,10},{6,14},... | collective-permute-start | bytes 3538952 | tf_op jit(solution)/shard_map/ppermute | solution.py:47
  158.9 5.6 %collective-permute-start.30 = (bf16[512,768]{1,0:T(8,128)(2,1)S(1)}, bf16[512,768]{1,0:T(8,128)(2,1)S(1)}, u32[]{:S(2)}, u32[]{:S(2)}) collective-permute-start(bf16[512,768]{1,0:T(8,128)(2,1)S(1)} %get-tuple-element.233), channel_id=1, source_target_pairs={{0,4},{4,0},{8,12},{12,8},{1,5},{5,1},{9,13},{13,9},{2,6},{6,2},{1... | collective-permute-start | bytes 2359304 | tf_op jit(solution)/shard_map/ppermute | solution.py:47
  159.2 38.4 %collective-permute-start.25 = (bf16[2,4,96,768]{3,2,1,0:T(8,128)(2,1)}, bf16[2,4,96,768]{3,2,1,0:T(8,128)(2,1)}, u32[]{:S(2)}, u32[]{:S(2)}) collective-permute-start(bf16[2,4,96,768]{3,2,1,0:T(8,128)(2,1)} %get-tuple-element.222), channel_id=1, source_target_pairs={{0,8},{4,12},{8,0},{12,4},{1,9},{5,13},{9,1},{13,5},{2,10},{6,14},... | collective-permute-start | bytes 3538952 | tf_op jit(solution)/shard_map/ppermute | solution.py:47
  160.3 20.4 %collective-permute-start.27 = (bf16[2,192,768]{2,1,0:T(8,128)(2,1)S(1)}, bf16[2,192,768]{2,1,0:T(8,128)(2,1)S(1)}, u32[]{:S(2)}, u32[]{:S(2)}) collective-permute-start(bf16[2,192,768]{2,1,0:T(8,128)(2,1)S(1)} %fusion.3), channel_id=1, source_target_pairs={{0,16},{16,0},{1,17},{17,1},{2,18},{18,2},{3,19},{19,3},{4,20},{20... | collective-permute-start | bytes 1769480 | tf_op jit(solution)/shard_map/ppermute | solution.py:204
  165.4 15.4 %collective-permute-start.32 = (bf16[128,768]{1,0:T(8,128)(2,1)S(1)}, bf16[128,768]{1,0:T(8,128)(2,1)S(1)}, u32[]{:S(2)}, u32[]{:S(2)}) collective-permute-start(bf16[128,768]{1,0:T(8,128)(2,1)S(1)} %get-tuple-element.244), channel_id=1, source_target_pairs={{0,3},{1,0},{2,1},{3,2},{4,7},{5,4},{6,5},{7,6},{8,11},{9,8},{10,9... | collective-permute-start | bytes 589832 | tf_op jit(solution)/shard_map/ppermute | solution.py:52
  173.9 15.8 %collective-permute-start.33 = (bf16[128,768]{1,0:T(8,128)(2,1)S(1)}, bf16[128,768]{1,0:T(8,128)(2,1)S(1)}, u32[]{:S(2)}, u32[]{:S(2)}) collective-permute-start(bf16[128,768]{1,0:T(8,128)(2,1)S(1)} %get-tuple-element.248), channel_id=1, source_target_pairs={{0,2},{1,3},{2,0},{3,1},{4,6},{5,7},{6,4},{7,5},{8,10},{9,11},{10,... | collective-permute-start | bytes 589832 | tf_op jit(solution)/shard_map/ppermute | solution.py:52
  180.1 9.6 %collective-permute-start.34 = (bf16[128,768]{1,0:T(8,128)(2,1)S(1)}, bf16[128,768]{1,0:T(8,128)(2,1)S(1)}, u32[]{:S(2)}, u32[]{:S(2)}) collective-permute-start(bf16[128,768]{1,0:T(8,128)(2,1)S(1)} %get-tuple-element.249), channel_id=1, source_target_pairs={{0,1},{1,2},{2,3},{3,0},{4,5},{5,6},{6,7},{7,4},{8,9},{9,10},{10,1... | collective-permute-start | bytes 589832 | tf_op jit(solution)/shard_map/ppermute | solution.py:52
  182.7 13.7 %collective-permute-start.31 = (bf16[4,96,768]{2,1,0:T(8,128)(2,1)}, bf16[4,96,768]{2,1,0:T(8,128)(2,1)}, u32[]{:S(2)}, u32[]{:S(2)}) collective-permute-start(bf16[4,96,768]{2,1,0:T(8,128)(2,1)} %fusion.4), channel_id=1, source_target_pairs={{0,16},{16,0},{1,17},{17,1},{2,18},{18,2},{3,19},{19,3},{4,20},{20... | collective-permute-start | bytes 1769480 | tf_op jit(solution)/shard_map/ppermute | solution.py:204
  183.3 14.3 %collective-permute-start.35 = (bf16[2,2,192,768]{3,2,1,0:T(8,128)(2,1)}, bf16[2,2,192,768]{3,2,1,0:T(8,128)(2,1)}, u32[]{:S(2)}, u32[]{:S(2)}) collective-permute-start(bf16[2,2,192,768]{3,2,1,0:T(8,128)(2,1)} %get-tuple-element.254), channel_id=1, source_target_pairs={{0,4},{4,0},{8,12},{12,8},{1,5},{5,1},{9,13},{13,9},{2,6},{6,2},{1... | collective-permute-start | bytes 3538952 | tf_op jit(solution)/shard_map/ppermute | solution.py:47
  199.5 16.0 %collective-permute-start.36 = (bf16[4,96,768]{2,1,0:T(8,128)(2,1)S(1)}, bf16[4,96,768]{2,1,0:T(8,128)(2,1)S(1)}, u32[]{:S(2)}, u32[]{:S(2)}) collective-permute-start(bf16[4,96,768]{2,1,0:T(8,128)(2,1)S(1)} %fusion.5), channel_id=1, source_target_pairs={{0,16},{16,0},{1,17},{17,1},{2,18},{18,2},{3,19},{19,3},{4,20},{20... | collective-permute-start | bytes 1769480 | tf_op jit(solution)/shard_map/ppermute | solution.py:204
  200.1 15.3 %collective-permute-start.37 = (bf16[192,768]{1,0:T(8,128)(2,1)S(1)}, bf16[192,768]{1,0:T(8,128)(2,1)S(1)}, u32[]{:S(2)}, u32[]{:S(2)}) collective-permute-start(bf16[192,768]{1,0:T(8,128)(2,1)S(1)} %fusion.9), channel_id=1, source_target_pairs={{0,8},{4,12},{8,0},{12,4},{1,9},{5,13},{9,1},{13,5},{2,10},{6,14},... | collective-permute-start | bytes 884744 | tf_op jit(solution)/shard_map/ppermute | solution.py:47
  201.5 8.2 %collective-permute-start.38 = (bf16[96,768]{1,0:T(8,128)(2,1)S(1)}, bf16[96,768]{1,0:T(8,128)(2,1)S(1)}, u32[]{:S(2)}, u32[]{:S(2)}) collective-permute-start(bf16[96,768]{1,0:T(8,128)(2,1)S(1)} %get-tuple-element.260), channel_id=1, source_target_pairs={{0,3},{1,0},{2,1},{3,2},{4,7},{5,4},{6,5},{7,6},{8,11},{9,8},{10,9... | collective-permute-start | bytes 442376 | tf_op jit(solution)/shard_map/ppermute | solution.py:52
  205.0 10.4 %collective-permute-start.39 = (bf16[96,768]{1,0:T(8,128)(2,1)S(1)}, bf16[96,768]{1,0:T(8,128)(2,1)S(1)}, u32[]{:S(2)}, u32[]{:S(2)}) collective-permute-start(bf16[96,768]{1,0:T(8,128)(2,1)S(1)} %get-tuple-element.261), channel_id=1, source_target_pairs={{0,2},{1,3},{2,0},{3,1},{4,6},{5,7},{6,4},{7,5},{8,10},{9,11},{10,... | collective-permute-start | bytes 442376 | tf_op jit(solution)/shard_map/ppermute | solution.py:52
  205.5 9.9 %collective-permute-start.40 = (bf16[96,768]{1,0:T(8,128)(2,1)S(1)}, bf16[96,768]{1,0:T(8,128)(2,1)S(1)}, u32[]{:S(2)}, u32[]{:S(2)}) collective-permute-start(bf16[96,768]{1,0:T(8,128)(2,1)S(1)} %get-tuple-element.262), channel_id=1, source_target_pairs={{0,1},{1,2},{2,3},{3,0},{4,5},{5,6},{6,7},{7,4},{8,9},{9,10},{10,1... | collective-permute-start | bytes 442376 | tf_op jit(solution)/shard_map/ppermute | solution.py:52
  215.7 15.2 %collective-permute-start.41 = (bf16[400,768]{1,0:T(8,128)(2,1)S(1)}, bf16[400,768]{1,0:T(8,128)(2,1)S(1)}, u32[]{:S(2)}, u32[]{:S(2)}) collective-permute-start(bf16[400,768]{1,0:T(8,128)(2,1)S(1)} %pad_maximum_fusion.4), channel_id=1, source_target_pairs={{0,8},{4,12},{8,0},{12,4},{1,9},{5,13},{9,1},{13,5},{2,10},{6,14},... | collective-permute-start | bytes 1843208 | tf_op jit(solution)/shard_map/ppermute | solution.py:47
  216.5 14.4 %collective-permute-start.42 = (bf16[192,768]{1,0:T(8,128)(2,1)S(1)}, bf16[192,768]{1,0:T(8,128)(2,1)S(1)}, u32[]{:S(2)}, u32[]{:S(2)}) collective-permute-start(bf16[192,768]{1,0:T(8,128)(2,1)S(1)} %fusion.8), channel_id=1, source_target_pairs={{0,16},{16,0},{1,17},{17,1},{2,18},{18,2},{3,19},{19,3},{4,20},{20... | collective-permute-start | bytes 884744 | tf_op jit(solution)/shard_map/ppermute | solution.py:204
  217.6 5.2 %collective-permute-start.43 = (bf16[96,768]{1,0:T(8,128)(2,1)S(1)}, bf16[96,768]{1,0:T(8,128)(2,1)S(1)}, u32[]{:S(2)}, u32[]{:S(2)}) collective-permute-start(bf16[96,768]{1,0:T(8,128)(2,1)S(1)} %get-tuple-element.271), channel_id=1, source_target_pairs={{0,3},{1,0},{2,1},{3,2},{4,7},{5,4},{6,5},{7,6},{8,11},{9,8},{10,9... | collective-permute-start | bytes 442376 | tf_op jit(solution)/shard_map/ppermute | solution.py:52
  218.6 12.2 %collective-permute-start.44 = (bf16[96,768]{1,0:T(8,128)(2,1)S(1)}, bf16[96,768]{1,0:T(8,128)(2,1)S(1)}, u32[]{:S(2)}, u32[]{:S(2)}) collective-permute-start(bf16[96,768]{1,0:T(8,128)(2,1)S(1)} %get-tuple-element.272), channel_id=1, source_target_pairs={{0,2},{1,3},{2,0},{3,1},{4,6},{5,7},{6,4},{7,5},{8,10},{9,11},{10,... | collective-permute-start | bytes 442376 | tf_op jit(solution)/shard_map/ppermute | solution.py:52
  219.3 11.5 %collective-permute-start.45 = (bf16[96,768]{1,0:T(8,128)(2,1)S(1)}, bf16[96,768]{1,0:T(8,128)(2,1)S(1)}, u32[]{:S(2)}, u32[]{:S(2)}) collective-permute-start(bf16[96,768]{1,0:T(8,128)(2,1)S(1)} %get-tuple-element.273), channel_id=1, source_target_pairs={{0,1},{1,2},{2,3},{3,0},{4,5},{5,6},{6,7},{7,4},{8,9},{9,10},{10,1... | collective-permute-start | bytes 442376 | tf_op jit(solution)/shard_map/ppermute | solution.py:52
  233.6 15.2 %collective-permute-start.47 = (bf16[2,192,768]{2,1,0:T(8,128)(2,1)}, bf16[2,192,768]{2,1,0:T(8,128)(2,1)}, u32[]{:S(2)}, u32[]{:S(2)}) collective-permute-start(bf16[2,192,768]{2,1,0:T(8,128)(2,1)} %get-tuple-element.283), channel_id=1, source_target_pairs={{0,8},{4,12},{8,0},{12,4},{1,9},{5,13},{9,1},{13,5},{2,10},{6,14},... | collective-permute-start | bytes 1769480 | tf_op jit(solution)/shard_map/ppermute | solution.py:47
  235.9 12.8 %collective-permute-start.46 = (bf16[208,768]{1,0:T(8,128)(2,1)}, bf16[208,768]{1,0:T(8,128)(2,1)}, u32[]{:S(2)}, u32[]{:S(2)}) collective-permute-start(bf16[208,768]{1,0:T(8,128)(2,1)} %pad_maximum_fusion.10), channel_id=1, source_target_pairs={{0,16},{16,0},{1,17},{17,1},{2,18},{18,2},{3,19},{19,3},{4,20},{20... | collective-permute-start | bytes 958472 | tf_op jit(solution)/shard_map/ppermute | solution.py:204
  238.0 8.1 %collective-permute-start.48 = (bf16[96,768]{1,0:T(8,128)(2,1)}, bf16[96,768]{1,0:T(8,128)(2,1)S(1)}, u32[]{:S(2)}, u32[]{:S(2)}) collective-permute-start(bf16[96,768]{1,0:T(8,128)(2,1)} %fusion.17), channel_id=1, source_target_pairs={{0,1},{1,2},{2,3},{3,0},{4,5},{5,6},{6,7},{7,4},{8,9},{9,10},{10,1... | collective-permute-start | bytes 442376 | tf_op jit(solution)/shard_map/ppermute | solution.py:52
  238.1 10.7 %collective-permute-start.49 = (bf16[96,768]{1,0:T(8,128)(2,1)}, bf16[96,768]{1,0:T(8,128)(2,1)S(1)}, u32[]{:S(2)}, u32[]{:S(2)}) collective-permute-start(bf16[96,768]{1,0:T(8,128)(2,1)} %fusion.17), channel_id=1, source_target_pairs={{0,2},{1,3},{2,0},{3,1},{4,6},{5,7},{6,4},{7,5},{8,10},{9,11},{10,... | collective-permute-start | bytes 442376 | tf_op jit(solution)/shard_map/ppermute | solution.py:52
  239.1 9.6 %collective-permute-start.50 = (bf16[96,768]{1,0:T(8,128)(2,1)}, bf16[96,768]{1,0:T(8,128)(2,1)S(1)}, u32[]{:S(2)}, u32[]{:S(2)}) collective-permute-start(bf16[96,768]{1,0:T(8,128)(2,1)} %fusion.17), channel_id=1, source_target_pairs={{0,3},{1,0},{2,1},{3,2},{4,7},{5,4},{6,5},{7,6},{8,11},{9,8},{10,9... | collective-permute-start | bytes 442376 | tf_op jit(solution)/shard_map/ppermute | solution.py:52
  251.6 17.9 %collective-permute-start.52 = (bf16[4,96,768]{2,1,0:T(8,128)(2,1)S(1)}, bf16[4,96,768]{2,1,0:T(8,128)(2,1)S(1)}, u32[]{:S(2)}, u32[]{:S(2)}) collective-permute-start(bf16[4,96,768]{2,1,0:T(8,128)(2,1)S(1)} %pad_maximum_fusion.6.mine_ref), channel_id=1, source_target_pairs={{0,16},{16,0},{1,17},{17,1},{2,18},{18,2},{3,19},{19,3},{4,20},{20... | collective-permute-start | bytes 1769480 | tf_op jit(solution)/shard_map/ppermute | solution.py:204
  252.0 17.5 %collective-permute-start.51 = (bf16[192,768]{1,0:T(8,128)(2,1)S(1)}, bf16[192,768]{1,0:T(8,128)(2,1)S(1)}, u32[]{:S(2)}, u32[]{:S(2)}) collective-permute-start(bf16[192,768]{1,0:T(8,128)(2,1)S(1)} %fusion.7), channel_id=1, source_target_pairs={{0,16},{16,0},{1,17},{17,1},{2,18},{18,2},{3,19},{19,3},{4,20},{20... | collective-permute-start | bytes 884744 | tf_op jit(solution)/shard_map/ppermute | solution.py:204
  253.7 10.7 %collective-permute-start.53 = (bf16[112,768]{1,0:T(8,128)(2,1)S(1)}, bf16[112,768]{1,0:T(8,128)(2,1)S(1)}, u32[]{:S(2)}, u32[]{:S(2)}) collective-permute-start(bf16[112,768]{1,0:T(8,128)(2,1)S(1)} %pad_maximum_fusion.11), channel_id=1, source_target_pairs={{0,1},{1,2},{2,3},{3,0},{4,5},{5,6},{6,7},{7,4},{8,9},{9,10},{10,1... | collective-permute-start | bytes 516104 | tf_op jit(solution)/shard_map/ppermute | solution.py:52
  256.3 13.2 %collective-permute-start.54 = (bf16[112,768]{1,0:T(8,128)(2,1)S(1)}, bf16[112,768]{1,0:T(8,128)(2,1)S(1)}, u32[]{:S(2)}, u32[]{:S(2)}) collective-permute-start(bf16[112,768]{1,0:T(8,128)(2,1)S(1)} %pad_maximum_fusion.11), channel_id=1, source_target_pairs={{0,2},{1,3},{2,0},{3,1},{4,6},{5,7},{6,4},{7,5},{8,10},{9,11},{10,... | collective-permute-start | bytes 516104 | tf_op jit(solution)/shard_map/ppermute | solution.py:52
  259.6 9.9 %collective-permute-start.55 = (bf16[112,768]{1,0:T(8,128)(2,1)S(1)}, bf16[112,768]{1,0:T(8,128)(2,1)S(1)}, u32[]{:S(2)}, u32[]{:S(2)}) collective-permute-start(bf16[112,768]{1,0:T(8,128)(2,1)S(1)} %pad_maximum_fusion.11), channel_id=1, source_target_pairs={{0,3},{1,0},{2,1},{3,2},{4,7},{5,4},{6,5},{7,6},{8,11},{9,8},{10,9... | collective-permute-start | bytes 516104 | tf_op jit(solution)/shard_map/ppermute | solution.py:52
  273.0 15.9 %collective-permute-start.59 = (bf16[4,192,768]{2,1,0:T(8,128)(2,1)S(1)}, bf16[4,192,768]{2,1,0:T(8,128)(2,1)S(1)}, u32[]{:S(2)}, u32[]{:S(2)}) collective-permute-start(bf16[4,192,768]{2,1,0:T(8,128)(2,1)S(1)} %bitcast.122), channel_id=1, source_target_pairs={{0,4},{4,0},{8,12},{12,8},{1,5},{5,1},{9,13},{13,9},{2,6},{6,2},{1... | collective-permute-start | bytes 3538952 | tf_op jit(solution)/shard_map/ppermute | solution.py:47
  273.1 15.7 %collective-permute-start.56 = (bf16[4,96,768]{2,1,0:T(8,128)(2,1)S(1)}, bf16[4,96,768]{2,1,0:T(8,128)(2,1)S(1)}, u32[]{:S(2)}, u32[]{:S(2)}) collective-permute-start(bf16[4,96,768]{2,1,0:T(8,128)(2,1)S(1)} %pad_maximum_fusion.7.mine_ref), channel_id=1, source_target_pairs={{0,16},{16,0},{1,17},{17,1},{2,18},{18,2},{3,19},{19,3},{4,20},{20... | collective-permute-start | bytes 1769480 | tf_op jit(solution)/shard_map/ppermute | solution.py:204
  273.5 15.4 %collective-permute-start.57 = (bf16[2,192,768]{2,1,0:T(8,128)(2,1)S(1)}, bf16[2,192,768]{2,1,0:T(8,128)(2,1)S(1)}, u32[]{:S(2)}, u32[]{:S(2)}) collective-permute-start(bf16[2,192,768]{2,1,0:T(8,128)(2,1)S(1)} %pad_maximum_fusion.8), channel_id=1, source_target_pairs={{0,8},{4,12},{8,0},{12,4},{1,9},{5,13},{9,1},{13,5},{2,10},{6,14},... | collective-permute-start | bytes 1769480 | tf_op jit(solution)/shard_map/ppermute | solution.py:47
  274.2 4.9 %collective-permute-start.58 = (f32[8,768]{1,0:T(8,128)S(1)}, f32[8,768]{1,0:T(8,128)S(1)}, u32[]{:S(2)}, u32[]{:S(2)}) collective-permute-start(f32[8,768]{1,0:T(8,128)S(1)} %copy-done.75), channel_id=1, source_target_pairs={{0,4},{4,0},{8,12},{12,8},{1,5},{5,1},{9,13},{13,9},{2,6},{6,2},{1... | collective-permute-start | bytes 73736 | tf_op jit(solution)/shard_map/ppermute | solution.py:47
  292.8 2.9 collective-permute-start.60
  (77 other events, 538.1 us)
Sparse Core Ops, SparseCore 0:
  132.9 34.0 reduce-scatter.1
  238.1 17.0 all-gather.2

commit v2 on v1

--- a/solution.py
+++ b/solution.py
@@ -1054,7 +1054,7 @@
     stream1, act = norm(spot, tok, gains, 1, [*terms, b_own, b_got])
 
     xs1 = gather_list(act)
-    slope1, hidden1, own1, out_parts = ff(spot, xs1, w_in, w_mlp, 1, True)
+    slope1, hidden1, own1, out_parts = ff(spot, xs1, w_in, w_mlp, 1)
     other1 = turn_low(own1)
     cot_tied, unused = tie(cot, own1)
     gs1 = gather_list(cot_tied)
@@ -1098,11 +1098,8 @@
     half_f1 = sum_of(keep_f1[0], [got_f1[0], got_x1])
     delta0, low0, gain0 = norm_back_call(spot, cot, gains, 0, tok, back0, delta1)
 
-    last = lax.psum_scatter(out_parts, "wide", scatter_dimension=0, tiled=False)
-    b_got1, last, stream1, low0 = tie(b_got1, last, stream1, low0)
-    half_w1, half_f1, last = tie(half_w1, half_f1, last)
-    delta_out = (stream1 - tok.astype(F32) + sum_of(b_own1, [b_got1, last])).astype(BF)
-    ends = lax.all_gather(jnp.concatenate([delta_out, low0], axis=1), "head", axis=0, tiled=False)
+    low0, *sent = tie(low0, *out_parts[1:])
+    last = [f(p) for p, f in zip(sent, shifts(-1))]
 
     gain = jnp.concatenate([gain0, gain1, jnp.zeros((6, width), F32)])
 
@@ -1114,7 +1111,9 @@
         return got[-16:-8].astype(F32) + got[-8:].astype(F32)
 
     got_f0 = turn_low(send_f0)
-    got_w0, half_w1, half_f1, got_f0 = tie(got_w0, half_w1, half_f1, got_f0)
+    got_w0, half_w1, half_f1, got_f0, *last = tie(got_w0, half_w1, half_f1, got_f0, *last)
+    delta_out = (stream1 - tok.astype(F32) + sum_of(b_own1, [b_got1, out_parts[0], *last])).astype(BF)
+    ends = lax.all_gather(jnp.concatenate([delta_out, low0], axis=1), "head", axis=0, tiled=False)
     sum_w0 = own_w0 + got_w0.astype(F32)
     got_w0, got_f1, *got_b1 = together(
         (sum_w0[1].astype(BF), turn_batch),
@@ -1151,11 +1150,9 @@
     rows_w = half_w0.shape[1]
     mine_w0 = jnp.stack([g[:rows_w] for g in (block_w0, *got_b0)])
     mine_w0, ends = tie(mine_w0, ends)
-    got_w0, got_f0, got_g, got_f1 = together(
-        (mine_w0, turn_batch), (pair_f0, turn_high), (gain, turn_low), (full_f1, turn_low)
-    )
+    got_w0, got_f0, got_f1 = together((mine_w0, turn_batch), (pair_f0, turn_high), (full_f1, turn_low))
     full_f0 = jnp.concatenate([pair_f0, got_f0])
-    got_f0 = turn_low(full_f0)
+    got_f0, got_g = turn_low(full_f0), turn_low(gain)
     d_gains = (gain + got_g)[:2]
     late = ff_finish(spot, 1, full_f1, got_f1, X_BIT)
     d_in, d_mlp = ff_finish(spot, 0, full_f0, got_f0, Y_BIT, late)

time: 310 us -> 309 us (level)
  waiting for transfers between devices: 77.5 us -> 107 us
  local copies, waits for them, and re-layouts: 27.4 us -> 15.7 us
  starting transfers between devices: 74.2 us -> 66.7 us
  Pallas kernels: 86.4 us -> 80.4 us
  other arithmetic: 25.1 us -> 20.6 us
    ppermute x33 -> x36, waiting for transfers between devices: 57 us -> 75.4 us  [shift(): lax.ppermute(x, 'wide', [(i, (i + step) % size) for i in range(size)])]
    unnamed x156 -> x92, local copies, waits for them, and re-layouts: 14.9 us -> 4.04 us
    ppermute x33 -> x36, starting transfers between devices: 56.7 us -> 47.4 us  [shift(): lax.ppermute(x, 'wide', [(i, (i + step) % size) for i in range(size)])]
    ppermute x20, waiting for transfers between devices: 7.44 us -> 15.9 us  [swap(): return lax.ppermute(x, 'head', [(i, i ^ bit) for i in range(size)])]
    pallas_call x21, Pallas kernels: 86.4 us -> 80.4 us  [call(): pl.pallas_call(kernel, grid_spec=pltpu.PrefetchScalarGridSpec(num_scalar_...]
  transfers between devices with their start and end apart: 63 -> 65, of which waited for: 16 -> 22; matrix products, arithmetic and copies ran while one was open for 10% -> 9% of each run, Pallas kernels for 25% -> 23%
where the time goes in v2:
time: 309 us; the launch traced here: 305 us
  waiting for transfers between devices  107 us (35%)
  Pallas kernels  80.4 us (26%)
  starting transfers between devices  66.7 us (22%)
  other arithmetic  20.6 us (7%)
  local copies, waits for them, and re-layouts  15.7 us (5%)
  between operations  15 us (5%)
    pallas_call x21, Pallas kernels, call(): pl.pallas_call(kernel, grid_spec=pltpu.PrefetchScalarGridSpec(num_scalar_...  80.4 us
    ppermute x36, waiting for transfers between devices, shift(): lax.ppermute(x, 'wide', [(i, (i + step) % size) for i in range(size)])  75.4 us
    ppermute x36, starting transfers between devices, shift(): lax.ppermute(x, 'wide', [(i, (i + step) % size) for i in range(size)])  47.4 us
    ppermute x20, waiting for transfers between devices, swap(): return lax.ppermute(x, 'head', [(i, i ^ bit) for i in range(size)])  15.9 us
    ppermute x8, waiting for transfers between devices, turn_batch(): return lax.ppermute(x, 'batch', [(i, size - 1 - i) for i in range(size)])  15.5 us
    ppermute x20, starting transfers between devices, swap(): return lax.ppermute(x, 'head', [(i, i ^ bit) for i in range(size)])  10.6 us
    ppermute x8, starting transfers between devices, turn_batch(): return lax.ppermute(x, 'batch', [(i, size - 1 - i) for i in range(size)])  8.6 us
  transfers between devices with their start and end apart: 65, of which 22 were waited for; matrix products, arithmetic and copies ran while one was open for 9% of the time, Pallas kernels for 23%

profile of v2, /device:TPU:0, one launch (start us, length us, event | category | flops | bytes accessed | tf_op | source)
XLA Modules:
  0.0 305.2 jit_solution(5340504821938213323)
XLA Ops:
  9.0 1.4 shard_map.135.refs_0_
  10.4 3.0 collective-permute-start
  13.4 2.6 collective-permute-start.1
  20.3 1.5 collective-permute-start.7
  23.8 2.9 fusion.34
  27.5 1.5 copy.36
  29.0 1.4 copy.35
  30.4 1.4 pad_maximum_fusion
  31.9 3.9 %shard_map.136 = (f32[512,768]{1,0:T(8,128)S(1)}, bf16[512,768]{1,0:T(8,128)(2,1)S(1)}, bf16[512,768]{1,0:T(8,128)(2,1)S(1)}, f32[128,768]{1,0:T(8,128)S(1)}, bf...) custom-call(s32[5]{0:T(128)S(1)} %stack.80.place_ref.spot_ref, ...), custom_call_target="tpu_custom_call" | custom-call | flops 100000000 | tf_op jit(solution)/shard_map/pallas_call | solution.py:480
  36.7 3.1 %collective-permute-start.3 = (bf16[128,768]{1,0:T(8,128)(2,1)S(1)}, bf16[128,768]{1,0:T(8,128)(2,1)S(1)}, u32[]{:S(2)}, u32[]{:S(2)}) collective-permute-start(bf16[128,768]{1,0:T(8,128)(2,1)S(1)} %get-tuple-element.170), channel_id=1, source_target_pairs={{0,3},{1,0},{2,1},{3,2},{4,7},{5,4},{6,5},{7,6},{8,11},{9,8},{10,9... | collective-permute-start | bytes 589832 | tf_op jit(solution)/shard_map/ppermute | solution.py:52
  40.4 7.1 %collective-permute-done.7.refs_4_.refs_5_ = bf16[4,192,768]{2,1,0:T(8,128)(2,1)} collective-permute-done((bf16[4,192,768]{2,1,0:T(8,128)(2,1)}, bf16[4,192,768]{2,1,0:T(8,128)(2,1)}, u32[]{:S(2)}, u32[]{:S(2)}) %collective-permute-start.7) | collective-permute-done | bytes 1179680 | tf_op jit(solution)/shard_map/ppermute | solution.py:47
  47.5 10.3 %shard_map.137 = (bf16[256,384]{1,0:T(8,128)(2,1)S(1)}, bf16[1024,384]{1,0:T(8,128)(2,1)S(1)}, bf16[1024,384]{1,0:T(8,128)(2,1)S(1)}, bf16[256,384]{1,0:T(8,128)...) custom-call(bf16[512,768]{1,0:T(8,128)(2,1)S(1)} %get-tuple-element.173.refs_0_.own_act., ...), custom_call_target="tpu_custom_call" | custom-call | flops 20000000000 | tf_op jit(solution)/shard_map/pallas_call | solution.py:480
  57.9 1.6 collective-permute-start.16
  60.9 2.6 collective-permute-start.11
  63.5 10.0 %collective-permute-done.10.refs_2_ = bf16[128,768]{1,0:T(8,128)(2,1)S(1)} collective-permute-done((bf16[128,768]{1,0:T(8,128)(2,1)S(1)}, bf16[128,768]{1,0:T(8,128)(2,1)S(1)}, u32[]{:S(2)}, u32[]{:S(2)}) %collective-permute-start.10) | collective-permute-done | bytes 196640 | tf_op jit(solution)/shard_map/ppermute | solution.py:52
  73.6 3.5 %collective-permute-done.9.refs_1_ = bf16[128,768]{1,0:T(8,128)(2,1)S(1)} collective-permute-done((bf16[128,768]{1,0:T(8,128)(2,1)S(1)}, bf16[128,768]{1,0:T(8,128)(2,1)S(1)}, u32[]{:S(2)}, u32[]{:S(2)}) %collective-permute-start.9) | collective-permute-done | bytes 196640 | tf_op jit(solution)/shard_map/ppermute | solution.py:52
  77.1 2.7 shard_map.139
  79.9 4.6 %collective-permute-start.12 = (bf16[128,768]{1,0:T(8,128)(2,1)S(1)}, bf16[128,768]{1,0:T(8,128)(2,1)S(1)}, u32[]{:S(2)}, u32[]{:S(2)}) collective-permute-start(bf16[128,768]{1,0:T(8,128)(2,1)S(1)} %copy-done.4), channel_id=1, source_target_pairs={{0,1},{1,2},{2,3},{3,0},{4,5},{5,6},{6,7},{7,4},{8,9},{9,10},{10,1... | collective-permute-start | bytes 589832 | tf_op jit(solution)/shard_map/ppermute | solution.py:52
  84.5 2.5 collective-permute-start.14
  88.0 17.3 %shard_map.141 = (bf16[256,384]{1,0:T(8,128)(2,1)S(1)}, bf16[1024,384]{1,0:T(8,128)(2,1)S(1)}, bf16[1024,384]{1,0:T(8,128)(2,1)S(1)}, bf16[256,384]{1,0:T(8,128)...) custom-call(bf16[512,768]{1,0:T(8,128)(2,1)S(1)} %get-tuple-element., ...), custom_call_target="tpu_custom_call" | custom-call | flops 20000000000 | tf_op jit(solution)/shard_map/pallas_call | solution.py:480
  106.3 1.4 collective-permute-done.17.got_ref
  108.5 2.0 collective-permute-start.18
  111.3 3.8 %shard_map.143 = (f32[2,2,192,768]{3,2,1,0:T(8,128)S(1)}, bf16[2,2,192,768]{3,2,1,0:T(8,128)(2,1)S(1)}) custom-call(s32[5]{0:T(128)S(1)} %stack.80.place_ref.spot_ref, bf16[512,768]{1,0:T(8,128)(2,1)} %copy-done.8, bf16[512,768]{1,0:T(8,128)(2,1)} %copy-done.14, bf16[512,768]{1,0:T(8,128)(2,1)} %copy-done.13, bf16[512,768]{1,0:T(8,128)(2,1)} %copy-done.10), custom_call_target="tpu_custom_call" | custom-call | flops 5000000000 | tf_op jit(solution)/shard_map/pallas_call | solution.py:480
  115.1 3.5 %shard_map.144 = (f32[2,4,96,768]{3,2,1,0:T(8,128)S(1)}, bf16[2,4,96,768]{3,2,1,0:T(8,128)(2,1)S(1)}) custom-call(s32[5]{0:T(128)S(1)} %stack.80.place_ref.spot_ref, bf16[512,768]{1,0:T(8,128)(2,1)S(1)} %copy-done.9, bf16[512,768]{1,0:T(8,128)(2,1)S(1)} %collective-permute-done.15.refs_1_.other_act, bf16[128,768]{1,0:T(8,128)(2,1)S(1)} %copy-done.4, ...), custom_call_target="tpu_custom_call" | custom-call | flops 5000000000 | tf_op jit(solution)/shard_map/pallas_call | solution.py:480
  118.7 8.9 %collective-permute-done.20.refs_2_ = bf16[128,768]{1,0:T(8,128)(2,1)S(1)} collective-permute-done((bf16[128,768]{1,0:T(8,128)(2,1)S(1)}, bf16[128,768]{1,0:T(8,128)(2,1)S(1)}, u32[]{:S(2)}, u32[]{:S(2)}) %collective-permute-start.20) | collective-permute-done | bytes 196640 | tf_op jit(solution)/shard_map/ppermute | solution.py:52
  129.8 2.0 collective-permute-start.28
  131.7 2.8 collective-permute-start.29
  135.9 11.2 %shard_map.146 = (bf16[256,384]{1,0:T(8,128)(2,1)S(1)}, bf16[1024,384]{1,0:T(8,128)(2,1)S(1)}, bf16[1024,384]{1,0:T(8,128)(2,1)S(1)}, f32[512,768]{1,0:T(8,128)S(1)}, bf16[512,768]{1,0:T(8,128)(2,1)S(1)}) custom-call(bf16[128,768]{1,0:T(8,128)(2,1)S(1)} %get-tuple-element.210.refs_0_.g_own, bf16[128,768]{1,0:T(8,128)(2,1)S(1)} %collective-permute-done.24.refs_1_.g_other, ...), custom_call_target="tpu_custom_call" | custom-call | flops 20000000000 | tf_op jit(solution)/shard_map/pallas_call | solution.py:480
  147.1 3.6 %shard_map.147 = (f32[2,4,96,768]{3,2,1,0:T(8,128)S(1)}, bf16[2,4,96,768]{3,2,1,0:T(8,128)(2,1)S(1)}) custom-call(s32[5]{0:T(128)S(1)} %stack.80.place_ref.spot_ref, bf16[512,768]{1,0:T(8,128)(2,1)S(1)} %get-tuple-element.173.refs_0_.own_act.x_ref, bf16[512,768]{1,0:T(8,128)(2,1)S(1)} %collective-permute-done.6.refs_1_.other_act, ...), custom_call_target="tpu_custom_call" | custom-call | flops 5000000000 | tf_op jit(solution)/shard_map/pallas_call | solution.py:480
  151.9 1.6 collective-permute-start.27
  156.0 3.8 %shard_map.150 = (f32[2,2,192,768]{3,2,1,0:T(8,128)S(1)}, bf16[2,2,192,768]{3,2,1,0:T(8,128)(2,1)S(1)}) custom-call(s32[5]{0:T(128)S(1)} %stack.80.place_ref.spot_ref, bf16[512,768]{1,0:T(8,128)(2,1)} %copy-done.7, bf16[512,768]{1,0:T(8,128)(2,1)} %copy-done.16, bf16[512,768]{1,0:T(8,128)(2,1)} %copy-done.15, bf16[512,768]{1,0:T(8,128)(2,1)} %copy-done.6), custom_call_target="tpu_custom_call" | custom-call | flops 5000000000 | tf_op jit(solution)/shard_map/pallas_call | solution.py:480
  159.9 3.5 %collective-permute-done.26 = bf16[2,4,96,768]{3,2,1,0:T(8,128)(2,1)S(1)} collective-permute-done((bf16[2,4,96,768]{3,2,1,0:T(8,128)(2,1)S(1)}, bf16[2,4,96,768]{3,2,1,0:T(8,128)(2,1)S(1)}, u32[]{:S(2)}, u32[]{:S(2)}) %collective-permute-start.26) | collective-permute-done | bytes 1179680 | tf_op jit(solution)/shard_map/ppermute | solution.py:47
  163.4 3.8 %collective-permute-done.27 = bf16[2,192,768]{2,1,0:T(8,128)(2,1)S(1)} collective-permute-done((bf16[2,192,768]{2,1,0:T(8,128)(2,1)S(1)}, bf16[2,192,768]{2,1,0:T(8,128)(2,1)S(1)}, u32[]{:S(2)}, u32[]{:S(2)}) %collective-permute-start.27) | collective-permute-done | bytes 589856 | tf_op jit(solution)/shard_map/ppermute | solution.py:204
  167.5 1.6 collective-permute-start.31
  169.1 4.1 %collective-permute-done.34.refs_3_ = bf16[128,768]{1,0:T(8,128)(2,1)S(1)} collective-permute-done((bf16[128,768]{1,0:T(8,128)(2,1)S(1)}, bf16[128,768]{1,0:T(8,128)(2,1)S(1)}, u32[]{:S(2)}, u32[]{:S(2)}) %collective-permute-start.34) | collective-permute-done | bytes 196640 | tf_op jit(solution)/shard_map/ppermute | solution.py:52
  173.2 1.7 shard_map.151
  175.6 1.9 collective-permute-start.37
  177.8 4.2 %collective-permute-done.31 = bf16[4,96,768]{2,1,0:T(8,128)(2,1)S(1)} collective-permute-done((bf16[4,96,768]{2,1,0:T(8,128)(2,1)S(1)}, bf16[4,96,768]{2,1,0:T(8,128)(2,1)S(1)}, u32[]{:S(2)}, u32[]{:S(2)}) %collective-permute-start.31) | collective-permute-done | bytes 589856 | tf_op jit(solution)/shard_map/ppermute | solution.py:204
  182.1 13.1 %collective-permute-done.37 = bf16[128,768]{1,0:T(8,128)(2,1)S(1)} collective-permute-done((bf16[128,768]{1,0:T(8,128)(2,1)S(1)}, bf16[128,768]{1,0:T(8,128)(2,1)S(1)}, u32[]{:S(2)}, u32[]{:S(2)}) %collective-permute-start.37) | collective-permute-done | bytes 196640 | tf_op jit(solution)/shard_map/ppermute | solution.py:52
  198.0 2.0 collective-permute-start.43
  200.3 3.2 %collective-permute-done.41 = bf16[96,768]{1,0:T(8,128)(2,1)S(1)} collective-permute-done((bf16[96,768]{1,0:T(8,128)(2,1)S(1)}, bf16[96,768]{1,0:T(8,128)(2,1)S(1)}, u32[]{:S(2)}, u32[]{:S(2)}) %collective-permute-start.41) | collective-permute-done | bytes 147488 | tf_op jit(solution)/shard_map/ppermute | solution.py:52
  203.5 7.4 %collective-permute-done.42 = bf16[96,768]{1,0:T(8,128)(2,1)S(1)} collective-permute-done((bf16[96,768]{1,0:T(8,128)(2,1)S(1)}, bf16[96,768]{1,0:T(8,128)(2,1)S(1)}, u32[]{:S(2)}, u32[]{:S(2)}) %collective-permute-start.42) | collective-permute-done | bytes 147488 | tf_op jit(solution)/shard_map/ppermute | solution.py:52
  214.4 2.2 collective-permute-start.47
  216.6 2.0 collective-permute-start.48
  219.2 10.4 %collective-permute-done.47 = bf16[96,768]{1,0:T(8,128)(2,1)S(1)} collective-permute-done((bf16[96,768]{1,0:T(8,128)(2,1)S(1)}, bf16[96,768]{1,0:T(8,128)(2,1)S(1)}, u32[]{:S(2)}, u32[]{:S(2)}) %collective-permute-start.47) | collective-permute-done | bytes 147488 | tf_op jit(solution)/shard_map/ppermute | solution.py:52
  237.0 2.9 collective-permute-start.53
  241.0 3.7 %collective-permute-done.51 = bf16[96,768]{1,0:T(8,128)(2,1)S(1)} collective-permute-done((bf16[96,768]{1,0:T(8,128)(2,1)S(1)}, bf16[96,768]{1,0:T(8,128)(2,1)S(1)}, u32[]{:S(2)}, u32[]{:S(2)}) %collective-permute-start.51) | collective-permute-done | bytes 147488 | tf_op jit(solution)/shard_map/ppermute | solution.py:52
  244.7 3.7 %collective-permute-done.52 = bf16[96,768]{1,0:T(8,128)(2,1)S(1)} collective-permute-done((bf16[96,768]{1,0:T(8,128)(2,1)S(1)}, bf16[96,768]{1,0:T(8,128)(2,1)S(1)}, u32[]{:S(2)}, u32[]{:S(2)}) %collective-permute-start.52) | collective-permute-done | bytes 147488 | tf_op jit(solution)/shard_map/ppermute | solution.py:52
  248.4 2.7 collective-permute-done.50
  253.4 2.0 collective-permute-start.54
  255.5 1.4 collective-permute-start.57
  256.9 2.3 collective-permute-start.58
  260.5 2.5 collective-permute-done.56
  263.0 4.4 %collective-permute-done.57 = bf16[112,768]{1,0:T(8,128)(2,1)S(1)} collective-permute-done((bf16[112,768]{1,0:T(8,128)(2,1)S(1)}, bf16[112,768]{1,0:T(8,128)(2,1)S(1)}, u32[]{:S(2)}, u32[]{:S(2)}) %collective-permute-start.57) | collective-permute-done | bytes 172064 | tf_op jit(solution)/shard_map/ppermute | solution.py:52
  267.4 1.7 collective-permute-done.54
  269.1 1.6 add_add_fusion
  272.5 1.5 collective-permute-start.59
  275.8 2.8 shard_map.152
  278.6 2.0 convert_add_fusion.3
  280.6 1.4 slice_add_fusion
  282.0 5.8 %collective-permute-done.59.got_ref = bf16[4,96,768]{2,1,0:T(8,128)(2,1)S(1)} collective-permute-done((bf16[4,96,768]{2,1,0:T(8,128)(2,1)S(1)}, bf16[4,96,768]{2,1,0:T(8,128)(2,1)S(1)}, u32[]{:S(2)}, u32[]{:S(2)}) %collective-permute-start.59) | collective-permute-done | bytes 589856 | tf_op jit(solution)/shard_map/ppermute | solution.py:204
  289.0 3.2 %shard_map.154 = (f32[2,768,768]{2,1,0:T(8,128)}, f32[2,768,768]{2,1,0:T(8,128)}) custom-call(s32[5]{0:T(128)S(1)} %stack.80.place_ref.spot_ref, bf16[4,192,768]{2,1,0:T(8,128)(2,1)S(1)} %bitcast.122, bf16[4,192,768]{2,1,0:T(8,128)(2,1)S(1)} %collective-permute-done.61.got_ref), custom_call_target="tpu_custom_call" | custom-call | flops 20000000000 | tf_op jit(solution)/shard_map/pallas_call | solution.py:480
  292.4 2.8 shard_map.153
  295.2 3.2 %shard_map.155 = (f32[2,768,768]{2,1,0:T(8,128)}, f32[2,768,768]{2,1,0:T(8,128)}) custom-call(s32[5]{0:T(128)S(1)} %stack.80.place_ref.spot_ref, bf16[4,192,768]{2,1,0:T(8,128)(2,1)S(1)} %pad_maximum_fusion.3.mine_ref, bf16[4,192,768]{2,1,0:T(8,128)(2,1)S(1)} %collective-permute-done.62.got_ref, ...), custom_call_target="tpu_custom_call", output_to_operand_aliasing={{0}: (3, {}), {1}: (4, {})} | custom-call | flops 20000000000 | tf_op jit(solution)/shard_map/pallas_call | solution.py:480
  (250 shorter events, 48.1 us)
Async XLA Ops:
  7.2 263.6 %all-gather.3.cloned.1.call-start = ((), (), s32[]{:S(2)}) async-start(), calls=%async_computation | async-start | bytes 1966080 | tf_op jit(solution)/shard_map/all_gather | solution.py:1116
  10.4 21.4 %collective-permute-start = (bf16[128,768]{1,0:T(8,128)(2,1)}, bf16[128,768]{1,0:T(8,128)(2,1)}, u32[]{:S(2)}, u32[]{:S(2)}) collective-permute-start(bf16[128,768]{1,0:T(8,128)(2,1)} %shard_map.135.refs_0_), channel_id=1, source_target_pairs={{0,1},{1,2},{2,3},{3,0},{4,5},{5,6},{6,7},{7,4},{8,9},{9,10},{10,1... | collective-permute-start | bytes 589832 | tf_op jit(solution)/shard_map/ppermute | solution.py:52
  13.4 18.4 %collective-permute-start.1 = (bf16[128,768]{1,0:T(8,128)(2,1)}, bf16[128,768]{1,0:T(8,128)(2,1)}, u32[]{:S(2)}, u32[]{:S(2)}) collective-permute-start(bf16[128,768]{1,0:T(8,128)(2,1)} %shard_map.135.refs_0_), channel_id=1, source_target_pairs={{0,2},{1,3},{2,0},{3,1},{4,6},{5,7},{6,4},{7,5},{8,10},{9,11},{10,... | collective-permute-start | bytes 589832 | tf_op jit(solution)/shard_map/ppermute | solution.py:52
  16.0 15.8 %collective-permute-start.2 = (bf16[128,768]{1,0:T(8,128)(2,1)}, bf16[128,768]{1,0:T(8,128)(2,1)}, u32[]{:S(2)}, u32[]{:S(2)}) collective-permute-start(bf16[128,768]{1,0:T(8,128)(2,1)} %shard_map.135.refs_0_), channel_id=1, source_target_pairs={{0,3},{1,0},{2,1},{3,2},{4,7},{5,4},{6,5},{7,6},{8,11},{9,8},{10,9... | collective-permute-start | bytes 589832 | tf_op jit(solution)/shard_map/ppermute | solution.py:52
  20.3 27.2 %collective-permute-start.7 = (bf16[4,192,768]{2,1,0:T(8,128)(2,1)}, bf16[4,192,768]{2,1,0:T(8,128)(2,1)}, u32[]{:S(2)}, u32[]{:S(2)}) collective-permute-start(bf16[4,192,768]{2,1,0:T(8,128)(2,1)} %pad_maximum_fusion.1), channel_id=1, source_target_pairs={{0,8},{4,12},{8,0},{12,4},{1,9},{5,13},{9,1},{13,5},{2,10},{6,14},... | collective-permute-start | bytes 3538952 | tf_op jit(solution)/shard_map/ppermute | solution.py:47
  36.7 10.8 %collective-permute-start.6 = (bf16[512,768]{1,0:T(8,128)(2,1)S(1)}, bf16[512,768]{1,0:T(8,128)(2,1)S(1)}, u32[]{:S(2)}, u32[]{:S(2)}) collective-permute-start(bf16[512,768]{1,0:T(8,128)(2,1)S(1)} %get-tuple-element.173.refs_0_.own_act.x_ref), channel_id=1, source_target_pairs={{0,4},{4,0},{8,12},{12,8},{1,5},{5,1},{9,13},{13,9},{2,6},{6,2},{1... | collective-permute-start | bytes 2359304 | tf_op jit(solution)/shard_map/ppermute | solution.py:47
  36.7 22.8 %collective-permute-start.3 = (bf16[128,768]{1,0:T(8,128)(2,1)S(1)}, bf16[128,768]{1,0:T(8,128)(2,1)S(1)}, u32[]{:S(2)}, u32[]{:S(2)}) collective-permute-start(bf16[128,768]{1,0:T(8,128)(2,1)S(1)} %get-tuple-element.170), channel_id=1, source_target_pairs={{0,3},{1,0},{2,1},{3,2},{4,7},{5,4},{6,5},{7,6},{8,11},{9,8},{10,9... | collective-permute-start | bytes 589832 | tf_op jit(solution)/shard_map/ppermute | solution.py:52
  39.7 19.8 %collective-permute-start.4 = (bf16[128,768]{1,0:T(8,128)(2,1)S(1)}, bf16[128,768]{1,0:T(8,128)(2,1)S(1)}, u32[]{:S(2)}, u32[]{:S(2)}) collective-permute-start(bf16[128,768]{1,0:T(8,128)(2,1)S(1)} %get-tuple-element.171), channel_id=1, source_target_pairs={{0,2},{1,3},{2,0},{3,1},{4,6},{5,7},{6,4},{7,5},{8,10},{9,11},{10,... | collective-permute-start | bytes 589832 | tf_op jit(solution)/shard_map/ppermute | solution.py:52
  40.2 19.3 %collective-permute-start.5 = (bf16[128,768]{1,0:T(8,128)(2,1)S(1)}, bf16[128,768]{1,0:T(8,128)(2,1)S(1)}, u32[]{:S(2)}, u32[]{:S(2)}) collective-permute-start(bf16[128,768]{1,0:T(8,128)(2,1)S(1)} %get-tuple-element.172), channel_id=1, source_target_pairs={{0,1},{1,2},{2,3},{3,0},{4,5},{5,6},{6,7},{7,4},{8,9},{9,10},{10,1... | collective-permute-start | bytes 589832 | tf_op jit(solution)/shard_map/ppermute | solution.py:52
  57.9 29.0 %collective-permute-start.16 = (bf16[4,192,768]{2,1,0:T(8,128)(2,1)S(1)}, bf16[4,192,768]{2,1,0:T(8,128)(2,1)S(1)}, u32[]{:S(2)}, u32[]{:S(2)}) collective-permute-start(bf16[4,192,768]{2,1,0:T(8,128)(2,1)S(1)} %pad_maximum_fusion), channel_id=1, source_target_pairs={{0,8},{4,12},{8,0},{12,4},{1,9},{5,13},{9,1},{13,5},{2,10},{6,14},... | collective-permute-start | bytes 3538952 | tf_op jit(solution)/shard_map/ppermute | solution.py:47
  60.4 13.1 %collective-permute-start.10 = (bf16[128,768]{1,0:T(8,128)(2,1)S(1)}, bf16[128,768]{1,0:T(8,128)(2,1)S(1)}, u32[]{:S(2)}, u32[]{:S(2)}) collective-permute-start(bf16[128,768]{1,0:T(8,128)(2,1)S(1)} %get-tuple-element.181.refs_0_), channel_id=1, source_target_pairs={{0,2},{1,3},{2,0},{3,1},{4,6},{5,7},{6,4},{7,5},{8,10},{9,11},{10,... | collective-permute-start | bytes 589832 | tf_op jit(solution)/shard_map/ppermute | solution.py:52
  60.9 12.6 %collective-permute-start.11 = (bf16[128,768]{1,0:T(8,128)(2,1)S(1)}, bf16[128,768]{1,0:T(8,128)(2,1)S(1)}, u32[]{:S(2)}, u32[]{:S(2)}) collective-permute-start(bf16[128,768]{1,0:T(8,128)(2,1)S(1)} %get-tuple-element.181.refs_0_), channel_id=1, source_target_pairs={{0,3},{1,0},{2,1},{3,2},{4,7},{5,4},{6,5},{7,6},{8,11},{9,8},{10,9... | collective-permute-start | bytes 589832 | tf_op jit(solution)/shard_map/ppermute | solution.py:52
  63.5 13.5 %collective-permute-start.9 = (bf16[128,768]{1,0:T(8,128)(2,1)S(1)}, bf16[128,768]{1,0:T(8,128)(2,1)S(1)}, u32[]{:S(2)}, u32[]{:S(2)}) collective-permute-start(bf16[128,768]{1,0:T(8,128)(2,1)S(1)} %get-tuple-element.181.refs_0_), channel_id=1, source_target_pairs={{0,1},{1,2},{2,3},{3,0},{4,5},{5,6},{6,7},{7,4},{8,9},{9,10},{10,1... | collective-permute-start | bytes 589832 | tf_op jit(solution)/shard_map/ppermute | solution.py:52
  79.8 7.1 %collective-permute-start.15 = (bf16[512,768]{1,0:T(8,128)(2,1)S(1)}, bf16[512,768]{1,0:T(8,128)(2,1)S(1)}, u32[]{:S(2)}, u32[]{:S(2)}) collective-permute-start(bf16[512,768]{1,0:T(8,128)(2,1)S(1)} %get-tuple-element.182.refs_0_.x_ref.own_act), channel_id=1, source_target_pairs={{0,4},{4,0},{8,12},{12,8},{1,5},{5,1},{9,13},{13,9},{2,6},{6,2},{1... | collective-permute-start | bytes 2359304 | tf_op jit(solution)/shard_map/ppermute | solution.py:47
  79.9 25.5 %collective-permute-start.12 = (bf16[128,768]{1,0:T(8,128)(2,1)S(1)}, bf16[128,768]{1,0:T(8,128)(2,1)S(1)}, u32[]{:S(2)}, u32[]{:S(2)}) collective-permute-start(bf16[128,768]{1,0:T(8,128)(2,1)S(1)} %copy-done.4), channel_id=1, source_target_pairs={{0,1},{1,2},{2,3},{3,0},{4,5},{5,6},{6,7},{7,4},{8,9},{9,10},{10,1... | collective-permute-start | bytes 589832 | tf_op jit(solution)/shard_map/ppermute | solution.py:52
  84.5 20.9 %collective-permute-start.13 = (bf16[128,768]{1,0:T(8,128)(2,1)S(1)}, bf16[128,768]{1,0:T(8,128)(2,1)S(1)}, u32[]{:S(2)}, u32[]{:S(2)}) collective-permute-start(bf16[128,768]{1,0:T(8,128)(2,1)S(1)} %copy-done.4), channel_id=1, source_target_pairs={{0,2},{1,3},{2,0},{3,1},{4,6},{5,7},{6,4},{7,5},{8,10},{9,11},{10,... | collective-permute-start | bytes 589832 | tf_op jit(solution)/shard_map/ppermute | solution.py:52
  84.5 20.9 %collective-permute-start.14 = (bf16[128,768]{1,0:T(8,128)(2,1)S(1)}, bf16[128,768]{1,0:T(8,128)(2,1)S(1)}, u32[]{:S(2)}, u32[]{:S(2)}) collective-permute-start(bf16[128,768]{1,0:T(8,128)(2,1)S(1)} %copy-done.4), channel_id=1, source_target_pairs={{0,3},{1,0},{2,1},{3,2},{4,7},{5,4},{6,5},{7,6},{8,11},{9,8},{10,9... | collective-permute-start | bytes 589832 | tf_op jit(solution)/shard_map/ppermute | solution.py:52
  105.3 2.4 collective-permute-start.17
  108.5 10.2 %collective-permute-start.18 = (bf16[128,768]{1,0:T(8,128)(2,1)S(1)}, bf16[128,768]{1,0:T(8,128)(2,1)S(1)}, u32[]{:S(2)}, u32[]{:S(2)}) collective-permute-start(bf16[128,768]{1,0:T(8,128)(2,1)S(1)} %get-tuple-element.195), channel_id=1, source_target_pairs={{0,3},{1,0},{2,1},{3,2},{4,7},{5,4},{6,5},{7,6},{8,11},{9,8},{10,9... | collective-permute-start | bytes 589832 | tf_op jit(solution)/shard_map/ppermute | solution.py:52
  110.5 8.2 %collective-permute-start.19 = (bf16[128,768]{1,0:T(8,128)(2,1)S(1)}, bf16[128,768]{1,0:T(8,128)(2,1)S(1)}, u32[]{:S(2)}, u32[]{:S(2)}) collective-permute-start(bf16[128,768]{1,0:T(8,128)(2,1)S(1)} %get-tuple-element.196), channel_id=1, source_target_pairs={{0,4},{4,0},{8,12},{12,8},{1,5},{5,1},{9,13},{13,9},{2,6},{6,2},{1... | collective-permute-start | bytes 589832 | tf_op jit(solution)/shard_map/ppermute | solution.py:47
  110.5 17.1 %collective-permute-start.20 = (bf16[128,768]{1,0:T(8,128)(2,1)S(1)}, bf16[128,768]{1,0:T(8,128)(2,1)S(1)}, u32[]{:S(2)}, u32[]{:S(2)}) collective-permute-start(bf16[128,768]{1,0:T(8,128)(2,1)S(1)} %get-tuple-element.208), channel_id=1, source_target_pairs={{0,2},{1,3},{2,0},{3,1},{4,6},{5,7},{6,4},{7,5},{8,10},{9,11},{10,... | collective-permute-start | bytes 589832 | tf_op jit(solution)/shard_map/ppermute | solution.py:52
  110.5 17.1 %collective-permute-start.21 = (bf16[128,768]{1,0:T(8,128)(2,1)S(1)}, bf16[128,768]{1,0:T(8,128)(2,1)S(1)}, u32[]{:S(2)}, u32[]{:S(2)}) collective-permute-start(bf16[128,768]{1,0:T(8,128)(2,1)S(1)} %get-tuple-element.209), channel_id=1, source_target_pairs={{0,1},{1,2},{2,3},{3,0},{4,5},{5,6},{6,7},{7,4},{8,9},{9,10},{10,1... | collective-permute-start | bytes 589832 | tf_op jit(solution)/shard_map/ppermute | solution.py:52
  128.6 6.0 %collective-permute-start.24 = (bf16[128,768]{1,0:T(8,128)(2,1)S(1)}, bf16[128,768]{1,0:T(8,128)(2,1)S(1)}, u32[]{:S(2)}, u32[]{:S(2)}) collective-permute-start(bf16[128,768]{1,0:T(8,128)(2,1)S(1)} %get-tuple-element.210.refs_0_.g_own), channel_id=1, source_target_pairs={{0,4},{4,0},{8,12},{12,8},{1,5},{5,1},{9,13},{13,9},{2,6},{6,2},{1... | collective-permute-start | bytes 589832 | tf_op jit(solution)/shard_map/ppermute | solution.py:47
  128.7 22.3 %collective-permute-start.22 = (bf16[128,768]{1,0:T(8,128)(2,1)S(1)}, bf16[128,768]{1,0:T(8,128)(2,1)S(1)}, u32[]{:S(2)}, u32[]{:S(2)}) collective-permute-start(bf16[128,768]{1,0:T(8,128)(2,1)S(1)} %get-tuple-element.210.refs_0_.g_own), channel_id=1, source_target_pairs={{0,1},{1,2},{2,3},{3,0},{4,5},{5,6},{6,7},{7,4},{8,9},{9,10},{10,1... | collective-permute-start | bytes 589832 | tf_op jit(solution)/shard_map/ppermute | solution.py:52
  129.8 22.1 %collective-permute-start.28 = (bf16[128,768]{1,0:T(8,128)(2,1)S(1)}, bf16[128,768]{1,0:T(8,128)(2,1)S(1)}, u32[]{:S(2)}, u32[]{:S(2)}) collective-permute-start(bf16[128,768]{1,0:T(8,128)(2,1)S(1)} %get-tuple-element.210.refs_0_.g_own), channel_id=1, source_target_pairs={{0,2},{1,3},{2,0},{3,1},{4,6},{5,7},{6,4},{7,5},{8,10},{9,11},{10,... | collective-permute-start | bytes 589832 | tf_op jit(solution)/shard_map/ppermute | solution.py:52
  131.7 21.7 %collective-permute-start.29 = (bf16[128,768]{1,0:T(8,128)(2,1)S(1)}, bf16[128,768]{1,0:T(8,128)(2,1)S(1)}, u32[]{:S(2)}, u32[]{:S(2)}) collective-permute-start(bf16[128,768]{1,0:T(8,128)(2,1)S(1)} %get-tuple-element.210.refs_0_.g_own), channel_id=1, source_target_pairs={{0,3},{1,0},{2,1},{3,2},{4,7},{5,4},{6,5},{7,6},{8,11},{9,8},{10,9... | collective-permute-start | bytes 589832 | tf_op jit(solution)/shard_map/ppermute | solution.py:52
  134.6 16.1 %collective-permute-start.23 = (bf16[2,2,192,768]{3,2,1,0:T(8,128)(2,1)S(1)}, bf16[2,2,192,768]{3,2,1,0:T(8,128)(2,1)S(1)}, u32[]{:S(2)}, u32[]{:S(2)}) collective-permute-start(bf16[2,2,192,768]{3,2,1,0:T(8,128)(2,1)S(1)} %get-tuple-element.211), channel_id=1, source_target_pairs={{0,4},{4,0},{8,12},{12,8},{1,5},{5,1},{9,13},{13,9},{2,6},{6,2},{1... | collective-permute-start | bytes 3538952 | tf_op jit(solution)/shard_map/ppermute | solution.py:47
  134.6 28.8 %collective-permute-start.26 = (bf16[2,4,96,768]{3,2,1,0:T(8,128)(2,1)S(1)}, bf16[2,4,96,768]{3,2,1,0:T(8,128)(2,1)S(1)}, u32[]{:S(2)}, u32[]{:S(2)}) collective-permute-start(bf16[2,4,96,768]{3,2,1,0:T(8,128)(2,1)S(1)} %get-tuple-element.226), channel_id=1, source_target_pairs={{0,8},{4,12},{8,0},{12,4},{1,9},{5,13},{9,1},{13,5},{2,10},{6,14},... | collective-permute-start | bytes 3538952 | tf_op jit(solution)/shard_map/ppermute | solution.py:47
  150.7 3.6 %collective-permute-start.30 = (bf16[512,768]{1,0:T(8,128)(2,1)S(1)}, bf16[512,768]{1,0:T(8,128)(2,1)S(1)}, u32[]{:S(2)}, u32[]{:S(2)}) collective-permute-start(bf16[512,768]{1,0:T(8,128)(2,1)S(1)} %get-tuple-element.234), channel_id=1, source_target_pairs={{0,4},{4,0},{8,12},{12,8},{1,5},{5,1},{9,13},{13,9},{2,6},{6,2},{1... | collective-permute-start | bytes 2359304 | tf_op jit(solution)/shard_map/ppermute | solution.py:47
  151.0 44.2 %collective-permute-start.25 = (bf16[2,4,96,768]{3,2,1,0:T(8,128)(2,1)S(1)}, bf16[2,4,96,768]{3,2,1,0:T(8,128)(2,1)S(1)}, u32[]{:S(2)}, u32[]{:S(2)}) collective-permute-start(bf16[2,4,96,768]{3,2,1,0:T(8,128)(2,1)S(1)} %get-tuple-element.223), channel_id=1, source_target_pairs={{0,8},{4,12},{8,0},{12,4},{1,9},{5,13},{9,1},{13,5},{2,10},{6,14},... | collective-permute-start | bytes 3538952 | tf_op jit(solution)/shard_map/ppermute | solution.py:47
  151.9 15.3 %collective-permute-start.27 = (bf16[2,192,768]{2,1,0:T(8,128)(2,1)S(1)}, bf16[2,192,768]{2,1,0:T(8,128)(2,1)S(1)}, u32[]{:S(2)}, u32[]{:S(2)}) collective-permute-start(bf16[2,192,768]{2,1,0:T(8,128)(2,1)S(1)} %fusion.3), channel_id=1, source_target_pairs={{0,16},{16,0},{1,17},{17,1},{2,18},{18,2},{3,19},{19,3},{4,20},{20... | collective-permute-start | bytes 1769480 | tf_op jit(solution)/shard_map/ppermute | solution.py:204
  155.4 11.8 %collective-permute-start.32 = (bf16[128,768]{1,0:T(8,128)(2,1)S(1)}, bf16[128,768]{1,0:T(8,128)(2,1)S(1)}, u32[]{:S(2)}, u32[]{:S(2)}) collective-permute-start(bf16[128,768]{1,0:T(8,128)(2,1)S(1)} %get-tuple-element.241), channel_id=1, source_target_pairs={{0,3},{1,0},{2,1},{3,2},{4,7},{5,4},{6,5},{7,6},{8,11},{9,8},{10,9... | collective-permute-start | bytes 589832 | tf_op jit(solution)/shard_map/ppermute | solution.py:52
  156.0 17.2 %collective-permute-start.34 = (bf16[128,768]{1,0:T(8,128)(2,1)S(1)}, bf16[128,768]{1,0:T(8,128)(2,1)S(1)}, u32[]{:S(2)}, u32[]{:S(2)}) collective-permute-start(bf16[128,768]{1,0:T(8,128)(2,1)S(1)} %get-tuple-element.248), channel_id=1, source_target_pairs={{0,2},{1,3},{2,0},{3,1},{4,6},{5,7},{6,4},{7,5},{8,10},{9,11},{10,... | collective-permute-start | bytes 589832 | tf_op jit(solution)/shard_map/ppermute | solution.py:52
  163.4 9.8 %collective-permute-start.35 = (bf16[128,768]{1,0:T(8,128)(2,1)S(1)}, bf16[128,768]{1,0:T(8,128)(2,1)S(1)}, u32[]{:S(2)}, u32[]{:S(2)}) collective-permute-start(bf16[128,768]{1,0:T(8,128)(2,1)S(1)} %get-tuple-element.249), channel_id=1, source_target_pairs={{0,1},{1,2},{2,3},{3,0},{4,5},{5,6},{6,7},{7,4},{8,9},{9,10},{10,1... | collective-permute-start | bytes 589832 | tf_op jit(solution)/shard_map/ppermute | solution.py:52
  167.5 14.5 %collective-permute-start.31 = (bf16[4,96,768]{2,1,0:T(8,128)(2,1)S(1)}, bf16[4,96,768]{2,1,0:T(8,128)(2,1)S(1)}, u32[]{:S(2)}, u32[]{:S(2)}) collective-permute-start(bf16[4,96,768]{2,1,0:T(8,128)(2,1)S(1)} %fusion.4), channel_id=1, source_target_pairs={{0,16},{16,0},{1,17},{17,1},{2,18},{18,2},{3,19},{19,3},{4,20},{20... | collective-permute-start | bytes 1769480 | tf_op jit(solution)/shard_map/ppermute | solution.py:204
  169.1 26.2 %collective-permute-start.33 = (bf16[2,2,192,768]{3,2,1,0:T(8,128)(2,1)S(1)}, bf16[2,2,192,768]{3,2,1,0:T(8,128)(2,1)S(1)}, u32[]{:S(2)}, u32[]{:S(2)}) collective-permute-start(bf16[2,2,192,768]{3,2,1,0:T(8,128)(2,1)S(1)} %get-tuple-element.244), channel_id=1, source_target_pairs={{0,4},{4,0},{8,12},{12,8},{1,5},{5,1},{9,13},{13,9},{2,6},{6,2},{1... | collective-permute-start | bytes 3538952 | tf_op jit(solution)/shard_map/ppermute | solution.py:47
  174.9 7.2 %collective-permute-start.36 = (bf16[128,768]{1,0:T(8,128)(2,1)S(1)}, bf16[128,768]{1,0:T(8,128)(2,1)S(1)}, u32[]{:S(2)}, u32[]{:S(2)}) collective-permute-start(bf16[128,768]{1,0:T(8,128)(2,1)S(1)} %get-tuple-element.254), channel_id=1, source_target_pairs={{0,3},{1,0},{2,1},{3,2},{4,7},{5,4},{6,5},{7,6},{8,11},{9,8},{10,9... | collective-permute-start | bytes 589832 | tf_op jit(solution)/shard_map/ppermute | solution.py:52
  175.6 19.6 %collective-permute-start.37 = (bf16[128,768]{1,0:T(8,128)(2,1)S(1)}, bf16[128,768]{1,0:T(8,128)(2,1)S(1)}, u32[]{:S(2)}, u32[]{:S(2)}) collective-permute-start(bf16[128,768]{1,0:T(8,128)(2,1)S(1)} %get-tuple-element.255), channel_id=1, source_target_pairs={{0,2},{1,3},{2,0},{3,1},{4,6},{5,7},{6,4},{7,5},{8,10},{9,11},{10,... | collective-permute-start | bytes 589832 | tf_op jit(solution)/shard_map/ppermute | solution.py:52
  182.0 13.3 %collective-permute-start.38 = (bf16[128,768]{1,0:T(8,128)(2,1)S(1)}, bf16[128,768]{1,0:T(8,128)(2,1)S(1)}, u32[]{:S(2)}, u32[]{:S(2)}) collective-permute-start(bf16[128,768]{1,0:T(8,128)(2,1)S(1)} %get-tuple-element.256), channel_id=1, source_target_pairs={{0,1},{1,2},{2,3},{3,0},{4,5},{5,6},{6,7},{7,4},{8,9},{9,10},{10,1... | collective-permute-start | bytes 589832 | tf_op jit(solution)/shard_map/ppermute | solution.py:52
  195.7 15.2 %collective-permute-start.39 = (bf16[4,96,768]{2,1,0:T(8,128)(2,1)S(1)}, bf16[4,96,768]{2,1,0:T(8,128)(2,1)S(1)}, u32[]{:S(2)}, u32[]{:S(2)}) collective-permute-start(bf16[4,96,768]{2,1,0:T(8,128)(2,1)S(1)} %fusion.5), channel_id=1, source_target_pairs={{0,16},{16,0},{1,17},{17,1},{2,18},{18,2},{3,19},{19,3},{4,20},{20... | collective-permute-start | bytes 1769480 | tf_op jit(solution)/shard_map/ppermute | solution.py:204
  196.4 14.5 %collective-permute-start.40 = (bf16[192,768]{1,0:T(8,128)(2,1)S(1)}, bf16[192,768]{1,0:T(8,128)(2,1)S(1)}, u32[]{:S(2)}, u32[]{:S(2)}) collective-permute-start(bf16[192,768]{1,0:T(8,128)(2,1)S(1)} %fusion.9), channel_id=1, source_target_pairs={{0,8},{4,12},{8,0},{12,4},{1,9},{5,13},{9,1},{13,5},{2,10},{6,14},... | collective-permute-start | bytes 884744 | tf_op jit(solution)/shard_map/ppermute | solution.py:47
  197.7 5.8 %collective-permute-start.41 = (bf16[96,768]{1,0:T(8,128)(2,1)S(1)}, bf16[96,768]{1,0:T(8,128)(2,1)S(1)}, u32[]{:S(2)}, u32[]{:S(2)}) collective-permute-start(bf16[96,768]{1,0:T(8,128)(2,1)S(1)} %get-tuple-element.262), channel_id=1, source_target_pairs={{0,3},{1,0},{2,1},{3,2},{4,7},{5,4},{6,5},{7,6},{8,11},{9,8},{10,9... | collective-permute-start | bytes 442376 | tf_op jit(solution)/shard_map/ppermute | solution.py:52
  197.7 13.2 %collective-permute-start.42 = (bf16[96,768]{1,0:T(8,128)(2,1)S(1)}, bf16[96,768]{1,0:T(8,128)(2,1)S(1)}, u32[]{:S(2)}, u32[]{:S(2)}) collective-permute-start(bf16[96,768]{1,0:T(8,128)(2,1)S(1)} %get-tuple-element.263), channel_id=1, source_target_pairs={{0,2},{1,3},{2,0},{3,1},{4,6},{5,7},{6,4},{7,5},{8,10},{9,11},{10,... | collective-permute-start | bytes 442376 | tf_op jit(solution)/shard_map/ppermute | solution.py:52
  198.0 12.9 %collective-permute-start.43 = (bf16[96,768]{1,0:T(8,128)(2,1)S(1)}, bf16[96,768]{1,0:T(8,128)(2,1)S(1)}, u32[]{:S(2)}, u32[]{:S(2)}) collective-permute-start(bf16[96,768]{1,0:T(8,128)(2,1)S(1)} %get-tuple-element.264), channel_id=1, source_target_pairs={{0,1},{1,2},{2,3},{3,0},{4,5},{5,6},{6,7},{7,4},{8,9},{9,10},{10,1... | collective-permute-start | bytes 442376 | tf_op jit(solution)/shard_map/ppermute | solution.py:52
  212.2 17.4 %collective-permute-start.44 = (bf16[400,768]{1,0:T(8,128)(2,1)S(1)}, bf16[400,768]{1,0:T(8,128)(2,1)S(1)}, u32[]{:S(2)}, u32[]{:S(2)}) collective-permute-start(bf16[400,768]{1,0:T(8,128)(2,1)S(1)} %pad_maximum_fusion.4), channel_id=1, source_target_pairs={{0,8},{4,12},{8,0},{12,4},{1,9},{5,13},{9,1},{13,5},{2,10},{6,14},... | collective-permute-start | bytes 1843208 | tf_op jit(solution)/shard_map/ppermute | solution.py:47
  213.1 16.4 %collective-permute-start.45 = (bf16[192,768]{1,0:T(8,128)(2,1)S(1)}, bf16[192,768]{1,0:T(8,128)(2,1)S(1)}, u32[]{:S(2)}, u32[]{:S(2)}) collective-permute-start(bf16[192,768]{1,0:T(8,128)(2,1)S(1)} %fusion.8), channel_id=1, source_target_pairs={{0,16},{16,0},{1,17},{17,1},{2,18},{18,2},{3,19},{19,3},{4,20},{20... | collective-permute-start | bytes 884744 | tf_op jit(solution)/shard_map/ppermute | solution.py:204
  213.8 5.3 %collective-permute-start.46 = (bf16[96,768]{1,0:T(8,128)(2,1)S(1)}, bf16[96,768]{1,0:T(8,128)(2,1)S(1)}, u32[]{:S(2)}, u32[]{:S(2)}) collective-permute-start(bf16[96,768]{1,0:T(8,128)(2,1)S(1)} %get-tuple-element.273), channel_id=1, source_target_pairs={{0,3},{1,0},{2,1},{3,2},{4,7},{5,4},{6,5},{7,6},{8,11},{9,8},{10,9... | collective-permute-start | bytes 442376 | tf_op jit(solution)/shard_map/ppermute | solution.py:52
  214.4 15.1 %collective-permute-start.47 = (bf16[96,768]{1,0:T(8,128)(2,1)S(1)}, bf16[96,768]{1,0:T(8,128)(2,1)S(1)}, u32[]{:S(2)}, u32[]{:S(2)}) collective-permute-start(bf16[96,768]{1,0:T(8,128)(2,1)S(1)} %get-tuple-element.274), channel_id=1, source_target_pairs={{0,2},{1,3},{2,0},{3,1},{4,6},{5,7},{6,4},{7,5},{8,10},{9,11},{10,... | collective-permute-start | bytes 442376 | tf_op jit(solution)/shard_map/ppermute | solution.py:52
  216.6 12.9 %collective-permute-start.48 = (bf16[96,768]{1,0:T(8,128)(2,1)S(1)}, bf16[96,768]{1,0:T(8,128)(2,1)S(1)}, u32[]{:S(2)}, u32[]{:S(2)}) collective-permute-start(bf16[96,768]{1,0:T(8,128)(2,1)S(1)} %get-tuple-element.275), channel_id=1, source_target_pairs={{0,1},{1,2},{2,3},{3,0},{4,5},{5,6},{6,7},{7,4},{8,9},{9,10},{10,1... | collective-permute-start | bytes 442376 | tf_op jit(solution)/shard_map/ppermute | solution.py:52
  232.1 19.0 %collective-permute-start.50 = (bf16[2,192,768]{2,1,0:T(8,128)(2,1)S(1)}, bf16[2,192,768]{2,1,0:T(8,128)(2,1)S(1)}, u32[]{:S(2)}, u32[]{:S(2)}) collective-permute-start(bf16[2,192,768]{2,1,0:T(8,128)(2,1)S(1)} %get-tuple-element.285), channel_id=1, source_target_pairs={{0,8},{4,12},{8,0},{12,4},{1,9},{5,13},{9,1},{13,5},{2,10},{6,14},... | collective-permute-start | bytes 1769480 | tf_op jit(solution)/shard_map/ppermute | solution.py:47
  234.6 13.8 %collective-permute-start.49 = (bf16[208,768]{1,0:T(8,128)(2,1)}, bf16[208,768]{1,0:T(8,128)(2,1)}, u32[]{:S(2)}, u32[]{:S(2)}) collective-permute-start(bf16[208,768]{1,0:T(8,128)(2,1)} %pad_maximum_fusion.10), channel_id=1, source_target_pairs={{0,16},{16,0},{1,17},{17,1},{2,18},{18,2},{3,19},{19,3},{4,20},{20... | collective-permute-start | bytes 958472 | tf_op jit(solution)/shard_map/ppermute | solution.py:204
  236.0 8.7 %collective-permute-start.51 = (bf16[96,768]{1,0:T(8,128)(2,1)S(1)}, bf16[96,768]{1,0:T(8,128)(2,1)S(1)}, u32[]{:S(2)}, u32[]{:S(2)}) collective-permute-start(bf16[96,768]{1,0:T(8,128)(2,1)S(1)} %fusion.17), channel_id=1, source_target_pairs={{0,1},{1,2},{2,3},{3,0},{4,5},{5,6},{6,7},{7,4},{8,9},{9,10},{10,1... | collective-permute-start | bytes 442376 | tf_op jit(solution)/shard_map/ppermute | solution.py:52
  236.1 12.4 %collective-permute-start.52 = (bf16[96,768]{1,0:T(8,128)(2,1)S(1)}, bf16[96,768]{1,0:T(8,128)(2,1)S(1)}, u32[]{:S(2)}, u32[]{:S(2)}) collective-permute-start(bf16[96,768]{1,0:T(8,128)(2,1)S(1)} %fusion.17), channel_id=1, source_target_pairs={{0,2},{1,3},{2,0},{3,1},{4,6},{5,7},{6,4},{7,5},{8,10},{9,11},{10,... | collective-permute-start | bytes 442376 | tf_op jit(solution)/shard_map/ppermute | solution.py:52
  237.0 11.4 %collective-permute-start.53 = (bf16[96,768]{1,0:T(8,128)(2,1)S(1)}, bf16[96,768]{1,0:T(8,128)(2,1)S(1)}, u32[]{:S(2)}, u32[]{:S(2)}) collective-permute-start(bf16[96,768]{1,0:T(8,128)(2,1)S(1)} %fusion.17), channel_id=1, source_target_pairs={{0,3},{1,0},{2,1},{3,2},{4,7},{5,4},{6,5},{7,6},{8,11},{9,8},{10,9... | collective-permute-start | bytes 442376 | tf_op jit(solution)/shard_map/ppermute | solution.py:52
  253.3 15.7 %collective-permute-start.55 = (bf16[4,96,768]{2,1,0:T(8,128)(2,1)S(1)}, bf16[4,96,768]{2,1,0:T(8,128)(2,1)S(1)}, u32[]{:S(2)}, u32[]{:S(2)}) collective-permute-start(bf16[4,96,768]{2,1,0:T(8,128)(2,1)S(1)} %pad_maximum_fusion.6.mine_ref), channel_id=1, source_target_pairs={{0,16},{16,0},{1,17},{17,1},{2,18},{18,2},{3,19},{19,3},{4,20},{20... | collective-permute-start | bytes 1769480 | tf_op jit(solution)/shard_map/ppermute | solution.py:204
  253.4 15.6 %collective-permute-start.54 = (bf16[192,768]{1,0:T(8,128)(2,1)S(1)}, bf16[192,768]{1,0:T(8,128)(2,1)S(1)}, u32[]{:S(2)}, u32[]{:S(2)}) collective-permute-start(bf16[192,768]{1,0:T(8,128)(2,1)S(1)} %fusion.7), channel_id=1, source_target_pairs={{0,16},{16,0},{1,17},{17,1},{2,18},{18,2},{3,19},{19,3},{4,20},{20... | collective-permute-start | bytes 884744 | tf_op jit(solution)/shard_map/ppermute | solution.py:204
  255.4 7.5 %collective-permute-start.56 = (bf16[112,768]{1,0:T(8,128)(2,1)S(1)}, bf16[112,768]{1,0:T(8,128)(2,1)S(1)}, u32[]{:S(2)}, u32[]{:S(2)}) collective-permute-start(bf16[112,768]{1,0:T(8,128)(2,1)S(1)} %pad_maximum_fusion.11), channel_id=1, source_target_pairs={{0,1},{1,2},{2,3},{3,0},{4,5},{5,6},{6,7},{7,4},{8,9},{9,10},{10,1... | collective-permute-start | bytes 516104 | tf_op jit(solution)/shard_map/ppermute | solution.py:52
  255.5 11.9 %collective-permute-start.57 = (bf16[112,768]{1,0:T(8,128)(2,1)S(1)}, bf16[112,768]{1,0:T(8,128)(2,1)S(1)}, u32[]{:S(2)}, u32[]{:S(2)}) collective-permute-start(bf16[112,768]{1,0:T(8,128)(2,1)S(1)} %pad_maximum_fusion.11), channel_id=1, source_target_pairs={{0,2},{1,3},{2,0},{3,1},{4,6},{5,7},{6,4},{7,5},{8,10},{9,11},{10,... | collective-permute-start | bytes 516104 | tf_op jit(solution)/shard_map/ppermute | solution.py:52
  256.9 10.5 %collective-permute-start.58 = (bf16[112,768]{1,0:T(8,128)(2,1)S(1)}, bf16[112,768]{1,0:T(8,128)(2,1)S(1)}, u32[]{:S(2)}, u32[]{:S(2)}) collective-permute-start(bf16[112,768]{1,0:T(8,128)(2,1)S(1)} %pad_maximum_fusion.11), channel_id=1, source_target_pairs={{0,3},{1,0},{2,1},{3,2},{4,7},{5,4},{6,5},{7,6},{8,11},{9,8},{10,9... | collective-permute-start | bytes 516104 | tf_op jit(solution)/shard_map/ppermute | solution.py:52
  270.6 10.0 %collective-permute-start.63 = (f32[8,768]{1,0:T(8,128)}, f32[8,768]{1,0:T(8,128)}, u32[]{:S(2)}, u32[]{:S(2)}) collective-permute-start(f32[8,768]{1,0:T(8,128)} %add_add_fusion), channel_id=1, source_target_pairs={{0,4},{4,0},{8,12},{12,8},{1,5},{5,1},{9,13},{13,9},{2,6},{6,2},{1... | collective-permute-start | bytes 73736 | tf_op jit(solution)/shard_map/ppermute | solution.py:47
  271.9 17.1 %collective-permute-start.61 = (bf16[4,192,768]{2,1,0:T(8,128)(2,1)S(1)}, bf16[4,192,768]{2,1,0:T(8,128)(2,1)S(1)}, u32[]{:S(2)}, u32[]{:S(2)}) collective-permute-start(bf16[4,192,768]{2,1,0:T(8,128)(2,1)S(1)} %bitcast.121), channel_id=1, source_target_pairs={{0,4},{4,0},{8,12},{12,8},{1,5},{5,1},{9,13},{13,9},{2,6},{6,2},{1... | collective-permute-start | bytes 3538952 | tf_op jit(solution)/shard_map/ppermute | solution.py:47
  272.5 15.3 %collective-permute-start.59 = (bf16[4,96,768]{2,1,0:T(8,128)(2,1)S(1)}, bf16[4,96,768]{2,1,0:T(8,128)(2,1)S(1)}, u32[]{:S(2)}, u32[]{:S(2)}) collective-permute-start(bf16[4,96,768]{2,1,0:T(8,128)(2,1)S(1)} %pad_maximum_fusion.7.mine_ref), channel_id=1, source_target_pairs={{0,16},{16,0},{1,17},{17,1},{2,18},{18,2},{3,19},{19,3},{4,20},{20... | collective-permute-start | bytes 1769480 | tf_op jit(solution)/shard_map/ppermute | solution.py:204
  274.0 15.0 %collective-permute-start.60 = (bf16[2,192,768]{2,1,0:T(8,128)(2,1)S(1)}, bf16[2,192,768]{2,1,0:T(8,128)(2,1)S(1)}, u32[]{:S(2)}, u32[]{:S(2)}) collective-permute-start(bf16[2,192,768]{2,1,0:T(8,128)(2,1)S(1)} %pad_maximum_fusion.8), channel_id=1, source_target_pairs={{0,8},{4,12},{8,0},{12,4},{1,9},{5,13},{9,1},{13,5},{2,10},{6,14},... | collective-permute-start | bytes 1769480 | tf_op jit(solution)/shard_map/ppermute | solution.py:47
  292.3 2.9 collective-permute-start.62
  (47 other events, 554.9 us)
Sparse Core Ops, SparseCore 0:
  236.1 19.9 all-gather.2

commit v3 on v2

--- a/solution.py
+++ b/solution.py
@@ -712,7 +712,9 @@
     inner = Y_BIT if outer == X_BIT else X_BIT
     spec = pl.BlockSpec((1, rows, width), lambda i, p: (i ^ (2 * p[outer] + p[inner]), 0, 0))
     out = ((2, 4 * rows, width), F32, pl.BlockSpec((1, rows, width), lambda i, p: (l, i, 0)))
-    return call(ff_finish_kernel, 4, [(mine, spec), (got, spec)], [out, out], prefetch=(spot,), earlier=earlier)
+    return call(
+        ff_finish_kernel, 4, [(mine, spec), (got, spec)], [out, out], prefetch=(spot,), earlier=earlier, cost=COST // 100
+    )
 
 
 def attn_kernel(mode, count, *refs):
@@ -939,6 +941,7 @@
         ],
         prefetch=(spot,),
         earlier=earlier,
+        cost=COST // 100,
     )
 
 
@@ -1150,15 +1153,18 @@
     rows_w = half_w0.shape[1]
     mine_w0 = jnp.stack([g[:rows_w] for g in (block_w0, *got_b0)])
     mine_w0, ends = tie(mine_w0, ends)
-    got_w0, got_f0, got_f1 = together((mine_w0, turn_batch), (pair_f0, turn_high), (full_f1, turn_low))
-    full_f0 = jnp.concatenate([pair_f0, got_f0])
-    got_f0, got_g = turn_low(full_f0), turn_low(gain)
-    d_gains = (gain + got_g)[:2]
+    mine_w0, pair_f0, full_f1 = tie(mine_w0, pair_f0, full_f1)
+    got_w0, got_f0, got_f1 = turn_batch(mine_w0), turn_high(pair_f0), turn_low(full_f1)
     late = ff_finish(spot, 1, full_f1, got_f1, X_BIT)
-    d_in, d_mlp = ff_finish(spot, 0, full_f0, got_f0, Y_BIT, late)
+    late_attn = attn_finish(spot, 1, mine_w1, got_w1)
     out = tokens.astype(F32) + ends[:, :, :width].astype(F32)
     d_tokens = cotangent.astype(F32) + ends[:, :, width:].astype(F32)
-    d_qkv, d_att = attn_finish(spot, 0, mine_w0, got_w0, attn_finish(spot, 1, mine_w1, got_w1))
+    d_gains = (gain + turn_low(gain))[:2]
+    got_w0, got_f0, late, late_attn, out, d_tokens, d_gains = tie(got_w0, got_f0, late, late_attn, out, d_tokens, d_gains)
+    full_f0 = jnp.concatenate([pair_f0, got_f0])
+    got_f0 = turn_low(full_f0)
+    d_in, d_mlp = ff_finish(spot, 0, full_f0, got_f0, Y_BIT, late)
+    d_qkv, d_att = attn_finish(spot, 0, mine_w0, got_w0, late_attn)
     return (out.reshape(shape), d_tokens.reshape(shape), d_qkv, d_att, d_in, d_mlp, d_gains)
 
 

time: 309 us -> 303 us (0.981); the launches traced: 305 us -> 302 us
    ppermute x20, waiting for transfers between devices: 15.9 us -> 19.5 us  [swap(): return lax.ppermute(x, 'head', [(i, i ^ bit) for i in range(size)])]
  transfers between devices with their start and end apart: 65 -> 65, of which waited for: 22 -> 21; matrix products, arithmetic and copies ran while one was open for 9% -> 8% of each run, Pallas kernels for 23% -> 24%
where the time goes in v3:
time: 303 us; the launch traced here: 302 us
  waiting for transfers between devices  105 us (35%)
  Pallas kernels  80.4 us (27%)
  starting transfers between devices  67.1 us (22%)
  other arithmetic  19.1 us (6%)
  local copies, waits for them, and re-layouts  15.7 us (5%)
  between operations  15 us (5%)
    pallas_call x21, Pallas kernels, call(): pl.pallas_call(kernel, grid_spec=pltpu.PrefetchScalarGridSpec(num_scalar_...  80.4 us
    ppermute x36, waiting for transfers between devices, shift(): lax.ppermute(x, 'wide', [(i, (i + step) % size) for i in range(size)])  73.1 us
    ppermute x36, starting transfers between devices, shift(): lax.ppermute(x, 'wide', [(i, (i + step) % size) for i in range(size)])  47.7 us
    ppermute x20, waiting for transfers between devices, swap(): return lax.ppermute(x, 'head', [(i, i ^ bit) for i in range(size)])  19.5 us
    ppermute x8, waiting for transfers between devices, turn_batch(): return lax.ppermute(x, 'batch', [(i, size - 1 - i) for i in range(size)])  12.6 us
    ppermute x20, starting transfers between devices, swap(): return lax.ppermute(x, 'head', [(i, i ^ bit) for i in range(size)])  11.8 us
    ppermute x8, starting transfers between devices, turn_batch(): return lax.ppermute(x, 'batch', [(i, size - 1 - i) for i in range(size)])  7.48 us
  transfers between devices with their start and end apart: 65, of which 21 were waited for; matrix products, arithmetic and copies ran while one was open for 8% of the time, Pallas kernels for 24%

profile of v3, /device:TPU:0, one launch (start us, length us, event | category | flops | bytes accessed | tf_op | source)
XLA Modules:
  0.0 302.4 jit_solution(11132502329656685990)
XLA Ops:
  9.0 1.4 shard_map.135.refs_0_
  10.4 3.0 collective-permute-start
  13.4 2.6 collective-permute-start.1
  16.0 1.3 collective-permute-start.2
  20.3 1.5 collective-permute-start.7
  23.8 1.9 fusion.35
  27.9 1.4 copy.35
  29.4 1.4 copy.36
  30.8 1.4 pad_maximum_fusion
  32.3 3.9 %shard_map.136 = (f32[512,768]{1,0:T(8,128)S(1)}, bf16[512,768]{1,0:T(8,128)(2,1)S(1)}, bf16[512,768]{1,0:T(8,128)(2,1)S(1)}, f32[128,768]{1,0:T(8,128)S(1)}, bf...) custom-call(s32[5]{0:T(128)S(1)} %stack.80.place_ref.spot_ref, ...), custom_call_target="tpu_custom_call" | custom-call | flops 100000000 | tf_op jit(solution)/shard_map/pallas_call | solution.py:480
  37.1 2.7 collective-permute-start.3
  40.4 7.1 %collective-permute-done.7.refs_4_.refs_5_ = bf16[4,192,768]{2,1,0:T(8,128)(2,1)} collective-permute-done((bf16[4,192,768]{2,1,0:T(8,128)(2,1)}, bf16[4,192,768]{2,1,0:T(8,128)(2,1)}, u32[]{:S(2)}, u32[]{:S(2)}) %collective-permute-start.7) | collective-permute-done | bytes 1179680 | tf_op jit(solution)/shard_map/ppermute | solution.py:47
  47.5 10.3 %shard_map.137 = (bf16[256,384]{1,0:T(8,128)(2,1)S(1)}, bf16[1024,384]{1,0:T(8,128)(2,1)S(1)}, bf16[1024,384]{1,0:T(8,128)(2,1)S(1)}, bf16[256,384]{1,0:T(8,128)...) custom-call(bf16[512,768]{1,0:T(8,128)(2,1)S(1)} %get-tuple-element.179.refs_0_.own_act., ...), custom_call_target="tpu_custom_call" | custom-call | flops 20000000000 | tf_op jit(solution)/shard_map/pallas_call | solution.py:480
  57.9 1.6 collective-permute-start.16
  61.5 2.8 collective-permute-start.11
  64.3 5.9 %collective-permute-done.9.refs_1_ = bf16[128,768]{1,0:T(8,128)(2,1)S(1)} collective-permute-done((bf16[128,768]{1,0:T(8,128)(2,1)S(1)}, bf16[128,768]{1,0:T(8,128)(2,1)S(1)}, u32[]{:S(2)}, u32[]{:S(2)}) %collective-permute-start.9) | collective-permute-done | bytes 196640 | tf_op jit(solution)/shard_map/ppermute | solution.py:52
  70.2 7.7 %collective-permute-done.10.refs_2_ = bf16[128,768]{1,0:T(8,128)(2,1)S(1)} collective-permute-done((bf16[128,768]{1,0:T(8,128)(2,1)S(1)}, bf16[128,768]{1,0:T(8,128)(2,1)S(1)}, u32[]{:S(2)}, u32[]{:S(2)}) %collective-permute-start.10) | collective-permute-done | bytes 196640 | tf_op jit(solution)/shard_map/ppermute | solution.py:52
  77.8 2.7 shard_map.139
  80.7 4.2 %collective-permute-start.12 = (bf16[128,768]{1,0:T(8,128)(2,1)S(1)}, bf16[128,768]{1,0:T(8,128)(2,1)S(1)}, u32[]{:S(2)}, u32[]{:S(2)}) collective-permute-start(bf16[128,768]{1,0:T(8,128)(2,1)S(1)} %copy-done.4), channel_id=1, source_target_pairs={{0,1},{1,2},{2,3},{3,0},{4,5},{5,6},{6,7},{7,4},{8,9},{9,10},{10,1... | collective-permute-start | bytes 589832 | tf_op jit(solution)/shard_map/ppermute | solution.py:52
  84.9 2.5 collective-permute-start.14
  88.4 17.3 %shard_map.141 = (bf16[256,384]{1,0:T(8,128)(2,1)S(1)}, bf16[1024,384]{1,0:T(8,128)(2,1)S(1)}, bf16[1024,384]{1,0:T(8,128)(2,1)S(1)}, bf16[256,384]{1,0:T(8,128)...) custom-call(bf16[512,768]{1,0:T(8,128)(2,1)S(1)} %get-tuple-element., ...), custom_call_target="tpu_custom_call" | custom-call | flops 20000000000 | tf_op jit(solution)/shard_map/pallas_call | solution.py:480
  106.7 1.4 collective-permute-done.17.got_ref
  108.9 2.0 collective-permute-start.18
  111.7 3.8 %shard_map.143 = (f32[2,2,192,768]{3,2,1,0:T(8,128)S(1)}, bf16[2,2,192,768]{3,2,1,0:T(8,128)(2,1)S(1)}) custom-call(s32[5]{0:T(128)S(1)} %stack.80.place_ref.spot_ref, bf16[512,768]{1,0:T(8,128)(2,1)} %copy-done.8, bf16[512,768]{1,0:T(8,128)(2,1)} %copy-done.12, bf16[512,768]{1,0:T(8,128)(2,1)} %copy-done.11, bf16[512,768]{1,0:T(8,128)(2,1)} %copy-done.10), custom_call_target="tpu_custom_call" | custom-call | flops 5000000000 | tf_op jit(solution)/shard_map/pallas_call | solution.py:480
  115.5 3.5 %shard_map.144 = (f32[2,4,96,768]{3,2,1,0:T(8,128)S(1)}, bf16[2,4,96,768]{3,2,1,0:T(8,128)(2,1)S(1)}) custom-call(s32[5]{0:T(128)S(1)} %stack.80.place_ref.spot_ref, bf16[512,768]{1,0:T(8,128)(2,1)S(1)} %copy-done.9, bf16[512,768]{1,0:T(8,128)(2,1)S(1)} %collective-permute-done.15.refs_1_.other_act, bf16[128,768]{1,0:T(8,128)(2,1)S(1)} %copy-done.4, ...), custom_call_target="tpu_custom_call" | custom-call | flops 5000000000 | tf_op jit(solution)/shard_map/pallas_call | solution.py:480
  119.1 8.6 %collective-permute-done.20.refs_2_ = bf16[128,768]{1,0:T(8,128)(2,1)S(1)} collective-permute-done((bf16[128,768]{1,0:T(8,128)(2,1)S(1)}, bf16[128,768]{1,0:T(8,128)(2,1)S(1)}, u32[]{:S(2)}, u32[]{:S(2)}) %collective-permute-start.20) | collective-permute-done | bytes 196640 | tf_op jit(solution)/shard_map/ppermute | solution.py:52
  128.8 1.3 collective-permute-start.22
  130.2 2.0 collective-permute-start.28
  132.1 2.9 collective-permute-start.29
  136.3 11.2 %shard_map.146 = (bf16[256,384]{1,0:T(8,128)(2,1)S(1)}, bf16[1024,384]{1,0:T(8,128)(2,1)S(1)}, bf16[1024,384]{1,0:T(8,128)(2,1)S(1)}, f32[512,768]{1,0:T(8,128)S(1)}, bf16[512,768]{1,0:T(8,128)(2,1)S(1)}) custom-call(bf16[128,768]{1,0:T(8,128)(2,1)S(1)} %get-tuple-element.216.refs_0_.g_own, bf16[128,768]{1,0:T(8,128)(2,1)S(1)} %collective-permute-done.24.refs_1_.g_other, ...), custom_call_target="tpu_custom_call" | custom-call | flops 20000000000 | tf_op jit(solution)/shard_map/pallas_call | solution.py:480
  147.5 3.6 %shard_map.147 = (f32[2,4,96,768]{3,2,1,0:T(8,128)S(1)}, bf16[2,4,96,768]{3,2,1,0:T(8,128)(2,1)S(1)}) custom-call(s32[5]{0:T(128)S(1)} %stack.80.place_ref.spot_ref, bf16[512,768]{1,0:T(8,128)(2,1)S(1)} %get-tuple-element.179.refs_0_.own_act.x_ref, bf16[512,768]{1,0:T(8,128)(2,1)S(1)} %collective-permute-done.6.refs_1_.other_act, ...), custom_call_target="tpu_custom_call" | custom-call | flops 5000000000 | tf_op jit(solution)/shard_map/pallas_call | solution.py:480
  152.3 1.6 collective-permute-start.27
  156.5 3.8 %shard_map.150 = (f32[2,2,192,768]{3,2,1,0:T(8,128)S(1)}, bf16[2,2,192,768]{3,2,1,0:T(8,128)(2,1)S(1)}) custom-call(s32[5]{0:T(128)S(1)} %stack.80.place_ref.spot_ref, bf16[512,768]{1,0:T(8,128)(2,1)} %copy-done.7, bf16[512,768]{1,0:T(8,128)(2,1)} %copy-done.14, bf16[512,768]{1,0:T(8,128)(2,1)} %copy-done.13, bf16[512,768]{1,0:T(8,128)(2,1)} %copy-done.6), custom_call_target="tpu_custom_call" | custom-call | flops 5000000000 | tf_op jit(solution)/shard_map/pallas_call | solution.py:480
  160.3 3.5 %collective-permute-done.26 = bf16[2,4,96,768]{3,2,1,0:T(8,128)(2,1)S(1)} collective-permute-done((bf16[2,4,96,768]{3,2,1,0:T(8,128)(2,1)S(1)}, bf16[2,4,96,768]{3,2,1,0:T(8,128)(2,1)S(1)}, u32[]{:S(2)}, u32[]{:S(2)}) %collective-permute-start.26) | collective-permute-done | bytes 1179680 | tf_op jit(solution)/shard_map/ppermute | solution.py:47
  163.8 3.8 %collective-permute-done.27 = bf16[2,192,768]{2,1,0:T(8,128)(2,1)S(1)} collective-permute-done((bf16[2,192,768]{2,1,0:T(8,128)(2,1)S(1)}, bf16[2,192,768]{2,1,0:T(8,128)(2,1)S(1)}, u32[]{:S(2)}, u32[]{:S(2)}) %collective-permute-start.27) | collective-permute-done | bytes 589856 | tf_op jit(solution)/shard_map/ppermute | solution.py:204
  167.9 1.6 collective-permute-start.31
  169.5 4.1 %collective-permute-done.34.refs_3_ = bf16[128,768]{1,0:T(8,128)(2,1)S(1)} collective-permute-done((bf16[128,768]{1,0:T(8,128)(2,1)S(1)}, bf16[128,768]{1,0:T(8,128)(2,1)S(1)}, u32[]{:S(2)}, u32[]{:S(2)}) %collective-permute-start.34) | collective-permute-done | bytes 196640 | tf_op jit(solution)/shard_map/ppermute | solution.py:52
  173.6 1.7 shard_map.151
  176.0 1.9 collective-permute-start.37
  178.2 4.2 %collective-permute-done.31 = bf16[4,96,768]{2,1,0:T(8,128)(2,1)S(1)} collective-permute-done((bf16[4,96,768]{2,1,0:T(8,128)(2,1)S(1)}, bf16[4,96,768]{2,1,0:T(8,128)(2,1)S(1)}, u32[]{:S(2)}, u32[]{:S(2)}) %collective-permute-start.31) | collective-permute-done | bytes 589856 | tf_op jit(solution)/shard_map/ppermute | solution.py:204
  182.5 13.2 %collective-permute-done.37 = bf16[128,768]{1,0:T(8,128)(2,1)S(1)} collective-permute-done((bf16[128,768]{1,0:T(8,128)(2,1)S(1)}, bf16[128,768]{1,0:T(8,128)(2,1)S(1)}, u32[]{:S(2)}, u32[]{:S(2)}) %collective-permute-start.37) | collective-permute-done | bytes 196640 | tf_op jit(solution)/shard_map/ppermute | solution.py:52
  196.9 1.3 collective-permute-start.40
  198.4 2.0 collective-permute-start.43
  200.8 3.2 %collective-permute-done.41 = bf16[96,768]{1,0:T(8,128)(2,1)S(1)} collective-permute-done((bf16[96,768]{1,0:T(8,128)(2,1)S(1)}, bf16[96,768]{1,0:T(8,128)(2,1)S(1)}, u32[]{:S(2)}, u32[]{:S(2)}) %collective-permute-start.41) | collective-permute-done | bytes 147488 | tf_op jit(solution)/shard_map/ppermute | solution.py:52
  204.0 7.4 %collective-permute-done.42 = bf16[96,768]{1,0:T(8,128)(2,1)S(1)} collective-permute-done((bf16[96,768]{1,0:T(8,128)(2,1)S(1)}, bf16[96,768]{1,0:T(8,128)(2,1)S(1)}, u32[]{:S(2)}, u32[]{:S(2)}) %collective-permute-start.42) | collective-permute-done | bytes 147488 | tf_op jit(solution)/shard_map/ppermute | solution.py:52
  215.1 2.2 collective-permute-start.47
  217.3 1.9 collective-permute-start.48
  220.0 10.2 %collective-permute-done.47 = bf16[96,768]{1,0:T(8,128)(2,1)S(1)} collective-permute-done((bf16[96,768]{1,0:T(8,128)(2,1)S(1)}, bf16[96,768]{1,0:T(8,128)(2,1)S(1)}, u32[]{:S(2)}, u32[]{:S(2)}) %collective-permute-start.47) | collective-permute-done | bytes 147488 | tf_op jit(solution)/shard_map/ppermute | solution.py:52
  235.8 3.4 %collective-permute-start.53 = (bf16[96,768]{1,0:T(8,128)(2,1)}, bf16[96,768]{1,0:T(8,128)(2,1)S(1)}, u32[]{:S(2)}, u32[]{:S(2)}) collective-permute-start(bf16[96,768]{1,0:T(8,128)(2,1)} %fusion.17), channel_id=1, source_target_pairs={{0,3},{1,0},{2,1},{3,2},{4,7},{5,4},{6,5},{7,6},{8,11},{9,8},{10,9... | collective-permute-start | bytes 442376 | tf_op jit(solution)/shard_map/ppermute | solution.py:52
  240.4 3.9 %collective-permute-done.51 = bf16[96,768]{1,0:T(8,128)(2,1)S(1)} collective-permute-done((bf16[96,768]{1,0:T(8,128)(2,1)}, bf16[96,768]{1,0:T(8,128)(2,1)S(1)}, u32[]{:S(2)}, u32[]{:S(2)}) %collective-permute-start.51) | collective-permute-done | bytes 147488 | tf_op jit(solution)/shard_map/ppermute | solution.py:52
  244.3 3.7 %collective-permute-done.52 = bf16[96,768]{1,0:T(8,128)(2,1)S(1)} collective-permute-done((bf16[96,768]{1,0:T(8,128)(2,1)}, bf16[96,768]{1,0:T(8,128)(2,1)S(1)}, u32[]{:S(2)}, u32[]{:S(2)}) %collective-permute-start.52) | collective-permute-done | bytes 147488 | tf_op jit(solution)/shard_map/ppermute | solution.py:52
  248.0 7.0 %collective-permute-done.50 = bf16[2,192,768]{2,1,0:T(8,128)(2,1)} collective-permute-done((bf16[2,192,768]{2,1,0:T(8,128)(2,1)}, bf16[2,192,768]{2,1,0:T(8,128)(2,1)}, u32[]{:S(2)}, u32[]{:S(2)}) %collective-permute-start.50) | collective-permute-done | bytes 589856 | tf_op jit(solution)/shard_map/ppermute | solution.py:47
  256.1 2.0 collective-permute-start.54
  258.1 3.8 %collective-permute-start.58 = (bf16[112,768]{1,0:T(8,128)(2,1)S(1)}, bf16[112,768]{1,0:T(8,128)(2,1)S(1)}, u32[]{:S(2)}, u32[]{:S(2)}) collective-permute-start(bf16[112,768]{1,0:T(8,128)(2,1)S(1)} %pad_maximum_fusion.10), channel_id=1, source_target_pairs={{0,3},{1,0},{2,1},{3,2},{4,7},{5,4},{6,5},{7,6},{8,11},{9,8},{10,9... | collective-permute-start | bytes 516104 | tf_op jit(solution)/shard_map/ppermute | solution.py:52
  263.2 2.3 collective-permute-done.56
  265.5 2.9 collective-permute-done.57
  268.4 2.8 collective-permute-done.54
  273.6 2.3 collective-permute-start.60
  276.9 3.6 %convert_add_fusion.3 = (f32[4,128,768]{2,1,0:T(8,128)}, f32[4,128,768]{2,1,0:T(8,128)}) fusion(bf16[4,128,768]{2,1,0:T(8,128)(2,1)S(1)} %bitcast.129, bf16[4,128,1536]{2,1,0:T(8,128)(2,1)} %bitcast.133, bf16[4,128,768]{2,1,0:T(8,128)(2,1)} %bitcast.132), kind=kLoop, calls=%fused_computation.4 | loop fusion | flops 2359296 | bytes 6291456 | tf_op jit(solution)/shard_map/add | solution.py:1161
  280.5 2.8 shard_map.153
  284.0 3.2 %shard_map.152 = (f32[2,768,768]{2,1,0:T(8,128)}, f32[2,768,768]{2,1,0:T(8,128)}) custom-call(s32[5]{0:T(128)S(1)} %stack.80.place_ref.spot_ref, bf16[4,192,768]{2,1,0:T(8,128)(2,1)S(1)} %bitcast.122, bf16[4,192,768]{2,1,0:T(8,128)(2,1)S(1)} %collective-permute-done.61.got_ref), custom_call_target="tpu_custom_call" | custom-call | flops 200000000 | tf_op jit(solution)/shard_map/pallas_call | solution.py:480
  287.1 1.8 collective-permute-done.59.got_ref
  289.6 2.8 shard_map.154
  292.5 3.2 %shard_map.155 = (f32[2,768,768]{2,1,0:T(8,128)}, f32[2,768,768]{2,1,0:T(8,128)}) custom-call(s32[5]{0:T(128)S(1)} %stack.80.place_ref.spot_ref, bf16[4,192,768]{2,1,0:T(8,128)(2,1)S(1)} %constant_dynamic-update-slice_fusion.mine_ref, bf16[4,192,768]{2,1,0:T(8,128)(2,1)S(1)} %collective-permute-done.63.got_ref, ...), custom_call_target="tpu_custom_call", output_to_operand_aliasing={{0}: (3, {}), {1}: (4, {})} | custom-call | flops 200000000 | tf_op jit(solution)/shard_map/pallas_call | solution.py:480
  (235 shorter events, 43.3 us)
Async XLA Ops:
  7.2 264.8 %all-gather.3.cloned.1.call-start = ((), (), s32[]{:S(2)}) async-start(), calls=%async_computation | async-start | bytes 1966080 | tf_op jit(solution)/shard_map/all_gather | solution.py:1119
  10.4 21.8 %collective-permute-start = (bf16[128,768]{1,0:T(8,128)(2,1)}, bf16[128,768]{1,0:T(8,128)(2,1)}, u32[]{:S(2)}, u32[]{:S(2)}) collective-permute-start(bf16[128,768]{1,0:T(8,128)(2,1)} %shard_map.135.refs_0_), channel_id=1, source_target_pairs={{0,1},{1,2},{2,3},{3,0},{4,5},{5,6},{6,7},{7,4},{8,9},{9,10},{10,1... | collective-permute-start | bytes 589832 | tf_op jit(solution)/shard_map/ppermute | solution.py:52
  13.4 18.8 %collective-permute-start.1 = (bf16[128,768]{1,0:T(8,128)(2,1)}, bf16[128,768]{1,0:T(8,128)(2,1)}, u32[]{:S(2)}, u32[]{:S(2)}) collective-permute-start(bf16[128,768]{1,0:T(8,128)(2,1)} %shard_map.135.refs_0_), channel_id=1, source_target_pairs={{0,2},{1,3},{2,0},{3,1},{4,6},{5,7},{6,4},{7,5},{8,10},{9,11},{10,... | collective-permute-start | bytes 589832 | tf_op jit(solution)/shard_map/ppermute | solution.py:52
  16.0 16.2 %collective-permute-start.2 = (bf16[128,768]{1,0:T(8,128)(2,1)}, bf16[128,768]{1,0:T(8,128)(2,1)}, u32[]{:S(2)}, u32[]{:S(2)}) collective-permute-start(bf16[128,768]{1,0:T(8,128)(2,1)} %shard_map.135.refs_0_), channel_id=1, source_target_pairs={{0,3},{1,0},{2,1},{3,2},{4,7},{5,4},{6,5},{7,6},{8,11},{9,8},{10,9... | collective-permute-start | bytes 589832 | tf_op jit(solution)/shard_map/ppermute | solution.py:52
  20.3 27.2 %collective-permute-start.7 = (bf16[4,192,768]{2,1,0:T(8,128)(2,1)}, bf16[4,192,768]{2,1,0:T(8,128)(2,1)}, u32[]{:S(2)}, u32[]{:S(2)}) collective-permute-start(bf16[4,192,768]{2,1,0:T(8,128)(2,1)} %pad_maximum_fusion.1), channel_id=1, source_target_pairs={{0,8},{4,12},{8,0},{12,4},{1,9},{5,13},{9,1},{13,5},{2,10},{6,14},... | collective-permute-start | bytes 3538952 | tf_op jit(solution)/shard_map/ppermute | solution.py:47
  37.1 10.4 %collective-permute-start.6 = (bf16[512,768]{1,0:T(8,128)(2,1)S(1)}, bf16[512,768]{1,0:T(8,128)(2,1)S(1)}, u32[]{:S(2)}, u32[]{:S(2)}) collective-permute-start(bf16[512,768]{1,0:T(8,128)(2,1)S(1)} %get-tuple-element.179.refs_0_.own_act.x_ref), channel_id=1, source_target_pairs={{0,4},{4,0},{8,12},{12,8},{1,5},{5,1},{9,13},{13,9},{2,6},{6,2},{1... | collective-permute-start | bytes 2359304 | tf_op jit(solution)/shard_map/ppermute | solution.py:47
  37.1 22.4 %collective-permute-start.3 = (bf16[128,768]{1,0:T(8,128)(2,1)S(1)}, bf16[128,768]{1,0:T(8,128)(2,1)S(1)}, u32[]{:S(2)}, u32[]{:S(2)}) collective-permute-start(bf16[128,768]{1,0:T(8,128)(2,1)S(1)} %get-tuple-element.176), channel_id=1, source_target_pairs={{0,3},{1,0},{2,1},{3,2},{4,7},{5,4},{6,5},{7,6},{8,11},{9,8},{10,9... | collective-permute-start | bytes 589832 | tf_op jit(solution)/shard_map/ppermute | solution.py:52
  39.7 19.8 %collective-permute-start.4 = (bf16[128,768]{1,0:T(8,128)(2,1)S(1)}, bf16[128,768]{1,0:T(8,128)(2,1)S(1)}, u32[]{:S(2)}, u32[]{:S(2)}) collective-permute-start(bf16[128,768]{1,0:T(8,128)(2,1)S(1)} %get-tuple-element.177), channel_id=1, source_target_pairs={{0,2},{1,3},{2,0},{3,1},{4,6},{5,7},{6,4},{7,5},{8,10},{9,11},{10,... | collective-permute-start | bytes 589832 | tf_op jit(solution)/shard_map/ppermute | solution.py:52
  40.2 19.3 %collective-permute-start.5 = (bf16[128,768]{1,0:T(8,128)(2,1)S(1)}, bf16[128,768]{1,0:T(8,128)(2,1)S(1)}, u32[]{:S(2)}, u32[]{:S(2)}) collective-permute-start(bf16[128,768]{1,0:T(8,128)(2,1)S(1)} %get-tuple-element.178), channel_id=1, source_target_pairs={{0,1},{1,2},{2,3},{3,0},{4,5},{5,6},{6,7},{7,4},{8,9},{9,10},{10,1... | collective-permute-start | bytes 589832 | tf_op jit(solution)/shard_map/ppermute | solution.py:52
  57.9 29.4 %collective-permute-start.16 = (bf16[4,192,768]{2,1,0:T(8,128)(2,1)S(1)}, bf16[4,192,768]{2,1,0:T(8,128)(2,1)S(1)}, u32[]{:S(2)}, u32[]{:S(2)}) collective-permute-start(bf16[4,192,768]{2,1,0:T(8,128)(2,1)S(1)} %pad_maximum_fusion), channel_id=1, source_target_pairs={{0,8},{4,12},{8,0},{12,4},{1,9},{5,13},{9,1},{13,5},{2,10},{6,14},... | collective-permute-start | bytes 3538952 | tf_op jit(solution)/shard_map/ppermute | solution.py:47
  60.4 9.7 %collective-permute-start.9 = (bf16[128,768]{1,0:T(8,128)(2,1)S(1)}, bf16[128,768]{1,0:T(8,128)(2,1)S(1)}, u32[]{:S(2)}, u32[]{:S(2)}) collective-permute-start(bf16[128,768]{1,0:T(8,128)(2,1)S(1)} %get-tuple-element.187.refs_0_), channel_id=1, source_target_pairs={{0,1},{1,2},{2,3},{3,0},{4,5},{5,6},{6,7},{7,4},{8,9},{9,10},{10,1... | collective-permute-start | bytes 589832 | tf_op jit(solution)/shard_map/ppermute | solution.py:52
  61.1 16.7 %collective-permute-start.10 = (bf16[128,768]{1,0:T(8,128)(2,1)S(1)}, bf16[128,768]{1,0:T(8,128)(2,1)S(1)}, u32[]{:S(2)}, u32[]{:S(2)}) collective-permute-start(bf16[128,768]{1,0:T(8,128)(2,1)S(1)} %get-tuple-element.187.refs_0_), channel_id=1, source_target_pairs={{0,2},{1,3},{2,0},{3,1},{4,6},{5,7},{6,4},{7,5},{8,10},{9,11},{10,... | collective-permute-start | bytes 589832 | tf_op jit(solution)/shard_map/ppermute | solution.py:52
  61.5 16.3 %collective-permute-start.11 = (bf16[128,768]{1,0:T(8,128)(2,1)S(1)}, bf16[128,768]{1,0:T(8,128)(2,1)S(1)}, u32[]{:S(2)}, u32[]{:S(2)}) collective-permute-start(bf16[128,768]{1,0:T(8,128)(2,1)S(1)} %get-tuple-element.187.refs_0_), channel_id=1, source_target_pairs={{0,3},{1,0},{2,1},{3,2},{4,7},{5,4},{6,5},{7,6},{8,11},{9,8},{10,9... | collective-permute-start | bytes 589832 | tf_op jit(solution)/shard_map/ppermute | solution.py:52
  80.6 6.7 %collective-permute-start.15 = (bf16[512,768]{1,0:T(8,128)(2,1)S(1)}, bf16[512,768]{1,0:T(8,128)(2,1)S(1)}, u32[]{:S(2)}, u32[]{:S(2)}) collective-permute-start(bf16[512,768]{1,0:T(8,128)(2,1)S(1)} %get-tuple-element.188.refs_0_.x_ref.own_act), channel_id=1, source_target_pairs={{0,4},{4,0},{8,12},{12,8},{1,5},{5,1},{9,13},{13,9},{2,6},{6,2},{1... | collective-permute-start | bytes 2359304 | tf_op jit(solution)/shard_map/ppermute | solution.py:47
  80.7 25.1 %collective-permute-start.12 = (bf16[128,768]{1,0:T(8,128)(2,1)S(1)}, bf16[128,768]{1,0:T(8,128)(2,1)S(1)}, u32[]{:S(2)}, u32[]{:S(2)}) collective-permute-start(bf16[128,768]{1,0:T(8,128)(2,1)S(1)} %copy-done.4), channel_id=1, source_target_pairs={{0,1},{1,2},{2,3},{3,0},{4,5},{5,6},{6,7},{7,4},{8,9},{9,10},{10,1... | collective-permute-start | bytes 589832 | tf_op jit(solution)/shard_map/ppermute | solution.py:52
  84.9 20.9 %collective-permute-start.13 = (bf16[128,768]{1,0:T(8,128)(2,1)S(1)}, bf16[128,768]{1,0:T(8,128)(2,1)S(1)}, u32[]{:S(2)}, u32[]{:S(2)}) collective-permute-start(bf16[128,768]{1,0:T(8,128)(2,1)S(1)} %copy-done.4), channel_id=1, source_target_pairs={{0,2},{1,3},{2,0},{3,1},{4,6},{5,7},{6,4},{7,5},{8,10},{9,11},{10,... | collective-permute-start | bytes 589832 | tf_op jit(solution)/shard_map/ppermute | solution.py:52
  84.9 20.9 %collective-permute-start.14 = (bf16[128,768]{1,0:T(8,128)(2,1)S(1)}, bf16[128,768]{1,0:T(8,128)(2,1)S(1)}, u32[]{:S(2)}, u32[]{:S(2)}) collective-permute-start(bf16[128,768]{1,0:T(8,128)(2,1)S(1)} %copy-done.4), channel_id=1, source_target_pairs={{0,3},{1,0},{2,1},{3,2},{4,7},{5,4},{6,5},{7,6},{8,11},{9,8},{10,9... | collective-permute-start | bytes 589832 | tf_op jit(solution)/shard_map/ppermute | solution.py:52
  105.7 2.4 collective-permute-start.17
  108.9 10.2 %collective-permute-start.18 = (bf16[128,768]{1,0:T(8,128)(2,1)S(1)}, bf16[128,768]{1,0:T(8,128)(2,1)S(1)}, u32[]{:S(2)}, u32[]{:S(2)}) collective-permute-start(bf16[128,768]{1,0:T(8,128)(2,1)S(1)} %get-tuple-element.201), channel_id=1, source_target_pairs={{0,3},{1,0},{2,1},{3,2},{4,7},{5,4},{6,5},{7,6},{8,11},{9,8},{10,9... | collective-permute-start | bytes 589832 | tf_op jit(solution)/shard_map/ppermute | solution.py:52
  110.9 8.2 %collective-permute-start.19 = (bf16[128,768]{1,0:T(8,128)(2,1)S(1)}, bf16[128,768]{1,0:T(8,128)(2,1)S(1)}, u32[]{:S(2)}, u32[]{:S(2)}) collective-permute-start(bf16[128,768]{1,0:T(8,128)(2,1)S(1)} %get-tuple-element.202), channel_id=1, source_target_pairs={{0,4},{4,0},{8,12},{12,8},{1,5},{5,1},{9,13},{13,9},{2,6},{6,2},{1... | collective-permute-start | bytes 589832 | tf_op jit(solution)/shard_map/ppermute | solution.py:47
  110.9 16.8 %collective-permute-start.20 = (bf16[128,768]{1,0:T(8,128)(2,1)S(1)}, bf16[128,768]{1,0:T(8,128)(2,1)S(1)}, u32[]{:S(2)}, u32[]{:S(2)}) collective-permute-start(bf16[128,768]{1,0:T(8,128)(2,1)S(1)} %get-tuple-element.214), channel_id=1, source_target_pairs={{0,2},{1,3},{2,0},{3,1},{4,6},{5,7},{6,4},{7,5},{8,10},{9,11},{10,... | collective-permute-start | bytes 589832 | tf_op jit(solution)/shard_map/ppermute | solution.py:52
  110.9 16.8 %collective-permute-start.21 = (bf16[128,768]{1,0:T(8,128)(2,1)S(1)}, bf16[128,768]{1,0:T(8,128)(2,1)S(1)}, u32[]{:S(2)}, u32[]{:S(2)}) collective-permute-start(bf16[128,768]{1,0:T(8,128)(2,1)S(1)} %get-tuple-element.215), channel_id=1, source_target_pairs={{0,1},{1,2},{2,3},{3,0},{4,5},{5,6},{6,7},{7,4},{8,9},{9,10},{10,1... | collective-permute-start | bytes 589832 | tf_op jit(solution)/shard_map/ppermute | solution.py:52
  128.7 6.3 %collective-permute-start.24 = (bf16[128,768]{1,0:T(8,128)(2,1)S(1)}, bf16[128,768]{1,0:T(8,128)(2,1)S(1)}, u32[]{:S(2)}, u32[]{:S(2)}) collective-permute-start(bf16[128,768]{1,0:T(8,128)(2,1)S(1)} %get-tuple-element.216.refs_0_.g_own), channel_id=1, source_target_pairs={{0,4},{4,0},{8,12},{12,8},{1,5},{5,1},{9,13},{13,9},{2,6},{6,2},{1... | collective-permute-start | bytes 589832 | tf_op jit(solution)/shard_map/ppermute | solution.py:47
  128.8 22.6 %collective-permute-start.22 = (bf16[128,768]{1,0:T(8,128)(2,1)S(1)}, bf16[128,768]{1,0:T(8,128)(2,1)S(1)}, u32[]{:S(2)}, u32[]{:S(2)}) collective-permute-start(bf16[128,768]{1,0:T(8,128)(2,1)S(1)} %get-tuple-element.216.refs_0_.g_own), channel_id=1, source_target_pairs={{0,1},{1,2},{2,3},{3,0},{4,5},{5,6},{6,7},{7,4},{8,9},{9,10},{10,1... | collective-permute-start | bytes 589832 | tf_op jit(solution)/shard_map/ppermute | solution.py:52
  130.2 22.1 %collective-permute-start.28 = (bf16[128,768]{1,0:T(8,128)(2,1)S(1)}, bf16[128,768]{1,0:T(8,128)(2,1)S(1)}, u32[]{:S(2)}, u32[]{:S(2)}) collective-permute-start(bf16[128,768]{1,0:T(8,128)(2,1)S(1)} %get-tuple-element.216.refs_0_.g_own), channel_id=1, source_target_pairs={{0,2},{1,3},{2,0},{3,1},{4,6},{5,7},{6,4},{7,5},{8,10},{9,11},{10,... | collective-permute-start | bytes 589832 | tf_op jit(solution)/shard_map/ppermute | solution.py:52
  132.1 21.7 %collective-permute-start.29 = (bf16[128,768]{1,0:T(8,128)(2,1)S(1)}, bf16[128,768]{1,0:T(8,128)(2,1)S(1)}, u32[]{:S(2)}, u32[]{:S(2)}) collective-permute-start(bf16[128,768]{1,0:T(8,128)(2,1)S(1)} %get-tuple-element.216.refs_0_.g_own), channel_id=1, source_target_pairs={{0,3},{1,0},{2,1},{3,2},{4,7},{5,4},{6,5},{7,6},{8,11},{9,8},{10,9... | collective-permute-start | bytes 589832 | tf_op jit(solution)/shard_map/ppermute | solution.py:52
  135.0 16.1 %collective-permute-start.23 = (bf16[2,2,192,768]{3,2,1,0:T(8,128)(2,1)S(1)}, bf16[2,2,192,768]{3,2,1,0:T(8,128)(2,1)S(1)}, u32[]{:S(2)}, u32[]{:S(2)}) collective-permute-start(bf16[2,2,192,768]{3,2,1,0:T(8,128)(2,1)S(1)} %get-tuple-element.217), channel_id=1, source_target_pairs={{0,4},{4,0},{8,12},{12,8},{1,5},{5,1},{9,13},{13,9},{2,6},{6,2},{1... | collective-permute-start | bytes 3538952 | tf_op jit(solution)/shard_map/ppermute | solution.py:47
  135.0 28.8 %collective-permute-start.26 = (bf16[2,4,96,768]{3,2,1,0:T(8,128)(2,1)S(1)}, bf16[2,4,96,768]{3,2,1,0:T(8,128)(2,1)S(1)}, u32[]{:S(2)}, u32[]{:S(2)}) collective-permute-start(bf16[2,4,96,768]{3,2,1,0:T(8,128)(2,1)S(1)} %get-tuple-element.232), channel_id=1, source_target_pairs={{0,8},{4,12},{8,0},{12,4},{1,9},{5,13},{9,1},{13,5},{2,10},{6,14},... | collective-permute-start | bytes 3538952 | tf_op jit(solution)/shard_map/ppermute | solution.py:47
  151.1 3.6 %collective-permute-start.30 = (bf16[512,768]{1,0:T(8,128)(2,1)S(1)}, bf16[512,768]{1,0:T(8,128)(2,1)S(1)}, u32[]{:S(2)}, u32[]{:S(2)}) collective-permute-start(bf16[512,768]{1,0:T(8,128)(2,1)S(1)} %get-tuple-element.240), channel_id=1, source_target_pairs={{0,4},{4,0},{8,12},{12,8},{1,5},{5,1},{9,13},{13,9},{2,6},{6,2},{1... | collective-permute-start | bytes 2359304 | tf_op jit(solution)/shard_map/ppermute | solution.py:47
  151.4 44.2 %collective-permute-start.25 = (bf16[2,4,96,768]{3,2,1,0:T(8,128)(2,1)S(1)}, bf16[2,4,96,768]{3,2,1,0:T(8,128)(2,1)S(1)}, u32[]{:S(2)}, u32[]{:S(2)}) collective-permute-start(bf16[2,4,96,768]{3,2,1,0:T(8,128)(2,1)S(1)} %get-tuple-element.229), channel_id=1, source_target_pairs={{0,8},{4,12},{8,0},{12,4},{1,9},{5,13},{9,1},{13,5},{2,10},{6,14},... | collective-permute-start | bytes 3538952 | tf_op jit(solution)/shard_map/ppermute | solution.py:47
  152.3 15.3 %collective-permute-start.27 = (bf16[2,192,768]{2,1,0:T(8,128)(2,1)S(1)}, bf16[2,192,768]{2,1,0:T(8,128)(2,1)S(1)}, u32[]{:S(2)}, u32[]{:S(2)}) collective-permute-start(bf16[2,192,768]{2,1,0:T(8,128)(2,1)S(1)} %fusion.3), channel_id=1, source_target_pairs={{0,16},{16,0},{1,17},{17,1},{2,18},{18,2},{3,19},{19,3},{4,20},{20... | collective-permute-start | bytes 1769480 | tf_op jit(solution)/shard_map/ppermute | solution.py:204
  155.8 11.7 %collective-permute-start.32 = (bf16[128,768]{1,0:T(8,128)(2,1)S(1)}, bf16[128,768]{1,0:T(8,128)(2,1)S(1)}, u32[]{:S(2)}, u32[]{:S(2)}) collective-permute-start(bf16[128,768]{1,0:T(8,128)(2,1)S(1)} %get-tuple-element.247), channel_id=1, source_target_pairs={{0,3},{1,0},{2,1},{3,2},{4,7},{5,4},{6,5},{7,6},{8,11},{9,8},{10,9... | collective-permute-start | bytes 589832 | tf_op jit(solution)/shard_map/ppermute | solution.py:52
  156.4 17.2 %collective-permute-start.34 = (bf16[128,768]{1,0:T(8,128)(2,1)S(1)}, bf16[128,768]{1,0:T(8,128)(2,1)S(1)}, u32[]{:S(2)}, u32[]{:S(2)}) collective-permute-start(bf16[128,768]{1,0:T(8,128)(2,1)S(1)} %get-tuple-element.254), channel_id=1, source_target_pairs={{0,2},{1,3},{2,0},{3,1},{4,6},{5,7},{6,4},{7,5},{8,10},{9,11},{10,... | collective-permute-start | bytes 589832 | tf_op jit(solution)/shard_map/ppermute | solution.py:52
  163.8 9.8 %collective-permute-start.35 = (bf16[128,768]{1,0:T(8,128)(2,1)S(1)}, bf16[128,768]{1,0:T(8,128)(2,1)S(1)}, u32[]{:S(2)}, u32[]{:S(2)}) collective-permute-start(bf16[128,768]{1,0:T(8,128)(2,1)S(1)} %get-tuple-element.255), channel_id=1, source_target_pairs={{0,1},{1,2},{2,3},{3,0},{4,5},{5,6},{6,7},{7,4},{8,9},{9,10},{10,1... | collective-permute-start | bytes 589832 | tf_op jit(solution)/shard_map/ppermute | solution.py:52
  167.9 14.4 %collective-permute-start.31 = (bf16[4,96,768]{2,1,0:T(8,128)(2,1)S(1)}, bf16[4,96,768]{2,1,0:T(8,128)(2,1)S(1)}, u32[]{:S(2)}, u32[]{:S(2)}) collective-permute-start(bf16[4,96,768]{2,1,0:T(8,128)(2,1)S(1)} %fusion.4), channel_id=1, source_target_pairs={{0,16},{16,0},{1,17},{17,1},{2,18},{18,2},{3,19},{19,3},{4,20},{20... | collective-permute-start | bytes 1769480 | tf_op jit(solution)/shard_map/ppermute | solution.py:204
  169.5 26.2 %collective-permute-start.33 = (bf16[2,2,192,768]{3,2,1,0:T(8,128)(2,1)S(1)}, bf16[2,2,192,768]{3,2,1,0:T(8,128)(2,1)S(1)}, u32[]{:S(2)}, u32[]{:S(2)}) collective-permute-start(bf16[2,2,192,768]{3,2,1,0:T(8,128)(2,1)S(1)} %get-tuple-element.250), channel_id=1, source_target_pairs={{0,4},{4,0},{8,12},{12,8},{1,5},{5,1},{9,13},{13,9},{2,6},{6,2},{1... | collective-permute-start | bytes 3538952 | tf_op jit(solution)/shard_map/ppermute | solution.py:47
  175.3 7.2 %collective-permute-start.36 = (bf16[128,768]{1,0:T(8,128)(2,1)S(1)}, bf16[128,768]{1,0:T(8,128)(2,1)S(1)}, u32[]{:S(2)}, u32[]{:S(2)}) collective-permute-start(bf16[128,768]{1,0:T(8,128)(2,1)S(1)} %get-tuple-element.260), channel_id=1, source_target_pairs={{0,3},{1,0},{2,1},{3,2},{4,7},{5,4},{6,5},{7,6},{8,11},{9,8},{10,9... | collective-permute-start | bytes 589832 | tf_op jit(solution)/shard_map/ppermute | solution.py:52
  176.0 19.6 %collective-permute-start.37 = (bf16[128,768]{1,0:T(8,128)(2,1)S(1)}, bf16[128,768]{1,0:T(8,128)(2,1)S(1)}, u32[]{:S(2)}, u32[]{:S(2)}) collective-permute-start(bf16[128,768]{1,0:T(8,128)(2,1)S(1)} %get-tuple-element.261), channel_id=1, source_target_pairs={{0,2},{1,3},{2,0},{3,1},{4,6},{5,7},{6,4},{7,5},{8,10},{9,11},{10,... | collective-permute-start | bytes 589832 | tf_op jit(solution)/shard_map/ppermute | solution.py:52
  182.4 13.3 %collective-permute-start.38 = (bf16[128,768]{1,0:T(8,128)(2,1)S(1)}, bf16[128,768]{1,0:T(8,128)(2,1)S(1)}, u32[]{:S(2)}, u32[]{:S(2)}) collective-permute-start(bf16[128,768]{1,0:T(8,128)(2,1)S(1)} %get-tuple-element.262), channel_id=1, source_target_pairs={{0,1},{1,2},{2,3},{3,0},{4,5},{5,6},{6,7},{7,4},{8,9},{9,10},{10,1... | collective-permute-start | bytes 589832 | tf_op jit(solution)/shard_map/ppermute | solution.py:52
  196.2 15.2 %collective-permute-start.39 = (bf16[4,96,768]{2,1,0:T(8,128)(2,1)S(1)}, bf16[4,96,768]{2,1,0:T(8,128)(2,1)S(1)}, u32[]{:S(2)}, u32[]{:S(2)}) collective-permute-start(bf16[4,96,768]{2,1,0:T(8,128)(2,1)S(1)} %fusion.5), channel_id=1, source_target_pairs={{0,16},{16,0},{1,17},{17,1},{2,18},{18,2},{3,19},{19,3},{4,20},{20... | collective-permute-start | bytes 1769480 | tf_op jit(solution)/shard_map/ppermute | solution.py:204
  196.9 14.5 %collective-permute-start.40 = (bf16[192,768]{1,0:T(8,128)(2,1)S(1)}, bf16[192,768]{1,0:T(8,128)(2,1)S(1)}, u32[]{:S(2)}, u32[]{:S(2)}) collective-permute-start(bf16[192,768]{1,0:T(8,128)(2,1)S(1)} %fusion.9), channel_id=1, source_target_pairs={{0,8},{4,12},{8,0},{12,4},{1,9},{5,13},{9,1},{13,5},{2,10},{6,14},... | collective-permute-start | bytes 884744 | tf_op jit(solution)/shard_map/ppermute | solution.py:47
  198.2 5.8 %collective-permute-start.41 = (bf16[96,768]{1,0:T(8,128)(2,1)S(1)}, bf16[96,768]{1,0:T(8,128)(2,1)S(1)}, u32[]{:S(2)}, u32[]{:S(2)}) collective-permute-start(bf16[96,768]{1,0:T(8,128)(2,1)S(1)} %get-tuple-element.268), channel_id=1, source_target_pairs={{0,3},{1,0},{2,1},{3,2},{4,7},{5,4},{6,5},{7,6},{8,11},{9,8},{10,9... | collective-permute-start | bytes 442376 | tf_op jit(solution)/shard_map/ppermute | solution.py:52
  198.2 13.2 %collective-permute-start.42 = (bf16[96,768]{1,0:T(8,128)(2,1)S(1)}, bf16[96,768]{1,0:T(8,128)(2,1)S(1)}, u32[]{:S(2)}, u32[]{:S(2)}) collective-permute-start(bf16[96,768]{1,0:T(8,128)(2,1)S(1)} %get-tuple-element.269), channel_id=1, source_target_pairs={{0,2},{1,3},{2,0},{3,1},{4,6},{5,7},{6,4},{7,5},{8,10},{9,11},{10,... | collective-permute-start | bytes 442376 | tf_op jit(solution)/shard_map/ppermute | solution.py:52
  198.4 12.9 %collective-permute-start.43 = (bf16[96,768]{1,0:T(8,128)(2,1)S(1)}, bf16[96,768]{1,0:T(8,128)(2,1)S(1)}, u32[]{:S(2)}, u32[]{:S(2)}) collective-permute-start(bf16[96,768]{1,0:T(8,128)(2,1)S(1)} %get-tuple-element.270), channel_id=1, source_target_pairs={{0,1},{1,2},{2,3},{3,0},{4,5},{5,6},{6,7},{7,4},{8,9},{9,10},{10,1... | collective-permute-start | bytes 442376 | tf_op jit(solution)/shard_map/ppermute | solution.py:52
  211.6 18.6 %collective-permute-start.44 = (bf16[400,768]{1,0:T(8,128)(2,1)S(1)}, bf16[400,768]{1,0:T(8,128)(2,1)S(1)}, u32[]{:S(2)}, u32[]{:S(2)}) collective-permute-start(bf16[400,768]{1,0:T(8,128)(2,1)S(1)} %pad_maximum_fusion.3), channel_id=1, source_target_pairs={{0,8},{4,12},{8,0},{12,4},{1,9},{5,13},{9,1},{13,5},{2,10},{6,14},... | collective-permute-start | bytes 1843208 | tf_op jit(solution)/shard_map/ppermute | solution.py:47
  212.6 17.6 %collective-permute-start.45 = (bf16[192,768]{1,0:T(8,128)(2,1)S(1)}, bf16[192,768]{1,0:T(8,128)(2,1)S(1)}, u32[]{:S(2)}, u32[]{:S(2)}) collective-permute-start(bf16[192,768]{1,0:T(8,128)(2,1)S(1)} %fusion.8), channel_id=1, source_target_pairs={{0,16},{16,0},{1,17},{17,1},{2,18},{18,2},{3,19},{19,3},{4,20},{20... | collective-permute-start | bytes 884744 | tf_op jit(solution)/shard_map/ppermute | solution.py:204
  214.4 5.5 %collective-permute-start.46 = (bf16[96,768]{1,0:T(8,128)(2,1)S(1)}, bf16[96,768]{1,0:T(8,128)(2,1)S(1)}, u32[]{:S(2)}, u32[]{:S(2)}) collective-permute-start(bf16[96,768]{1,0:T(8,128)(2,1)S(1)} %get-tuple-element.279), channel_id=1, source_target_pairs={{0,3},{1,0},{2,1},{3,2},{4,7},{5,4},{6,5},{7,6},{8,11},{9,8},{10,9... | collective-permute-start | bytes 442376 | tf_op jit(solution)/shard_map/ppermute | solution.py:52
  215.1 15.1 %collective-permute-start.47 = (bf16[96,768]{1,0:T(8,128)(2,1)S(1)}, bf16[96,768]{1,0:T(8,128)(2,1)S(1)}, u32[]{:S(2)}, u32[]{:S(2)}) collective-permute-start(bf16[96,768]{1,0:T(8,128)(2,1)S(1)} %get-tuple-element.280), channel_id=1, source_target_pairs={{0,2},{1,3},{2,0},{3,1},{4,6},{5,7},{6,4},{7,5},{8,10},{9,11},{10,... | collective-permute-start | bytes 442376 | tf_op jit(solution)/shard_map/ppermute | solution.py:52
  217.3 12.9 %collective-permute-start.48 = (bf16[96,768]{1,0:T(8,128)(2,1)S(1)}, bf16[96,768]{1,0:T(8,128)(2,1)S(1)}, u32[]{:S(2)}, u32[]{:S(2)}) collective-permute-start(bf16[96,768]{1,0:T(8,128)(2,1)S(1)} %get-tuple-element.281), channel_id=1, source_target_pairs={{0,1},{1,2},{2,3},{3,0},{4,5},{5,6},{6,7},{7,4},{8,9},{9,10},{10,1... | collective-permute-start | bytes 442376 | tf_op jit(solution)/shard_map/ppermute | solution.py:52
  232.8 22.3 %collective-permute-start.50 = (bf16[2,192,768]{2,1,0:T(8,128)(2,1)}, bf16[2,192,768]{2,1,0:T(8,128)(2,1)}, u32[]{:S(2)}, u32[]{:S(2)}) collective-permute-start(bf16[2,192,768]{2,1,0:T(8,128)(2,1)} %get-tuple-element.291), channel_id=1, source_target_pairs={{0,8},{4,12},{8,0},{12,4},{1,9},{5,13},{9,1},{13,5},{2,10},{6,14},... | collective-permute-start | bytes 1769480 | tf_op jit(solution)/shard_map/ppermute | solution.py:47
  234.9 13.2 %collective-permute-start.49 = (bf16[208,768]{1,0:T(8,128)(2,1)}, bf16[208,768]{1,0:T(8,128)(2,1)S(1)}, u32[]{:S(2)}, u32[]{:S(2)}) collective-permute-start(bf16[208,768]{1,0:T(8,128)(2,1)} %pad_maximum_fusion.9), channel_id=1, source_target_pairs={{0,16},{16,0},{1,17},{17,1},{2,18},{18,2},{3,19},{19,3},{4,20},{20... | collective-permute-start | bytes 958472 | tf_op jit(solution)/shard_map/ppermute | solution.py:204
  235.4 8.9 %collective-permute-start.51 = (bf16[96,768]{1,0:T(8,128)(2,1)}, bf16[96,768]{1,0:T(8,128)(2,1)S(1)}, u32[]{:S(2)}, u32[]{:S(2)}) collective-permute-start(bf16[96,768]{1,0:T(8,128)(2,1)} %fusion.17), channel_id=1, source_target_pairs={{0,1},{1,2},{2,3},{3,0},{4,5},{5,6},{6,7},{7,4},{8,9},{9,10},{10,1... | collective-permute-start | bytes 442376 | tf_op jit(solution)/shard_map/ppermute | solution.py:52
  235.4 12.6 %collective-permute-start.52 = (bf16[96,768]{1,0:T(8,128)(2,1)}, bf16[96,768]{1,0:T(8,128)(2,1)S(1)}, u32[]{:S(2)}, u32[]{:S(2)}) collective-permute-start(bf16[96,768]{1,0:T(8,128)(2,1)} %fusion.17), channel_id=1, source_target_pairs={{0,2},{1,3},{2,0},{3,1},{4,6},{5,7},{6,4},{7,5},{8,10},{9,11},{10,... | collective-permute-start | bytes 442376 | tf_op jit(solution)/shard_map/ppermute | solution.py:52
  235.8 12.2 %collective-permute-start.53 = (bf16[96,768]{1,0:T(8,128)(2,1)}, bf16[96,768]{1,0:T(8,128)(2,1)S(1)}, u32[]{:S(2)}, u32[]{:S(2)}) collective-permute-start(bf16[96,768]{1,0:T(8,128)(2,1)} %fusion.17), channel_id=1, source_target_pairs={{0,3},{1,0},{2,1},{3,2},{4,7},{5,4},{6,5},{7,6},{8,11},{9,8},{10,9... | collective-permute-start | bytes 442376 | tf_op jit(solution)/shard_map/ppermute | solution.py:52
  256.0 15.2 %collective-permute-start.55 = (bf16[4,96,768]{2,1,0:T(8,128)(2,1)S(1)}, bf16[4,96,768]{2,1,0:T(8,128)(2,1)S(1)}, u32[]{:S(2)}, u32[]{:S(2)}) collective-permute-start(bf16[4,96,768]{2,1,0:T(8,128)(2,1)S(1)} %pad_maximum_fusion.5.mine_ref), channel_id=1, source_target_pairs={{0,16},{16,0},{1,17},{17,1},{2,18},{18,2},{3,19},{19,3},{4,20},{20... | collective-permute-start | bytes 1769480 | tf_op jit(solution)/shard_map/ppermute | solution.py:204
  256.1 15.1 %collective-permute-start.54 = (bf16[192,768]{1,0:T(8,128)(2,1)S(1)}, bf16[192,768]{1,0:T(8,128)(2,1)S(1)}, u32[]{:S(2)}, u32[]{:S(2)}) collective-permute-start(bf16[192,768]{1,0:T(8,128)(2,1)S(1)} %fusion.7), channel_id=1, source_target_pairs={{0,16},{16,0},{1,17},{17,1},{2,18},{18,2},{3,19},{19,3},{4,20},{20... | collective-permute-start | bytes 884744 | tf_op jit(solution)/shard_map/ppermute | solution.py:204
  258.1 7.4 %collective-permute-start.56 = (bf16[112,768]{1,0:T(8,128)(2,1)S(1)}, bf16[112,768]{1,0:T(8,128)(2,1)S(1)}, u32[]{:S(2)}, u32[]{:S(2)}) collective-permute-start(bf16[112,768]{1,0:T(8,128)(2,1)S(1)} %pad_maximum_fusion.10), channel_id=1, source_target_pairs={{0,1},{1,2},{2,3},{3,0},{4,5},{5,6},{6,7},{7,4},{8,9},{9,10},{10,1... | collective-permute-start | bytes 516104 | tf_op jit(solution)/shard_map/ppermute | solution.py:52
  258.1 10.3 %collective-permute-start.57 = (bf16[112,768]{1,0:T(8,128)(2,1)S(1)}, bf16[112,768]{1,0:T(8,128)(2,1)S(1)}, u32[]{:S(2)}, u32[]{:S(2)}) collective-permute-start(bf16[112,768]{1,0:T(8,128)(2,1)S(1)} %pad_maximum_fusion.10), channel_id=1, source_target_pairs={{0,2},{1,3},{2,0},{3,1},{4,6},{5,7},{6,4},{7,5},{8,10},{9,11},{10,... | collective-permute-start | bytes 516104 | tf_op jit(solution)/shard_map/ppermute | solution.py:52
  258.1 10.3 %collective-permute-start.58 = (bf16[112,768]{1,0:T(8,128)(2,1)S(1)}, bf16[112,768]{1,0:T(8,128)(2,1)S(1)}, u32[]{:S(2)}, u32[]{:S(2)}) collective-permute-start(bf16[112,768]{1,0:T(8,128)(2,1)S(1)} %pad_maximum_fusion.10), channel_id=1, source_target_pairs={{0,3},{1,0},{2,1},{3,2},{4,7},{5,4},{6,5},{7,6},{8,11},{9,8},{10,9... | collective-permute-start | bytes 516104 | tf_op jit(solution)/shard_map/ppermute | solution.py:52
  273.1 10.9 %collective-permute-start.61 = (bf16[4,192,768]{2,1,0:T(8,128)(2,1)S(1)}, bf16[4,192,768]{2,1,0:T(8,128)(2,1)S(1)}, u32[]{:S(2)}, u32[]{:S(2)}) collective-permute-start(bf16[4,192,768]{2,1,0:T(8,128)(2,1)S(1)} %bitcast.121), channel_id=1, source_target_pairs={{0,4},{4,0},{8,12},{12,8},{1,5},{5,1},{9,13},{13,9},{2,6},{6,2},{1... | collective-permute-start | bytes 3538952 | tf_op jit(solution)/shard_map/ppermute | solution.py:47
  273.2 15.7 %collective-permute-start.59 = (bf16[4,96,768]{2,1,0:T(8,128)(2,1)S(1)}, bf16[4,96,768]{2,1,0:T(8,128)(2,1)S(1)}, u32[]{:S(2)}, u32[]{:S(2)}) collective-permute-start(bf16[4,96,768]{2,1,0:T(8,128)(2,1)S(1)} %pad_maximum_fusion.6.mine_ref), channel_id=1, source_target_pairs={{0,16},{16,0},{1,17},{17,1},{2,18},{18,2},{3,19},{19,3},{4,20},{20... | collective-permute-start | bytes 1769480 | tf_op jit(solution)/shard_map/ppermute | solution.py:204
  273.6 15.9 %collective-permute-start.60 = (bf16[2,192,768]{2,1,0:T(8,128)(2,1)S(1)}, bf16[2,192,768]{2,1,0:T(8,128)(2,1)S(1)}, u32[]{:S(2)}, u32[]{:S(2)}) collective-permute-start(bf16[2,192,768]{2,1,0:T(8,128)(2,1)S(1)} %pad_maximum_fusion.7), channel_id=1, source_target_pairs={{0,8},{4,12},{8,0},{12,4},{1,9},{5,13},{9,1},{13,5},{2,10},{6,14},... | collective-permute-start | bytes 1769480 | tf_op jit(solution)/shard_map/ppermute | solution.py:47
  276.8 6.6 %collective-permute-start.62 = (f32[8,768]{1,0:T(8,128)S(1)}, f32[8,768]{1,0:T(8,128)S(1)}, u32[]{:S(2)}, u32[]{:S(2)}) collective-permute-start(f32[8,768]{1,0:T(8,128)S(1)} %add_add_fusion), channel_id=1, source_target_pairs={{0,4},{4,0},{8,12},{12,8},{1,5},{5,1},{9,13},{13,9},{2,6},{6,2},{1... | collective-permute-start | bytes 73736 | tf_op jit(solution)/shard_map/ppermute | solution.py:47
  289.5 2.9 collective-permute-start.63
  (39 other events, 415.6 us)
Sparse Core Ops, SparseCore 0:
  235.0 21.9 all-gather.2
